TPU v7x, 512 devices: a whole 4x8x8 slice. The times are simulated.
512 devices in a mesh: tm: 16 (over y, core), lat: 32 (over x, z).
Axes of the slice: x: 4, y: 8, z: 8, core: 2. Of those that a mesh axis runs over, the one named last changes fastest.
Arguments:
- forcing_rhs: float32 [16, 4, 32, 49320], P('tm', None, 'lat'), may hold values from -6 to 6
- courant_lon: float32 [16, 32, 49320], P('tm', 'lat'), may hold values from -0.45 to 0.45
- courant_lat: float32 [16, 32, 49320], P('tm', 'lat'), may hold values from -0.45 to 0.45
- error_weight: float32 [16, 4, 32, 49320], P('tm', None, 'lat'), may hold values from 0.25 to 4
- obs_cell: int32 [16, 65536], P('tm', 'lat'), may hold values from 0 to 197279
- obs_weight: float32 [16, 65536], P('tm', 'lat'), may hold values from 0.5 to 8
Outputs:
- increment: float32 [16, 4, 32, 49320], P('tm', None, 'lat')
- slid_increment: float32 [16, 4, 32, 49320], P('tm', None, 'lat')
All inputs are finite; a program needn't handle non-finite values.
Results may differ from a plain program's by a relative error of at most 0.0003.
Values sent between devices are 32-bit elements; how exact they have to be, the bound alone decides.
No kernel may reach another device: no remote copies, remote signals or barrier semaphores. Data moves between devices by JAX's collectives and lax.ppermute only.
A program may use at most 64 MiB of HBM per device.

v0:
```python
import jax
import jax.numpy as jnp
from jax import lax
from jax.sharding import PartitionSpec as P

LEV = 137
STEPS = 3
ITERS = 2


def extended(block, sides, width):
    for axis, dim in sides:
        count = lax.axis_size(axis)
        forward = [(i, i + 1) for i in range(count - 1)]
        backward = [(target, source) for source, target in forward]
        low = lax.ppermute(
            lax.slice_in_dim(block, block.shape[dim] - width, None, axis=dim), axis, forward
        )
        high = lax.ppermute(lax.slice_in_dim(block, 0, width, axis=dim), axis, backward)
        block = jnp.concatenate([low, block, high], axis=dim)
    return block


def passed_along(shard, axis, by):
    devices = lax.axis_size(axis)
    pairs = [(i, i + by) for i in range(devices) if 0 <= i + by < devices]
    return lax.ppermute(shard, axis, pairs)


def squares(residual_now):
    return lax.psum(jnp.sum(residual_now * residual_now), ("tm", "lat"))


def body(forcing_rhs, courant_lon, courant_lat, error_weight, obs_cell, obs_weight):
    lon_plus = jnp.maximum(courant_lon, 0.0)[:, None]
    lon_minus = jnp.minimum(courant_lon, 0.0)[:, None]
    lat_plus = jnp.maximum(courant_lat, 0.0)[:, None]
    lat_minus = jnp.minimum(courant_lat, 0.0)[:, None]
    diagonal_part = 1.0 - lon_plus + lon_minus - lat_plus + lat_minus

    def advance(state_now):
        padded = extended(state_now, (("lat", 2),), 1)
        south_row = padded[:, :, :-2]
        north_row = padded[:, :, 2:]
        west_col = jnp.roll(state_now, LEV, axis=3)
        east_col = jnp.roll(state_now, -LEV, axis=3)
        return (
            state_now
            - lon_plus * (state_now - west_col)
            - lon_minus * (east_col - state_now)
            - lat_plus * (state_now - south_row)
            - lat_minus * (north_row - state_now)
        )

    def propagate(state_now):
        for sweep in range(STEPS):
            state_now = advance(state_now)
        return state_now

    cols_here = forcing_rhs.shape[3]
    plane_size = 4 * cols_here
    local_cell = obs_cell[0]
    cell_row = local_cell // plane_size
    cell_comp = local_cell // cols_here % 4
    cell_col = local_cell % cols_here
    increment = jnp.zeros_like(forcing_rhs)
    moved_total = jnp.zeros_like(forcing_rhs)
    residual = forcing_rhs
    direction = forcing_rhs
    norm_now = squares(residual)
    for sweep in range(ITERS):
        moved = propagate(direction)
        arriving = passed_along(moved, "tm", 1)
        weighted = error_weight * (direction - arriving)
        later_weight = passed_along(weighted, "tm", -1)
        adjoint_term = later_weight
        for apply_sweep in range(STEPS):
            plus_rows = extended(lat_plus * adjoint_term, (("lat", 2),), 1)
            minus_rows = extended(lat_minus * adjoint_term, (("lat", 2),), 1)
            adjoint_term = (
                diagonal_part * adjoint_term
                + jnp.roll(lon_plus * adjoint_term, -LEV, axis=3)
                - jnp.roll(lon_minus * adjoint_term, LEV, axis=3)
                + plus_rows[:, :, 2:]
                - minus_rows[:, :, :-2]
            )
        observed = direction[0, cell_comp, cell_row, cell_col]
        obs_back = (
            jnp.zeros_like(direction)
            .at[0, cell_comp, cell_row, cell_col]
            .add(obs_weight[0] * observed)
        )
        image, moved = (weighted - adjoint_term + obs_back, moved)
        step_size = norm_now / lax.psum(jnp.sum(direction * image), ("tm", "lat"))
        increment = increment + step_size * direction
        moved_total = moved_total + step_size * moved
        residual = residual - step_size * image
        if sweep + 1 < ITERS:
            norm_next = squares(residual)
            direction = residual + norm_next / norm_now * direction
            norm_now = norm_next
    final_moved = propagate(increment)
    following = passed_along(increment, "tm", -1)
    is_final = lax.axis_index("tm") == lax.axis_size("tm") - 1
    slid_increment = jnp.where(is_final, final_moved, following)
    return (increment, slid_increment)


def solution(mesh):
    placed = (
        P("tm", None, "lat", None),
        P("tm", "lat", None),
        P("tm", "lat", None),
        P("tm", None, "lat", None),
        P("tm", "lat"),
        P("tm", "lat"),
    )
    return jax.shard_map(
        body,
        mesh=mesh,
        in_specs=placed,
        out_specs=(P("tm", None, "lat", None), P("tm", None, "lat", None)),
        check_vma=False,
    )
```

profile of v0, /device:TPU:26, one launch (start us, length us, event | category | flops | bytes accessed | tf_op | source)
XLA Modules:
  0.0 861.8 jit_solution(10861426749373500803)
XLA Ops:
  19.0 10.5 %collective-permute-done = f32[1,4,1,49320]{3,2,1,0:T(1,128)S(1)} collective-permute-done((f32[1,4,1,49320]{3,2,1,0:T(1,128)}, f32[1,4,1,49320]{3,2,1,0:T(1,128)S(1)}, u32[]{:S(2)}, u32[]{:S(2)}) %collective-permute-start) | collective-permute-done | bytes 789152 | tf_op jit(solution)/shard_map/ppermute | solution.py:16
  46.1 13.1 %collective-permute-done.2 = f32[1,4,1,49320]{3,2,1,0:T(1,128)S(1)} collective-permute-done((f32[1,4,1,49320]{3,2,1,0:T(1,128)S(1)}, f32[1,4,1,49320]{3,2,1,0:T(1,128)S(1)}, u32[]{:S(2)}, u32[]{:S(2)}) %collective-permute-start.2) | collective-permute-done | bytes 789152 | tf_op jit(solution)/shard_map/ppermute | solution.py:16
  75.9 12.0 %collective-permute-done.4 = f32[1,4,1,49320]{3,2,1,0:T(1,128)S(1)} collective-permute-done((f32[1,4,1,49320]{3,2,1,0:T(1,128)S(1)}, f32[1,4,1,49320]{3,2,1,0:T(1,128)S(1)}, u32[]{:S(2)}, u32[]{:S(2)}) %collective-permute-start.4) | collective-permute-done | bytes 789152 | tf_op jit(solution)/shard_map/ppermute | solution.py:16
  96.2 11.4 %collective-permute-done.6 = f32[1,4,1,49320]{3,2,1,0:T(1,128)S(1)} collective-permute-done((f32[1,4,1,49320]{3,2,1,0:T(1,128)S(1)}, f32[1,4,1,49320]{3,2,1,0:T(1,128)S(1)}, u32[]{:S(2)}, u32[]{:S(2)}) %collective-permute-start.6) | collective-permute-done | bytes 789152 | tf_op jit(solution)/shard_map/ppermute | solution.py:27
  110.6 9.5 %collective-permute-done.7 = f32[1,4,1,49320]{3,2,1,0:T(1,128)S(1)} collective-permute-done((f32[1,4,1,49320]{3,2,1,0:T(1,128)S(1)}, f32[1,4,1,49320]{3,2,1,0:T(1,128)S(1)}, u32[]{:S(2)}, u32[]{:S(2)}) %collective-permute-start.7) | collective-permute-done | bytes 789152 | tf_op jit(solution)/shard_map/ppermute | solution.py:27
  132.4 10.8 %collective-permute-done.8 = f32[1,4,1,49320]{3,2,1,0:T(1,128)S(1)} collective-permute-done((f32[1,4,1,49320]{3,2,1,0:T(1,128)S(1)}, f32[1,4,1,49320]{3,2,1,0:T(1,128)S(1)}, u32[]{:S(2)}, u32[]{:S(2)}) %collective-permute-start.8) | collective-permute-done | bytes 789152 | tf_op jit(solution)/shard_map/ppermute | solution.py:19
  163.6 12.5 %collective-permute-done.10 = f32[1,4,1,49320]{3,2,1,0:T(1,128)S(1)} collective-permute-done((f32[1,4,1,49320]{3,2,1,0:T(1,128)S(1)}, f32[1,4,1,49320]{3,2,1,0:T(1,128)S(1)}, u32[]{:S(2)}, u32[]{:S(2)}) %collective-permute-start.10) | collective-permute-done | bytes 789152 | tf_op jit(solution)/shard_map/ppermute | solution.py:19
  193.4 15.1 %gather_fusion = f32[2048]{0:T(1024)S(1)} fusion(f32[1,4,1,49320]{3,2,1,0:T(1,128)S(1)} %copy-done, s32[2048]{0:T(1024)S(1)} %bitcast.37), kind=kCustom, calls=%fused_computation | custom fusion | bytes 49152 | tf_op jit(solution)/shard_map/gather | solution.py:87
  220.6 12.1 %scatter_fusion = f32[197280]{0:T(1024)S(1)} fusion(f32[197280]{0:T(1024)S(1)} %reshape.213, s32[2048]{0:T(1024)S(1)} %broadcast_select_fusion.1, f32[2048]{0:T(1024)S(1)} %mul.218), kind=kCustom, calls=%fused_computation.2 | custom fusion | flops 2048 | bytes 32768
  236.0 98.8 %all-reduce = (f32[]{:T(128)}, f32[]{:T(128)}) all-reduce(f32[]{:T(128)} %get-tuple-element.3, f32[]{:T(128)} %get-tuple-element.2), channel_id=1, replica_groups=mesh['tm'=16,'lat'=32] {'tm','lat'}, use_global_device_ids=true, to_apply=%region_1.2 | all-reduce | flops 2 | bytes 16 | tf_op jit(solution)/shard_map/psum | solution.py:31
  338.4 96.0 %psum.30 = f32[]{:T(128)} all-reduce(f32[]{:T(128)} %multiply_reduce_fusion.1), channel_id=1, replica_groups=mesh['tm'=16,'lat'=32] {'tm','lat'}, use_global_device_ids=true, to_apply=%region_6.7 | all-reduce | flops 1 | bytes 8 | tf_op jit(solution)/shard_map/psum | solution.py:31
  446.3 14.1 %collective-permute-done.14 = f32[1,4,1,49320]{3,2,1,0:T(1,128)S(1)} collective-permute-done((f32[1,4,1,49320]{3,2,1,0:T(1,128)S(1)}, f32[1,4,1,49320]{3,2,1,0:T(1,128)S(1)}, u32[]{:S(2)}, u32[]{:S(2)}) %collective-permute-start.14) | collective-permute-done | bytes 789152 | tf_op jit(solution)/shard_map/ppermute | solution.py:16
  477.2 13.1 %collective-permute-done.16 = f32[1,4,1,49320]{3,2,1,0:T(1,128)S(1)} collective-permute-done((f32[1,4,1,49320]{3,2,1,0:T(1,128)S(1)}, f32[1,4,1,49320]{3,2,1,0:T(1,128)S(1)}, u32[]{:S(2)}, u32[]{:S(2)}) %collective-permute-start.16) | collective-permute-done | bytes 789152 | tf_op jit(solution)/shard_map/ppermute | solution.py:16
  506.8 12.4 %collective-permute-done.18 = f32[1,4,1,49320]{3,2,1,0:T(1,128)S(1)} collective-permute-done((f32[1,4,1,49320]{3,2,1,0:T(1,128)S(1)}, f32[1,4,1,49320]{3,2,1,0:T(1,128)S(1)}, u32[]{:S(2)}, u32[]{:S(2)}) %collective-permute-start.18) | collective-permute-done | bytes 789152 | tf_op jit(solution)/shard_map/ppermute | solution.py:16
  527.5 11.4 %collective-permute-done.20 = f32[1,4,1,49320]{3,2,1,0:T(1,128)S(1)} collective-permute-done((f32[1,4,1,49320]{3,2,1,0:T(1,128)S(1)}, f32[1,4,1,49320]{3,2,1,0:T(1,128)S(1)}, u32[]{:S(2)}, u32[]{:S(2)}) %collective-permute-start.20) | collective-permute-done | bytes 789152 | tf_op jit(solution)/shard_map/ppermute | solution.py:27
  542.0 9.5 %collective-permute-done.21 = f32[1,4,1,49320]{3,2,1,0:T(1,128)S(1)} collective-permute-done((f32[1,4,1,49320]{3,2,1,0:T(1,128)S(1)}, f32[1,4,1,49320]{3,2,1,0:T(1,128)S(1)}, u32[]{:S(2)}, u32[]{:S(2)}) %collective-permute-start.21) | collective-permute-done | bytes 789152 | tf_op jit(solution)/shard_map/ppermute | solution.py:27
  563.9 13.6 %collective-permute-done.22 = f32[1,4,1,49320]{3,2,1,0:T(1,128)S(1)} collective-permute-done((f32[1,4,1,49320]{3,2,1,0:T(1,128)S(1)}, f32[1,4,1,49320]{3,2,1,0:T(1,128)S(1)}, u32[]{:S(2)}, u32[]{:S(2)}) %collective-permute-start.22) | collective-permute-done | bytes 789152 | tf_op jit(solution)/shard_map/ppermute | solution.py:19
  597.7 13.8 %collective-permute-done.24 = f32[1,4,1,49320]{3,2,1,0:T(1,128)S(1)} collective-permute-done((f32[1,4,1,49320]{3,2,1,0:T(1,128)S(1)}, f32[1,4,1,49320]{3,2,1,0:T(1,128)S(1)}, u32[]{:S(2)}, u32[]{:S(2)}) %collective-permute-start.24) | collective-permute-done | bytes 789152 | tf_op jit(solution)/shard_map/ppermute | solution.py:19
  629.7 15.1 %gather_fusion.1 = f32[2048]{0:T(1024)S(1)} fusion(f32[1,4,1,49320]{3,2,1,0:T(1,128)S(1)} %multiply_add_fusion.1, s32[2048]{0:T(1024)S(1)} %bitcast.38), kind=kCustom, calls=%fused_computation.1 | custom fusion | bytes 49152 | tf_op jit(solution)/shard_map/gather | solution.py:87
  658.0 11.7 %scatter_fusion.1 = f32[197280]{0:T(1024)S(1)} fusion(f32[197280]{0:T(1024)S(1)} %reshape.217, s32[2048]{0:T(1024)S(1)} %broadcast_select_fusion.1, f32[2048]{0:T(1024)S(1)} %mul.254), kind=kCustom, calls=%fused_computation.3 | custom fusion | flops 2048 | bytes 32768
  675.0 94.9 %psum.31 = f32[]{:T(128)} all-reduce(f32[]{:T(128)} %multiply_reduce_fusion), channel_id=1, replica_groups=mesh['tm'=16,'lat'=32] {'tm','lat'}, use_global_device_ids=true, to_apply=%region_9.10 | all-reduce | flops 1 | bytes 8 | tf_op jit(solution)/shard_map/psum | solution.py:94
  783.9 12.0 %collective-permute-done.28 = f32[1,4,1,49320]{3,2,1,0:T(1,128)S(1)} collective-permute-done((f32[1,4,1,49320]{3,2,1,0:T(1,128)S(1)}, f32[1,4,1,49320]{3,2,1,0:T(1,128)S(1)}, u32[]{:S(2)}, u32[]{:S(2)}) %collective-permute-start.28) | collective-permute-done | bytes 789152 | tf_op jit(solution)/shard_map/ppermute | solution.py:16
  812.4 13.2 %collective-permute-done.30 = f32[1,4,1,49320]{3,2,1,0:T(1,128)S(1)} collective-permute-done((f32[1,4,1,49320]{3,2,1,0:T(1,128)S(1)}, f32[1,4,1,49320]{3,2,1,0:T(1,128)S(1)}, u32[]{:S(2)}, u32[]{:S(2)}) %collective-permute-start.30) | collective-permute-done | bytes 789152 | tf_op jit(solution)/shard_map/ppermute | solution.py:16
  842.1 12.3 %collective-permute-done.32 = f32[1,4,1,49320]{3,2,1,0:T(1,128)S(1)} collective-permute-done((f32[1,4,1,49320]{3,2,1,0:T(1,128)S(1)}, f32[1,4,1,49320]{3,2,1,0:T(1,128)S(1)}, u32[]{:S(2)}, u32[]{:S(2)}) %collective-permute-start.32) | collective-permute-done | bytes 789152 | tf_op jit(solution)/shard_map/ppermute | solution.py:16
  (168 shorter events, 307.1 us)
Async XLA Ops:
  0.6 28.9 %collective-permute-start = (f32[1,4,1,49320]{3,2,1,0:T(1,128)}, f32[1,4,1,49320]{3,2,1,0:T(1,128)S(1)}, u32[]{:S(2)}, u32[]{:S(2)}) collective-permute-start(f32[1,4,1,49320]{3,2,1,0:T(1,128)} %param.6), channel_id=1, source_target_pairs={{0,1},{1,2},{2,3},{3,4},{4,5},{5,6},{6,7},{7,8},{8,9},{9,10},{10,1... | collective-permute-start | bytes 2367368 | tf_op jit(solution)/shard_map/ppermute | solution.py:16
  5.1 25.8 %collective-permute-start.1 = (f32[1,4,1,49320]{3,2,1,0:T(1,128)}, f32[1,4,1,49320]{3,2,1,0:T(1,128)S(1)}, u32[]{:S(2)}, u32[]{:S(2)}) collective-permute-start(f32[1,4,1,49320]{3,2,1,0:T(1,128)} %param.6), channel_id=1, source_target_pairs={{1,0},{2,1},{3,2},{4,3},{5,4},{6,5},{7,6},{8,7},{9,8},{10,9},{11,1... | collective-permute-start | bytes 2367368 | tf_op jit(solution)/shard_map/ppermute | solution.py:19
  36.0 23.1 %collective-permute-start.2 = (f32[1,4,1,49320]{3,2,1,0:T(1,128)S(1)}, f32[1,4,1,49320]{3,2,1,0:T(1,128)S(1)}, u32[]{:S(2)}, u32[]{:S(2)}) collective-permute-start(f32[1,4,1,49320]{3,2,1,0:T(1,128)S(1)} %multiply_subtract_fusion.8), channel_id=1, source_target_pairs={{0,1},{1,2},{2,3},{3,4},{4,5},{5,6},{6,7},{7,8},{8,9},{9,10},{10,1... | collective-permute-start | bytes 2367368 | tf_op jit(solution)/shard_map/ppermute | solution.py:16
  37.9 22.4 %collective-permute-start.3 = (f32[1,4,1,49320]{3,2,1,0:T(1,128)S(1)}, f32[1,4,1,49320]{3,2,1,0:T(1,128)S(1)}, u32[]{:S(2)}, u32[]{:S(2)}) collective-permute-start(f32[1,4,1,49320]{3,2,1,0:T(1,128)S(1)} %multiply_subtract_fusion.8), channel_id=1, source_target_pairs={{1,0},{2,1},{3,2},{4,3},{5,4},{6,5},{7,6},{8,7},{9,8},{10,9},{11,1... | collective-permute-start | bytes 2367368 | tf_op jit(solution)/shard_map/ppermute | solution.py:19
  65.5 22.3 %collective-permute-start.4 = (f32[1,4,1,49320]{3,2,1,0:T(1,128)S(1)}, f32[1,4,1,49320]{3,2,1,0:T(1,128)S(1)}, u32[]{:S(2)}, u32[]{:S(2)}) collective-permute-start(f32[1,4,1,49320]{3,2,1,0:T(1,128)S(1)} %multiply_subtract_fusion.7), channel_id=1, source_target_pairs={{0,1},{1,2},{2,3},{3,4},{4,5},{5,6},{6,7},{7,8},{8,9},{9,10},{10,1... | collective-permute-start | bytes 2367368 | tf_op jit(solution)/shard_map/ppermute | solution.py:16
  157.6 22.5 %collective-permute-start.11 = (f32[1,4,1,49320]{3,2,1,0:T(1,128)S(1)}, f32[1,4,1,49320]{3,2,1,0:T(1,128)S(1)}, u32[]{:S(2)}, u32[]{:S(2)}) collective-permute-start(f32[1,4,1,49320]{3,2,1,0:T(1,128)S(1)} %get-tuple-element.61), channel_id=1, source_target_pairs={{0,1},{1,2},{2,3},{3,4},{4,5},{5,6},{6,7},{7,8},{8,9},{9,10},{10,1... | collective-permute-start | bytes 2367368 | tf_op jit(solution)/shard_map/ppermute | solution.py:16
  187.4 25.5 %collective-permute-start.12 = (f32[1,4,1,49320]{3,2,1,0:T(1,128)}, f32[1,4,1,49320]{3,2,1,0:T(1,128)}, u32[]{:S(2)}, u32[]{:S(2)}) collective-permute-start(f32[1,4,1,49320]{3,2,1,0:T(1,128)} %get-tuple-element.57), channel_id=1, source_target_pairs={{1,0},{2,1},{3,2},{4,3},{5,4},{6,5},{7,6},{8,7},{9,8},{10,9},{11,1... | collective-permute-start | bytes 2367368 | tf_op jit(solution)/shard_map/ppermute | solution.py:19
  189.3 24.0 %collective-permute-start.13 = (f32[1,4,1,49320]{3,2,1,0:T(1,128)}, f32[1,4,1,49320]{3,2,1,0:T(1,128)}, u32[]{:S(2)}, u32[]{:S(2)}) collective-permute-start(f32[1,4,1,49320]{3,2,1,0:T(1,128)} %get-tuple-element.58), channel_id=1, source_target_pairs={{0,1},{1,2},{2,3},{3,4},{4,5},{5,6},{6,7},{7,8},{8,9},{9,10},{10,1... | collective-permute-start | bytes 2367368 | tf_op jit(solution)/shard_map/ppermute | solution.py:16
  436.5 23.9 %collective-permute-start.14 = (f32[1,4,1,49320]{3,2,1,0:T(1,128)S(1)}, f32[1,4,1,49320]{3,2,1,0:T(1,128)S(1)}, u32[]{:S(2)}, u32[]{:S(2)}) collective-permute-start(f32[1,4,1,49320]{3,2,1,0:T(1,128)S(1)} %multiply_add_fusion.1), channel_id=1, source_target_pairs={{0,1},{1,2},{2,3},{3,4},{4,5},{5,6},{6,7},{7,8},{8,9},{9,10},{10,1... | collective-permute-start | bytes 2367368 | tf_op jit(solution)/shard_map/ppermute | solution.py:16
  438.5 23.1 %collective-permute-start.15 = (f32[1,4,1,49320]{3,2,1,0:T(1,128)S(1)}, f32[1,4,1,49320]{3,2,1,0:T(1,128)S(1)}, u32[]{:S(2)}, u32[]{:S(2)}) collective-permute-start(f32[1,4,1,49320]{3,2,1,0:T(1,128)S(1)} %multiply_add_fusion.1), channel_id=1, source_target_pairs={{1,0},{2,1},{3,2},{4,3},{5,4},{6,5},{7,6},{8,7},{9,8},{10,9},{11,1... | collective-permute-start | bytes 2367368 | tf_op jit(solution)/shard_map/ppermute | solution.py:19
  466.8 23.5 %collective-permute-start.16 = (f32[1,4,1,49320]{3,2,1,0:T(1,128)S(1)}, f32[1,4,1,49320]{3,2,1,0:T(1,128)S(1)}, u32[]{:S(2)}, u32[]{:S(2)}) collective-permute-start(f32[1,4,1,49320]{3,2,1,0:T(1,128)S(1)} %multiply_subtract_fusion.4), channel_id=1, source_target_pairs={{0,1},{1,2},{2,3},{3,4},{4,5},{5,6},{6,7},{7,8},{8,9},{9,10},{10,1... | collective-permute-start | bytes 2367368 | tf_op jit(solution)/shard_map/ppermute | solution.py:16
  468.7 22.7 %collective-permute-start.17 = (f32[1,4,1,49320]{3,2,1,0:T(1,128)S(1)}, f32[1,4,1,49320]{3,2,1,0:T(1,128)S(1)}, u32[]{:S(2)}, u32[]{:S(2)}) collective-permute-start(f32[1,4,1,49320]{3,2,1,0:T(1,128)S(1)} %multiply_subtract_fusion.4), channel_id=1, source_target_pairs={{1,0},{2,1},{3,2},{4,3},{5,4},{6,5},{7,6},{8,7},{9,8},{10,9},{11,1... | collective-permute-start | bytes 2367368 | tf_op jit(solution)/shard_map/ppermute | solution.py:19
  496.6 22.6 %collective-permute-start.18 = (f32[1,4,1,49320]{3,2,1,0:T(1,128)S(1)}, f32[1,4,1,49320]{3,2,1,0:T(1,128)S(1)}, u32[]{:S(2)}, u32[]{:S(2)}) collective-permute-start(f32[1,4,1,49320]{3,2,1,0:T(1,128)S(1)} %multiply_subtract_fusion.3), channel_id=1, source_target_pairs={{0,1},{1,2},{2,3},{3,4},{4,5},{5,6},{6,7},{7,8},{8,9},{9,10},{10,1... | collective-permute-start | bytes 2367368 | tf_op jit(solution)/shard_map/ppermute | solution.py:16
  553.5 24.1 %collective-permute-start.22 = (f32[1,4,1,49320]{3,2,1,0:T(1,128)S(1)}, f32[1,4,1,49320]{3,2,1,0:T(1,128)S(1)}, u32[]{:S(2)}, u32[]{:S(2)}) collective-permute-start(f32[1,4,1,49320]{3,2,1,0:T(1,128)S(1)} %get-tuple-element.42), channel_id=1, source_target_pairs={{1,0},{2,1},{3,2},{4,3},{5,4},{6,5},{7,6},{8,7},{9,8},{10,9},{11,1... | collective-permute-start | bytes 2367368 | tf_op jit(solution)/shard_map/ppermute | solution.py:19
  560.0 24.3 %collective-permute-start.23 = (f32[1,4,1,49320]{3,2,1,0:T(1,128)S(1)}, f32[1,4,1,49320]{3,2,1,0:T(1,128)S(1)}, u32[]{:S(2)}, u32[]{:S(2)}) collective-permute-start(f32[1,4,1,49320]{3,2,1,0:T(1,128)S(1)} %get-tuple-element.41), channel_id=1, source_target_pairs={{0,1},{1,2},{2,3},{3,4},{4,5},{5,6},{6,7},{7,8},{8,9},{9,10},{10,1... | collective-permute-start | bytes 2367368 | tf_op jit(solution)/shard_map/ppermute | solution.py:16
  591.9 23.7 %collective-permute-start.25 = (f32[1,4,1,49320]{3,2,1,0:T(1,128)S(1)}, f32[1,4,1,49320]{3,2,1,0:T(1,128)S(1)}, u32[]{:S(2)}, u32[]{:S(2)}) collective-permute-start(f32[1,4,1,49320]{3,2,1,0:T(1,128)S(1)} %get-tuple-element.39), channel_id=1, source_target_pairs={{0,1},{1,2},{2,3},{3,4},{4,5},{5,6},{6,7},{7,8},{8,9},{9,10},{10,1... | collective-permute-start | bytes 2367368 | tf_op jit(solution)/shard_map/ppermute | solution.py:16
  623.4 25.1 %collective-permute-start.26 = (f32[1,4,1,49320]{3,2,1,0:T(1,128)}, f32[1,4,1,49320]{3,2,1,0:T(1,128)}, u32[]{:S(2)}, u32[]{:S(2)}) collective-permute-start(f32[1,4,1,49320]{3,2,1,0:T(1,128)} %get-tuple-element.35), channel_id=1, source_target_pairs={{1,0},{2,1},{3,2},{4,3},{5,4},{6,5},{7,6},{8,7},{9,8},{10,9},{11,1... | collective-permute-start | bytes 2367368 | tf_op jit(solution)/shard_map/ppermute | solution.py:19
  625.4 23.2 %collective-permute-start.27 = (f32[1,4,1,49320]{3,2,1,0:T(1,128)}, f32[1,4,1,49320]{3,2,1,0:T(1,128)}, u32[]{:S(2)}, u32[]{:S(2)}) collective-permute-start(f32[1,4,1,49320]{3,2,1,0:T(1,128)} %get-tuple-element.36), channel_id=1, source_target_pairs={{0,1},{1,2},{2,3},{3,4},{4,5},{5,6},{6,7},{7,8},{8,9},{9,10},{10,1... | collective-permute-start | bytes 2367368 | tf_op jit(solution)/shard_map/ppermute | solution.py:16
  772.0 23.8 %collective-permute-start.28 = (f32[1,4,1,49320]{3,2,1,0:T(1,128)S(1)}, f32[1,4,1,49320]{3,2,1,0:T(1,128)S(1)}, u32[]{:S(2)}, u32[]{:S(2)}) collective-permute-start(f32[1,4,1,49320]{3,2,1,0:T(1,128)S(1)} %multiply_add_fusion), channel_id=1, source_target_pairs={{0,1},{1,2},{2,3},{3,4},{4,5},{5,6},{6,7},{7,8},{8,9},{9,10},{10,1... | collective-permute-start | bytes 2367368 | tf_op jit(solution)/shard_map/ppermute | solution.py:16
  774.5 22.5 %collective-permute-start.29 = (f32[1,4,1,49320]{3,2,1,0:T(1,128)S(1)}, f32[1,4,1,49320]{3,2,1,0:T(1,128)S(1)}, u32[]{:S(2)}, u32[]{:S(2)}) collective-permute-start(f32[1,4,1,49320]{3,2,1,0:T(1,128)S(1)} %multiply_add_fusion), channel_id=1, source_target_pairs={{1,0},{2,1},{3,2},{4,3},{5,4},{6,5},{7,6},{8,7},{9,8},{10,9},{11,1... | collective-permute-start | bytes 2367368 | tf_op jit(solution)/shard_map/ppermute | solution.py:19
  781.8 60.3 %collective-permute-start.34 = (f32[1,4,1,49320]{3,2,1,0:T(1,128)S(1)}, f32[1,4,1,49320]{3,2,1,0:T(1,128)S(1)}, u32[]{:S(2)}, u32[]{:S(2)}) collective-permute-start(f32[1,4,1,49320]{3,2,1,0:T(1,128)S(1)} %multiply_add_fusion), channel_id=1, source_target_pairs={{32,0},{64,32},{96,64},{128,96},{160,128},{192,160},{224,192},{256... | collective-permute-start | bytes 2367368 | tf_op jit(solution)/shard_map/ppermute | solution.py:27
  802.2 23.4 %collective-permute-start.30 = (f32[1,4,1,49320]{3,2,1,0:T(1,128)S(1)}, f32[1,4,1,49320]{3,2,1,0:T(1,128)S(1)}, u32[]{:S(2)}, u32[]{:S(2)}) collective-permute-start(f32[1,4,1,49320]{3,2,1,0:T(1,128)S(1)} %multiply_subtract_fusion.1), channel_id=1, source_target_pairs={{0,1},{1,2},{2,3},{3,4},{4,5},{5,6},{6,7},{7,8},{8,9},{9,10},{10,1... | collective-permute-start | bytes 2367368 | tf_op jit(solution)/shard_map/ppermute | solution.py:16
  804.1 22.7 %collective-permute-start.31 = (f32[1,4,1,49320]{3,2,1,0:T(1,128)S(1)}, f32[1,4,1,49320]{3,2,1,0:T(1,128)S(1)}, u32[]{:S(2)}, u32[]{:S(2)}) collective-permute-start(f32[1,4,1,49320]{3,2,1,0:T(1,128)S(1)} %multiply_subtract_fusion.1), channel_id=1, source_target_pairs={{1,0},{2,1},{3,2},{4,3},{5,4},{6,5},{7,6},{8,7},{9,8},{10,9},{11,1... | collective-permute-start | bytes 2367368 | tf_op jit(solution)/shard_map/ppermute | solution.py:19
  831.9 22.5 %collective-permute-start.32 = (f32[1,4,1,49320]{3,2,1,0:T(1,128)S(1)}, f32[1,4,1,49320]{3,2,1,0:T(1,128)S(1)}, u32[]{:S(2)}, u32[]{:S(2)}) collective-permute-start(f32[1,4,1,49320]{3,2,1,0:T(1,128)S(1)} %multiply_subtract_fusion), channel_id=1, source_target_pairs={{0,1},{1,2},{2,3},{3,4},{4,5},{5,6},{6,7},{7,8},{8,9},{9,10},{10,1... | collective-permute-start | bytes 2367368 | tf_op jit(solution)/shard_map/ppermute | solution.py:16
  (27 other events, 353.7 us)
where the time goes:
time: 870 us; the launch traced here: 862 us
  blocking collectives  290 us (33%)
  waiting for transfers between devices  238 us (27%)
  starting transfers between devices  130 us (15%)
  other arithmetic  130 us (15%)
  local copies, waits for them, and re-layouts  67.6 us (8%)
    psum x2, blocking collectives, squares(): return lax.psum(jnp.sum(residual_now * residual_now), ('tm', 'lat'))  195 us
    ppermute x15, waiting for transfers between devices, extended(): lax.ppermute(lax.slice_in_dim(block, block.shape[dim] - width, None, axis...  135 us
    psum x1, blocking collectives, body(): step_size = norm_now / lax.psum(jnp.sum(direction * image), ('tm', 'lat'))  94.9 us
    ppermute x15, starting transfers between devices, extended(): lax.ppermute(lax.slice_in_dim(block, 0, width, axis=dim), axis, backward)  79.5 us
    ppermute x15, waiting for transfers between devices, extended(): lax.ppermute(lax.slice_in_dim(block, 0, width, axis=dim), axis, backward)  61.5 us
    ppermute x5, waiting for transfers between devices, passed_along(): return lax.ppermute(shard, axis, pairs)  41.9 us
    sub x8, other arithmetic, advance(): state_now - lon_plus * (state_now - west_col)  41.4 us
    ppermute x15, starting transfers between devices, extended(): lax.ppermute(lax.slice_in_dim(block, block.shape[dim] - width, None, axis...  41.3 us
  transfers between devices with their start and end apart: 35, of which 31 were waited for; matrix products, arithmetic and copies ran while one was open for 8% of the time, Pallas kernels for 0%

commit v1 on v0

v1 whole, which is shorter than its diff:
```python
import functools
import math

import jax
import jax.numpy as jnp
from jax import lax
from jax.experimental import pallas as pl
from jax.experimental.pallas import tpu as pltpu
from jax.sharding import PartitionSpec as P

LEV = 137
LON = 360
STEPS = 3
EDGE = 12
WIDE = LON + 2 * EDGE
UNITS = 18
SPAN = 5
LANES = 128
CUTS = WIDE // LANES


def whole_rows(n):
    return -(-n // 8) * 8


def planes(fields):
    count = fields.shape[0]
    turned = fields.reshape(count, LON, LEV).transpose(0, 2, 1)
    turned = jnp.pad(turned, ((0, 0), (0, 144 - LEV), (EDGE, EDGE)))
    return turned.reshape(count, 16, 9, WIDE)


def dealt(fields):
    p = planes(fields)
    even = jnp.concatenate([p[0, :, :5], p[1, :, :5], p[2, :, :4], p[3, :, :4]], 1)
    odd = jnp.concatenate([p[2, :, 4:], p[3, :, 4:], p[0, :, 5:], p[1, :, 5:]], 1)
    return jnp.stack([even, odd], 1).reshape(32, UNITS, WIDE)


def dealt_levels(plane):
    p = planes(plane)[0]
    return jnp.stack([p[:, :5], p[:, 4:]], 1).reshape(32, SPAN, WIDE)


def gathered(chunks):
    c = chunks.reshape(16, 2, UNITS, WIDE)[..., EDGE : EDGE + LON]
    e, o = c[:, 0], c[:, 1]
    per_field = [
        jnp.concatenate([e[:, 0:5], o[:, 10:14]], 1),
        jnp.concatenate([e[:, 5:10], o[:, 14:18]], 1),
        jnp.concatenate([e[:, 10:14], o[:, 0:5]], 1),
        jnp.concatenate([e[:, 14:18], o[:, 5:10]], 1),
    ]
    p = jnp.stack(per_field).reshape(4, 144, LON)[:, :LEV]
    return p.transpose(0, 2, 1).reshape(4, LON * LEV)


def sent(*parts):
    joined = jnp.concatenate([p.reshape(32, -1, LANES) for p in parts], 1)
    rows = joined.shape[1]
    return jnp.pad(joined, ((0, 0), (0, whole_rows(rows) - rows), (0, 0)))


def exchanged(buffer):
    got = lax.all_to_all(buffer, "lat", 0, 0, tiled=True)
    return got.reshape(-1, LANES)


def plane_of(ref, rows, first):
    return jnp.concatenate(
        [ref[pl.ds(first + cut, 32, stride=rows), :] for cut in range(CUTS)], axis=1
    )


def put_plane(ref, rows, first, value):
    for cut in range(CUTS):
        ref[pl.ds(first + cut, 32, stride=rows), :] = value[:, cut * LANES : (cut + 1) * LANES]


def lane_index():
    return lax.broadcasted_iota(jnp.int32, (32, WIDE), 1)


def wrapped(v):
    lane = lane_index()
    v = jnp.where(lane < EDGE, pltpu.roll(v, 2 * EDGE, 1), v)
    return jnp.where(lane >= EDGE + LON, pltpu.roll(v, LON, 1), v)


def fill_coefficients(got_ref, rows, base, coef):
    lat = lax.broadcasted_iota(jnp.int32, (32, WIDE), 0)

    def one(level, carry):
        a = wrapped(plane_of(got_ref, rows, base + CUTS * level))
        c = wrapped(plane_of(got_ref, rows, base + CUTS * (SPAN + level)))
        coef[level, 0] = 1.0 - jnp.abs(a) - jnp.abs(c)
        coef[level, 1] = jnp.maximum(a, 0.0)
        coef[level, 2] = jnp.maximum(-a, 0.0)
        coef[level, 3] = jnp.where(lat == 0, 0.0, jnp.maximum(c, 0.0))
        coef[level, 4] = jnp.where(lat == 31, 0.0, jnp.maximum(-c, 0.0))
        return carry

    lax.fori_loop(0, SPAN, one, 0)


def level_of(unit, odd):
    return jnp.where(unit < 10, lax.rem(unit, 5), lax.rem(unit - 10, 4) + odd)


def forward(v, coef, level):
    for step in range(STEPS):
        v = (
            coef[level, 0] * v
            + coef[level, 1] * pltpu.roll(v, 1, 1)
            + coef[level, 2] * pltpu.roll(v, WIDE - 1, 1)
            + coef[level, 3] * pltpu.roll(v, 1, 0)
            + coef[level, 4] * pltpu.roll(v, 31, 0)
        )
    return v


def backward(v, coef, level):
    for step in range(STEPS):
        v = (
            coef[level, 0] * v
            + pltpu.roll(coef[level, 1] * v, WIDE - 1, 1)
            + pltpu.roll(coef[level, 2] * v, 1, 1)
            + pltpu.roll(coef[level, 3] * v, 31, 0)
            + pltpu.roll(coef[level, 4] * v, 1, 0)
        )
    return v


def inner_lanes():
    lane = lane_index()
    return jnp.where((lane >= EDGE) & (lane < EDGE + LON), 1.0, 0.0)


def row_sum(v):
    total = jnp.sum(v, axis=0, keepdims=True)
    return total[:, :LANES] + total[:, LANES : 2 * LANES] + total[:, 2 * LANES :]


def moved_kernel(rows, odd_ref, got_ref, state_ref, moved_ref, coef):
    fill_coefficients(got_ref, rows, CUTS * UNITS, coef)
    odd = odd_ref[0]

    def one(unit, carry):
        v = wrapped(plane_of(got_ref, rows, CUTS * unit))
        state_ref[unit] = v
        moved_ref[unit] = forward(v, coef, level_of(unit, odd))
        return carry

    lax.fori_loop(0, UNITS, one, 0)


def weighted_kernel(rows, state_ref, arriving_ref, got_ref, weighted_ref):
    def one(unit, carry):
        w = wrapped(plane_of(got_ref, rows, CUTS * unit))
        weighted_ref[unit] = w * (state_ref[unit] - arriving_ref[unit])
        return carry

    lax.fori_loop(0, UNITS, one, 0)


def image_kernel(
    rows, got_rows, odd_ref, got_ref, obs_ref, state_ref, weighted_ref, later_ref,
    image_ref, moved_ref, back_ref, sums_ref, coef,
):
    fill_coefficients(got_ref, rows, CUTS * UNITS, coef)
    odd = odd_ref[0]
    inner = inner_lanes()
    back_rows = whole_rows(CUTS * UNITS)

    def one(unit, carry):
        level = level_of(unit, odd)
        state = state_ref[unit]
        obs = plane_of(obs_ref, got_rows, CUTS * (UNITS + unit))
        image = weighted_ref[unit] - backward(later_ref[unit], coef, level) + obs * state
        image = wrapped(image)
        image_ref[unit] = image
        put_plane(back_ref, back_rows, CUTS * unit, image)
        moved_ref[unit] = forward(image, coef, level)
        own, cross, square = carry
        core = inner * image
        return (
            own + row_sum(inner * state * state),
            cross + row_sum(core * state),
            square + row_sum(core * image),
        )

    zero = jnp.zeros((1, LANES), jnp.float32)
    sums = lax.fori_loop(0, UNITS, one, (zero, zero, zero))
    for row in range(3):
        sums_ref[row : row + 1, :] = sums[row]
    sums_ref[3:8, :] = jnp.zeros((5, LANES), jnp.float32)
    for row in range(CUTS * UNITS, back_rows):
        back_ref[pl.ds(row, 32, stride=back_rows), :] = jnp.zeros((32, LANES), jnp.float32)


def norm_kernel(got_rows, image_ref, arriving_ref, got_ref, sums_ref, out_ref):
    inner = inner_lanes()

    def one(unit, carry):
        w = plane_of(got_ref, got_rows, CUTS * unit)
        obs = plane_of(got_ref, got_rows, CUTS * (UNITS + unit))
        image = image_ref[unit]
        change = image - arriving_ref[unit]
        return carry + row_sum(inner * (w * change * change + obs * image * image))

    total = lax.fori_loop(0, UNITS, one, jnp.zeros((1, LANES), jnp.float32))
    out_ref[...] = sums_ref[...]
    out_ref[3:4, :] = total


def last_kernel(scale_ref, state_moved_ref, image_moved_ref, back_ref):
    back_rows = whole_rows(CUTS * UNITS)
    first, second = scale_ref[0], scale_ref[1]

    def one(unit, carry):
        value = first * state_moved_ref[unit] + second * image_moved_ref[unit]
        put_plane(back_ref, back_rows, CUTS * unit, value)
        return carry

    lax.fori_loop(0, UNITS, one, 0)
    for row in range(CUTS * UNITS, back_rows):
        back_ref[pl.ds(row, 32, stride=back_rows), :] = jnp.zeros((32, LANES), jnp.float32)


VMEM = pl.BlockSpec(memory_space=pltpu.VMEM)
SMEM = pl.BlockSpec(memory_space=pltpu.SMEM)
PLANES = jax.ShapeDtypeStruct((UNITS, 32, WIDE), jnp.float32)
BACK = jax.ShapeDtypeStruct((32 * whole_rows(CUTS * UNITS), LANES), jnp.float32)
SUMS = jax.ShapeDtypeStruct((8, LANES), jnp.float32)
COEF = pltpu.VMEM((SPAN, 5, 32, WIDE), jnp.float32)


def call(kernel, outs, ins, scratch=(), flops=0):
    moved = sum(4 * math.prod(o.shape) for o in outs)
    return pl.pallas_call(
        kernel,
        out_shape=outs,
        in_specs=[SMEM if i == "s" else VMEM for i in ins],
        out_specs=[VMEM] * len(outs),
        scratch_shapes=list(scratch),
        compiler_params=pltpu.CompilerParams(vmem_limit_bytes=40 * 2**20),
        cost_estimate=pl.CostEstimate(flops=flops, bytes_accessed=3 * moved, transcendentals=0),
    )


def passed_along(shard, by):
    devices = lax.axis_size("tm")
    pairs = [(i, i + by) for i in range(devices) if 0 <= i + by < devices]
    return lax.ppermute(shard, "tm", pairs)


def summed(tile):
    for axis in ("lat", "tm"):
        count = lax.axis_size(axis)
        tile = lax.all_to_all(
            jnp.broadcast_to(tile[None], (count, 8, LANES)), axis, 0, 0, tiled=True
        ).sum(0)
    return tile.sum(1)


def body(forcing_rhs, courant_lon, courant_lat, error_weight, obs_cell, obs_weight):
    own = forcing_rhs[0, :, 0]
    odd = lax.rem(lax.axis_index("lat"), 2).reshape(1)

    first = sent(dealt(own), dealt_levels(courant_lon[0]), dealt_levels(courant_lat[0]))
    rows = first.shape[1]
    got = exchanged(first)

    cell = obs_cell[0]
    field, column = cell // (LON * LEV), cell % (LON * LEV)
    lon, lev = column // LEV, column % LEV
    pair, inside = lev // 9, lev % 9
    low = field < 2
    is_even = inside < jnp.where(low, 5, 4)
    slot = field % 2
    unit = jnp.where(
        is_even,
        jnp.where(low, slot * 5 + inside, 10 + slot * 4 + inside),
        jnp.where(low, 10 + slot * 4 + inside - 5, slot * 5 + inside - 4),
    )
    place = ((2 * pair + jnp.where(is_even, 0, 1)) * UNITS + unit) * WIDE + lon + EDGE
    cell_weight = jnp.zeros((32 * UNITS * WIDE,), jnp.float32).at[place].add(obs_weight[0])

    second = sent(dealt(error_weight[0, :, 0]), cell_weight.reshape(32, UNITS, WIDE))
    got_rows = second.shape[1]
    got_second = exchanged(second)

    state, moved = call(
        functools.partial(moved_kernel, rows), [PLANES, PLANES], "sv", [COEF], 10**8
    )(odd, got)
    arriving = passed_along(moved, 1)
    (weighted,) = call(functools.partial(weighted_kernel, got_rows), [PLANES], "vvv")(
        state, arriving, got_second
    )
    later = passed_along(weighted, -1)
    image, image_moved, back, sums = call(
        functools.partial(image_kernel, rows, got_rows),
        [PLANES, PLANES, BACK, SUMS],
        "svvvvv",
        [COEF],
        2 * 10**8,
    )(odd, got, got_second, state, weighted, later)
    image_arriving = passed_along(image_moved, 1)
    image_own = gathered(exchanged(back.reshape(32, -1, LANES)).reshape(32, -1, LANES)[:, : CUTS * UNITS].reshape(32, UNITS, WIDE))
    next_own = passed_along(own, -1)
    next_image = passed_along(image_own, -1)
    (sums,) = call(functools.partial(norm_kernel, got_rows), [SUMS], "vvvv")(
        image, image_arriving, got_second, sums
    )
    total = summed(sums)
    bb, bq, qq, qaq = total[0], total[1], total[2], total[3]
    step_0 = bb / bq
    rr = step_0 * step_0 * qq - bb
    ratio = rr / bb
    grown = 1.0 + ratio
    curve = grown * grown * bq - 2.0 * grown * step_0 * qq + step_0 * step_0 * qaq
    step_1 = rr / curve
    on_own = step_0 + step_1 * grown
    on_image = -step_1 * step_0
    increment = on_own * own + on_image * image_own
    is_final = lax.axis_index("tm") == lax.axis_size("tm") - 1
    scales = jnp.stack([on_own, on_image])

    def last(_):
        (final_back,) = call(last_kernel, [BACK], "svv")(scales, moved, image_moved)
        return gathered(
            exchanged(final_back.reshape(32, -1, LANES)).reshape(32, -1, LANES)[:, : CUTS * UNITS].reshape(32, UNITS, WIDE)
        )

    slid = lax.cond(is_final, last, lambda _: on_own * next_own + on_image * next_image, 0)
    return increment[None, :, None], slid[None, :, None]


def solution(mesh):
    placed = (
        P("tm", None, "lat", None),
        P("tm", "lat", None),
        P("tm", "lat", None),
        P("tm", None, "lat", None),
        P("tm", "lat"),
        P("tm", "lat"),
    )
    return jax.shard_map(
        body,
        mesh=mesh,
        in_specs=placed,
        out_specs=(P("tm", None, "lat", None), P("tm", None, "lat", None)),
        check_vma=False,
    )
```

time: 870 us -> 260 us (0.30)
  the two profiles are of different devices: /device:TPU:26 before, /device:TPU:57 now
where the time goes in v1:
time: 260 us; the launch traced here: 259 us
  waiting for transfers between devices  70.6 us (27%)
  blocking collectives  59.9 us (23%)
  starting transfers between devices  39.3 us (15%)
  Pallas kernels  30.1 us (12%)
  local copies, waits for them, and re-layouts  27.7 us (11%)
  other arithmetic  25.1 us (10%)
  between operations  6.28 us (2%)
    all_to_all x3, waiting for transfers between devices, exchanged(): got = lax.all_to_all(buffer, 'lat', 0, 0, tiled=True)  57.3 us
    all_to_all x2, blocking collectives, summed(): lax.all_to_all(jnp.broadcast_to(tile[None], (count, 8, LANES)), axis, 0,...  39.3 us
    all_to_all x3, starting transfers between devices, exchanged(): got = lax.all_to_all(buffer, 'lat', 0, 0, tiled=True)  25 us
    all_to_all x1, blocking collectives, exchanged(): got = lax.all_to_all(buffer, 'lat', 0, 0, tiled=True)  20.6 us
    pallas_call x1, Pallas kernels, body(): call(functools.partial(image_kernel, rows, got_rows), [PLANES, PLANES, BA...  14.4 us
    ppermute x5, starting transfers between devices, passed_along(): return lax.ppermute(shard, 'tm', pairs)  14.4 us
    ppermute x5, waiting for transfers between devices, passed_along(): return lax.ppermute(shard, 'tm', pairs)  13.3 us
    scatter-add x1, other arithmetic, body(): jnp.zeros((32 * UNITS * WIDE,), jnp.float32).at[place].add(obs_weight[0])  12.3 us
  transfers between devices with their start and end apart: 8, of which 6 were waited for; matrix products, arithmetic and copies ran while one was open for 12% of the time, Pallas kernels for 4%

profile of v1, /device:TPU:57, one launch (start us, length us, event | category | flops | bytes accessed | tf_op | source)
XLA Modules:
  0.0 259.1 jit_solution(10399708773925641713)
XLA Ops:
  0.6 3.2 %reduce.1 = f32[4,49320]{1,0:T(4,128)S(1)} reduce(f32[1,4,1,49320]{3,2,1,0:T(1,128)} %param.8, f32[]{:T(128)} %constant.118), dimensions={0,2}, to_apply=%param.8.reduce_sub_computation | reduce | bytes 1578244 | tf_op args[0]
  12.5 13.2 %all-to-all-start.1 = ((f32[32,88,128]{2,1,0:T(8,128)}), f32[32,88,128]{2,1,0:T(8,128)S(1)}, u32[]{:S(2)}, u32[]{:S(2)}) async-start(f32[32,88,128]{2,1,0:T(8,128)} %select_maximum_fusion.1), calls=%async_computation.1 | async-start | bytes 2883584 | tf_op jit(solution)/shard_map/all_to_all | solution.py:65
  25.7 3.2 %reduce.4 = f32[4,49320]{1,0:T(4,128)} reduce(f32[1,4,1,49320]{3,2,1,0:T(1,128)S(1)} %copy-done.6, f32[]{:T(128)} %constant.118), dimensions={0,2}, to_apply=%param.11.reduce_sub_computation | reduce | bytes 1578244 | tf_op args[3]
  29.0 2.1 reshape_squeeze.15
  36.6 12.3 %scatter_custom_fusion = f32[221184]{0:T(1024)} fusion(s32[2048]{0:T(1024)S(1)} %bitcast.124, f32[2048]{0:T(1024)} %bitcast.125, f32[]{:T(128)} %constant.80.clone.1), kind=kCustom, calls=%fused_computation.32 | custom fusion | flops 2048 | bytes 885248 | tf_op jit(solution)/shard_map/scatter-add | solution.py:287
  51.6 8.0 %all-to-all-done.1 = f32[32,88,128]{2,1,0:T(8,128)S(1)} async-done(((f32[32,88,128]{2,1,0:T(8,128)}), f32[32,88,128]{2,1,0:T(8,128)S(1)}, u32[]{:S(2)}, u32[]{:S(2)}) %all-to-all-start.1) | async-done | bytes 1441824 | tf_op jit(solution)/shard_map/all_to_all | solution.py:65
  59.6 7.6 %all-to-all-start.2 = ((f32[32,112,128]{2,1,0:T(8,128)}), f32[32,112,128]{2,1,0:T(8,128)S(1)}, u32[]{:S(2)}, u32[]{:S(2)}) async-start(f32[32,112,128]{2,1,0:T(8,128)} %select_maximum_fusion), calls=%async_computation.2 | async-start | bytes 3670016 | tf_op jit(solution)/shard_map/all_to_all | solution.py:65
  67.2 9.1 %shard_map.77 = (f32[18,32,384]{2,1,0:T(8,128)S(1)}, f32[18,32,384]{2,1,0:T(8,128)}) custom-call(s32[1]{0:T(128)} %bitcast.5.odd_ref, f32[2816,128]{1,0:T(8,128)S(1)} %bitcast.111), custom_call_target="tpu_custom_call" | custom-call | flops 100000000 | bytes 5308416 | tf_op jit(solution)/shard_map/pallas_call | solution.py:293
  78.5 31.7 %all-to-all-done.2 = f32[32,112,128]{2,1,0:T(8,128)S(1)} async-done(((f32[32,112,128]{2,1,0:T(8,128)}), f32[32,112,128]{2,1,0:T(8,128)S(1)}, u32[]{:S(2)}, u32[]{:S(2)}) %all-to-all-start.2) | async-done | bytes 1835040 | tf_op jit(solution)/shard_map/all_to_all | solution.py:65
  111.4 4.1 %shard_map.78.weighted_ref = f32[18,32,384]{2,1,0:T(8,128)S(1)} custom-call(f32[18,32,384]{2,1,0:T(8,128)S(1)} %copy-done.1, f32[18,32,384]{2,1,0:T(8,128)} %collective-permute-done.arriving_ref, f32[3584,128]{1,0:T(8,128)S(1)} %bitcast.108), custom_call_target="tpu_custom_call" | custom-call | bytes 2654208 | tf_op jit(solution)/shard_map/pallas_call | solution.py:297
  115.5 4.8 %collective-permute-start.1 = (f32[18,32,384]{2,1,0:T(8,128)S(1)}, f32[18,32,384]{2,1,0:T(8,128)S(1)}, u32[]{:S(2)}, u32[]{:S(2)}) collective-permute-start(f32[18,32,384]{2,1,0:T(8,128)S(1)} %shard_map.78.weighted_ref), channel_id=1, source_target_pairs={{32,0},{64,32},{96,64},{128,96},{160,128},{192,160},{224,192},{256... | collective-permute-start | bytes 2654216 | tf_op jit(solution)/shard_map/ppermute | solution.py:254
  120.3 2.0 collective-permute-done.1.later_ref
  122.2 14.4 %shard_map.79 = (f32[18,32,384]{2,1,0:T(8,128)S(1)}, f32[18,32,384]{2,1,0:T(8,128)S(1)}, f32[1792,128]{1,0:T(8,128)}, f32[8,128]{1,0:T(8,128)S(1)}) custom-call(s32[1]{0:T(128)} %bitcast.5.odd_ref, f32[2816,128]{1,0:T(8,128)S(1)} %bitcast.112, f32[3584,128]{1,0:T(8,128)S(1)} %bitcast.109, f32[18,32,384]{2,1,0:T(8,128)S(1)} %copy-done.2, ...), custom_call_target="tpu_custom_call" | custom-call | flops 200000000 | bytes 8073216 | tf_op jit(solution)/shard_map/pallas_call | solution.py:301
  138.0 11.0 %collective-permute-done.2.arriving_ref = f32[18,32,384]{2,1,0:T(8,128)S(1)} collective-permute-done((f32[18,32,384]{2,1,0:T(8,128)S(1)}, f32[18,32,384]{2,1,0:T(8,128)S(1)}, u32[]{:S(2)}, u32[]{:S(2)}) %collective-permute-start.2) | collective-permute-done | bytes 884768 | tf_op jit(solution)/shard_map/ppermute | solution.py:254
  150.1 14.6 %all_to_all.30 = f32[32,8,128]{2,1,0:T(8,128)S(1)} all-to-all(f32[32,8,128]{2,1,0:T(8,128)S(1)} %broadcast_in_dim.37), channel_id=1, replica_groups=mesh['tm'=16,'lat'=32] {'lat'}, dimensions={0} | all-to-all | bytes 262144 | tf_op jit(solution)/shard_map/all_to_all | solution.py:260
  164.7 24.7 %all_to_all.31 = f32[16,8,128]{2,1,0:T(8,128)S(1)} all-to-all(f32[16,8,128]{2,1,0:T(8,128)S(1)} %broadcast_in_dim.38), channel_id=1, replica_groups=mesh['tm'=16,'lat'=32] {'tm'}, dimensions={0} | all-to-all | bytes 131072 | tf_op jit(solution)/shard_map/all_to_all | solution.py:260
  189.4 4.1 %all-to-all-start.5 = ((f32[32,56,128]{2,1,0:T(8,128)}), f32[32,56,128]{2,1,0:T(8,128)S(1)}, u32[]{:S(2)}, u32[]{:S(2)}) async-start(f32[32,56,128]{2,1,0:T(8,128)} %bitcast.47), calls=%async_computation.5 | async-start | bytes 1835008 | tf_op jit(solution)/shard_map/all_to_all | solution.py:65
  199.5 17.6 %all-to-all-done.5 = f32[32,56,128]{2,1,0:T(8,128)S(1)} async-done(((f32[32,56,128]{2,1,0:T(8,128)}), f32[32,56,128]{2,1,0:T(8,128)S(1)}, u32[]{:S(2)}, u32[]{:S(2)}) %all-to-all-start.5) | async-done | bytes 917536 | tf_op jit(solution)/shard_map/all_to_all | solution.py:65
  218.8 1.9 reshape.310
  220.6 5.6 %collective-permute-start.4 = (f32[4,49320]{1,0:T(4,128)}, f32[4,49320]{1,0:T(4,128)}, u32[]{:S(2)}, u32[]{:S(2)}) collective-permute-start(f32[4,49320]{1,0:T(4,128)} %reshape.310), channel_id=1, source_target_pairs={{32,0},{64,32},{96,64},{128,96},{160,128},{192,160},{224,192},{256... | collective-permute-start | bytes 2367368 | tf_op jit(solution)/shard_map/ppermute | solution.py:254
  230.7 1.7 copy.208
  232.7 26.5 %conditional.1 = (f32[1,4,1,49320]{3,2,1,0:T(1,128)}) conditional(s32[]{:T(128)} %convert_element_type.13, (f32[]{:T(128)}, f32[4,49320]{1,0:T(4,128)S(1)}, f32[]{:T(128)}, f32[4,49320]{1,0:T(4,128)}) %tuple.16, (f32[2]{0:T(128)S(1)}, f32[18,32,384]{2,1,0:T(8,128)}, f32[18,32,384]{2,1,0:T(8,128)S(1)}) %tuple.69), branch_computations={%region_3.4_spmd, %region_4.5_spmd} | conditional | flops 799200 | bytes 17767560 | solution.py:335
  234.1 20.6 %all_to_all.29 = f32[32,56,128]{2,1,0:T(8,128)S(1)} all-to-all(f32[32,56,128]{2,1,0:T(8,128)S(1)} %bitcast.113), channel_id=1, replica_groups=mesh['tm'=16,'lat'=32] {'lat'}, dimensions={0} | all-to-all | bytes 1835008 | tf_op jit(solution)/shard_map/cond/branch_1_fun/all_to_all | solution.py:65
  256.4 2.7 %broadcast_in_dim.39 = f32[1,4,1,49320]{3,2,1,0:T(1,128)} reshape(f32[4,360,137]{2,1,0:T(8,128)S(1)} %copy.179) | data formatting | bytes 1578240 | tf_op jit(solution)/shard_map/broadcast_in_dim | solution.py:336
  (117 shorter events, 32.5 us)
Async XLA Ops:
  5.8 1.2 copy-start.7
  8.3 0.9 copy-start.8
  12.5 13.2 %copy-start.6 = (f32[1,4,1,49320]{3,2,1,0:T(1,128)S(1)}, f32[1,4,1,49320]{3,2,1,0:T(1,128)}, u32[]{:S(2)}) copy-start(f32[1,4,1,49320]{3,2,1,0:T(1,128)} %param.11) | copy-start | bytes 2367364
  12.5 47.0 %all-to-all-start.1 = ((f32[32,88,128]{2,1,0:T(8,128)}), f32[32,88,128]{2,1,0:T(8,128)S(1)}, u32[]{:S(2)}, u32[]{:S(2)}) async-start(f32[32,88,128]{2,1,0:T(8,128)} %select_maximum_fusion.1), calls=%async_computation.1 | async-start | bytes 2883584 | tf_op jit(solution)/shard_map/all_to_all | solution.py:65
  35.6 0.7 copy-start.9
  59.6 50.6 %all-to-all-start.2 = ((f32[32,112,128]{2,1,0:T(8,128)}), f32[32,112,128]{2,1,0:T(8,128)S(1)}, u32[]{:S(2)}, u32[]{:S(2)}) async-start(f32[32,112,128]{2,1,0:T(8,128)} %select_maximum_fusion), calls=%async_computation.2 | async-start | bytes 3670016 | tf_op jit(solution)/shard_map/all_to_all | solution.py:65
  76.3 0.9 copy-start
  77.2 33.0 %collective-permute-start = (f32[18,32,384]{2,1,0:T(8,128)}, f32[18,32,384]{2,1,0:T(8,128)}, u32[]{:S(2)}, u32[]{:S(2)}) collective-permute-start(f32[18,32,384]{2,1,0:T(8,128)} %get-tuple-element.34), channel_id=1, source_target_pairs={{0,32},{32,64},{64,96},{96,128},{128,160},{160,192},{192,224},{224... | collective-permute-start | bytes 2654216 | tf_op jit(solution)/shard_map/ppermute | solution.py:254
  110.2 1.2 copy-start.1
  111.4 10.8 %copy-start.2 = (f32[18,32,384]{2,1,0:T(8,128)S(1)}, f32[18,32,384]{2,1,0:T(8,128)}, u32[]{:S(2)}) copy-start(f32[18,32,384]{2,1,0:T(8,128)} %copy-done) | copy-start | bytes 2654212
  115.5 6.8 %collective-permute-start.1 = (f32[18,32,384]{2,1,0:T(8,128)S(1)}, f32[18,32,384]{2,1,0:T(8,128)S(1)}, u32[]{:S(2)}, u32[]{:S(2)}) collective-permute-start(f32[18,32,384]{2,1,0:T(8,128)S(1)} %shard_map.78.weighted_ref), channel_id=1, source_target_pairs={{32,0},{64,32},{96,64},{128,96},{160,128},{192,160},{224,192},{256... | collective-permute-start | bytes 2654216 | tf_op jit(solution)/shard_map/ppermute | solution.py:254
  136.7 13.4 %copy-start.4 = (f32[18,32,384]{2,1,0:T(8,128)}, f32[18,32,384]{2,1,0:T(8,128)S(1)}, u32[]{:S(2)}) copy-start(f32[18,32,384]{2,1,0:T(8,128)S(1)} %get-tuple-element.36) | copy-start | bytes 2654212
  136.7 12.3 %collective-permute-start.2 = (f32[18,32,384]{2,1,0:T(8,128)S(1)}, f32[18,32,384]{2,1,0:T(8,128)S(1)}, u32[]{:S(2)}, u32[]{:S(2)}) collective-permute-start(f32[18,32,384]{2,1,0:T(8,128)S(1)} %get-tuple-element.36), channel_id=1, source_target_pairs={{0,32},{32,64},{64,96},{96,128},{128,160},{160,192},{192,224},{224... | collective-permute-start | bytes 2654216 | tf_op jit(solution)/shard_map/ppermute | solution.py:254
  189.4 27.6 %all-to-all-start.5 = ((f32[32,56,128]{2,1,0:T(8,128)}), f32[32,56,128]{2,1,0:T(8,128)S(1)}, u32[]{:S(2)}, u32[]{:S(2)}) async-start(f32[32,56,128]{2,1,0:T(8,128)} %bitcast.47), calls=%async_computation.5 | async-start | bytes 1835008 | tf_op jit(solution)/shard_map/all_to_all | solution.py:65
  220.6 11.7 %collective-permute-start.4 = (f32[4,49320]{1,0:T(4,128)}, f32[4,49320]{1,0:T(4,128)}, u32[]{:S(2)}, u32[]{:S(2)}) collective-permute-start(f32[4,49320]{1,0:T(4,128)} %reshape.310), channel_id=1, source_target_pairs={{32,0},{64,32},{96,64},{128,96},{160,128},{192,160},{224,192},{256... | collective-permute-start | bytes 2367368 | tf_op jit(solution)/shard_map/ppermute | solution.py:254
  226.8 1.1 copy-start.3
  229.1 3.5 %copy-start.5 = (f32[18,32,384]{2,1,0:T(8,128)S(1)}, f32[18,32,384]{2,1,0:T(8,128)}, u32[]{:S(2)}) copy-start(f32[18,32,384]{2,1,0:T(8,128)} %copy-done.4) | copy-start | bytes 2654212
  229.1 3.5 %collective-permute-start.3 = (f32[4,49320]{1,0:T(4,128)}, f32[4,49320]{1,0:T(4,128)S(1)}, u32[]{:S(2)}, u32[]{:S(2)}) collective-permute-start(f32[4,49320]{1,0:T(4,128)} %get-tuple-element.84), channel_id=1, source_target_pairs={{32,0},{64,32},{96,64},{128,96},{160,128},{192,160},{224,192},{256... | collective-permute-start | bytes 2367368 | tf_op jit(solution)/shard_map/ppermute | solution.py:254

commit v2 on v0

v2 whole, which is shorter than its diff:
```python
import functools
import math

import jax
import jax.numpy as jnp
from jax import lax
from jax.experimental import pallas as pl
from jax.experimental.pallas import tpu as pltpu
from jax.sharding import PartitionSpec as P

LEV = 137
LON = 360
COLS = LON * LEV
STEPS = 3
LANES = 128
CUTS = 3
WIDE = CUTS * LANES
LEFT = 8
RIGHT = WIDE - LEFT - LON
UNITS = 18
SPAN = 5
EVEN_AT, EVEN_N, ODD_AT = (0, 5, 10, 14), (5, 5, 4, 4), (10, 14, 0, 5)


def whole_rows(n):
    return -(-n // 8) * 8


LON_AT = CUTS * UNITS
LAT_AT = LON_AT + CUTS * SPAN
WEIGHT_AT = LAT_AT + CUTS * SPAN
SEND_ROWS = whole_rows(WEIGHT_AT + CUTS * UNITS)
BACK_ROWS = whole_rows(CUTS * UNITS)
PAIR_ROWS = whole_rows(2 * CUTS * UNITS + 4)


def exchanged(buffer):
    chunks = buffer.reshape(32, -1, LANES)
    return lax.all_to_all(chunks, "lat", 0, 0, tiled=True).reshape(-1, LANES)


LEAP = 14


def lay_rows(piece, line):
    at = 0
    while at < COLS:
        if COLS - at >= 8 * LANES:
            line[pl.ds(8 + at // LANES, 8), :] = piece(at, 8 * LANES).reshape(8, LANES)
            at += 8 * LANES
        else:
            n = min(LANES, COLS - at)
            line[pl.ds(8 + at // LANES, 1), pl.ds(0, n)] = piece(at, n)
            at += n


def turn_right(x, by, stride):
    by %= LANES
    extra = by if by + 8 * stride > LANES else 0
    x = pltpu.roll(x, by - extra, 1, stride=stride, stride_axis=0)
    return pltpu.roll(x, extra, 1) if extra else x


def split_longitudes(line, tall, tall_rest):
    lane = lax.broadcasted_iota(jnp.int32, (8, LANES), 1)
    place = lane - 2 * lax.broadcasted_iota(jnp.int32, (8, LANES), 0)
    groups = [8 * LEAP * g for g in range(LON // (8 * LEAP))] + [LON - 8 * LEAP]
    for lon in [g + k for g in groups for k in range(LEAP)]:
        row, first = divmod(LEV * lon, LANES)
        if first < 16:
            row, first = row - 1, first + LANES
        count = 3 if first + LEV - 1 >= 2 * LANES else 2
        r = [
            turn_right(line[pl.ds(8 + row + j, 8, stride=15), :], -first, 2) for j in range(count)
        ]
        t = place + first
        main, rest = jnp.where(t < LANES, r[0], r[1]), r[1]
        if count == 3:
            main = jnp.where(t < 2 * LANES, main, r[2])
            rest = jnp.where(t < LANES, r[1], r[2])
        tall[pl.ds(LEFT + lon, 8, stride=LEAP), :] = main
        tall_rest[pl.ds(LEFT + lon, 8, stride=LEAP), :] = jnp.where(
            lane < LEV - LANES, rest, 0.0
        )


def deal(tall, tall_rest, out_ref, slots):
    for cut in range(CUTS):
        main = tall[pl.ds(cut * LANES, LANES), :].T
        rest = tall_rest[pl.ds(cut * LANES, LANES), :].T
        for i in range(9):
            value = main[16 * i : 16 * i + 16] if i < 8 else rest[:16]
            for parity, row in slots[i](cut):
                out_ref[pl.ds(parity * SEND_ROWS + row, 16, stride=2 * SEND_ROWS), :] = value


def slots_of_field(f, base):
    def slot(i):
        even = i < EVEN_N[f]
        unit = EVEN_AT[f] + i if even else ODD_AT[f] + i - EVEN_N[f]
        return lambda cut: [(0 if even else 1, base + cut * UNITS + unit)]

    return [slot(i) for i in range(9)]


def slots_of_level(base):
    def slot(i):
        return lambda cut: [
            (parity, base + cut * SPAN + i - 4 * parity)
            for parity in (0, 1)
            if 0 <= i - 4 * parity < SPAN
        ]

    return [slot(i) for i in range(9)]


def pack_kernel(
    own_hbm, lon_hbm, lat_hbm, weight_hbm, out_ref, own, lon, lat, weight, line, tall, tall_rest, sems
):
    copies = [
        pltpu.make_async_copy(src, dst, sems.at[k])
        for k, (src, dst) in enumerate(
            ((own_hbm, own), (lon_hbm, lon), (lat_hbm, lat), (weight_hbm, weight))
        )
    ]
    for copy in copies:
        copy.start()
    line[...] = jnp.zeros_like(line)
    tall[...] = jnp.zeros_like(tall)
    tall_rest[...] = jnp.zeros_like(tall_rest)
    for row in range(WEIGHT_AT + CUTS * UNITS, SEND_ROWS):
        out_ref[pl.ds(row, 32, stride=SEND_ROWS), :] = jnp.zeros((32, LANES), jnp.float32)

    def one(piece, slots):
        lay_rows(piece, line)
        split_longitudes(line, tall, tall_rest)
        deal(tall, tall_rest, out_ref, slots)

    copies[0].wait()
    for f in range(4):
        one(lambda at, n: own[0, f, :, pl.ds(at, n)], slots_of_field(f, 0))
    copies[1].wait()
    one(lambda at, n: lon[0, :, pl.ds(at, n)], slots_of_level(LON_AT))
    copies[2].wait()
    one(lambda at, n: lat[0, :, pl.ds(at, n)], slots_of_level(LAT_AT))
    copies[3].wait()
    for f in range(4):
        one(lambda at, n: weight[0, f, :, pl.ds(at, n)], slots_of_field(f, WEIGHT_AT))


def pack(*arrays):
    scratch = [pltpu.VMEM(x.shape, jnp.float32) for x in arrays]
    scratch += [pltpu.VMEM((408, LANES), jnp.float32)]
    scratch += [pltpu.VMEM((WIDE, LANES), jnp.float32)] * 2 + [pltpu.SemaphoreType.DMA((4,))]
    return pl.pallas_call(
        pack_kernel,
        out_shape=jax.ShapeDtypeStruct((32 * SEND_ROWS, LANES), jnp.float32),
        in_specs=[pl.BlockSpec(memory_space=pl.ANY)] * 4,
        out_specs=VMEM,
        scratch_shapes=scratch,
        compiler_params=pltpu.CompilerParams(vmem_limit_bytes=60 * 2**20),
    )(*arrays)


def collect(load, f, tall, tall_rest):
    for cut in range(CUTS):
        parts = []
        for i in range(9):
            even = i < EVEN_N[f]
            unit = EVEN_AT[f] + i if even else ODD_AT[f] + i - EVEN_N[f]
            parts.append(load(0 if even else 1, cut * UNITS + unit))
        rest = jnp.concatenate([parts[8], jnp.zeros((LANES - 16, LANES), jnp.float32)], 0)
        main, rest = jnp.concatenate(parts[:8], 0).T, rest.T
        for at in range(0, LANES, 8):
            lon = cut * LANES + at - LEFT
            for source, held in ((main, tall), (rest, tall_rest)):
                held[pl.ds(cut * LANES + at, 8), :] = turn_right(
                    source[at : at + 8], LEV * lon, LEV - LANES
                )


def join_longitudes(tall, tall_rest, put_piece):
    lane = lax.broadcasted_iota(jnp.int32, (8, LANES), 1)
    place = lane - 9 * lax.broadcasted_iota(jnp.int32, (8, LANES), 0)
    for at in range(0, COLS, 8 * LANES):
        lon, first = divmod(at, LEV)
        if first < 7 * 9:
            lon, first = lon - 1, first + LEV
        value = None
        for ahead in range(3):
            for source, low, high in ((tall, 0, LANES), (tall_rest, LANES, LEV)):
                low, high = low + LEV * ahead, high + LEV * ahead
                if first - 7 * 9 >= high or first + LANES - 1 < low:
                    continue
                x = source[pl.ds(LEFT + lon + ahead, 8), :]
                value = x if value is None else jnp.where(place + first < low, value, x)
        if COLS - at >= 8 * LANES:
            put_piece(at, value.reshape(1, 8 * LANES))
        else:
            for row in range(whole_rows(COLS - at) // LANES + 1):
                n = min(LANES, COLS - at - row * LANES)
                if n > 0:
                    put_piece(at + row * LANES, value[row : row + 1, :n])


def unpack_kernel(got_ref, out_ref, tall, tall_rest):
    def load(parity, row):
        return got_ref[pl.ds(parity * BACK_ROWS + row, 16, stride=2 * BACK_ROWS), :]

    write_fields(load, out_ref, tall, tall_rest)


def write_fields(load, out_ref, tall, tall_rest):
    tall[pl.ds(WIDE, 16), :] = jnp.zeros((16, LANES), jnp.float32)
    tall_rest[pl.ds(WIDE, 16), :] = jnp.zeros((16, LANES), jnp.float32)
    for f in range(4):

        def put_piece(at, value):
            out_ref[0, f, :, pl.ds(at, value.shape[1])] = value

        collect(load, f, tall, tall_rest)
        join_longitudes(tall, tall_rest, put_piece)


def pieces():
    size = 8 * 8 * LANES
    return [(at, min(size, COLS - at)) for at in range(0, COLS, size)]


def combined(out_ref, on_first, first_ref, on_second, second_ref):
    for f in range(4):
        for at, n in pieces():
            part = (0, f, slice(None), pl.ds(at, n))
            out_ref[part] = on_first * first_ref[part] + on_second * second_ref[part]


def last_kernel(got_ref, own_ref, image_ref, increment_ref, slid_ref, tall, tall_rest):
    on_own, on_image = scales_in(got_ref, PAIR_ROWS, 2 * CUTS * UNITS)

    def load(parity, row):
        first = pl.ds(parity * PAIR_ROWS + row, 16, stride=2 * PAIR_ROWS)
        second = pl.ds(parity * PAIR_ROWS + CUTS * UNITS + row, 16, stride=2 * PAIR_ROWS)
        return on_own * got_ref[first, :] + on_image * got_ref[second, :]

    write_fields(load, slid_ref, tall, tall_rest)
    combined(increment_ref, on_own, own_ref, on_image, image_ref)


def other_kernel(
    got_ref, own_ref, image_ref, next_own_ref, next_got_ref, increment_ref, slid_ref, next_image,
    tall, tall_rest,
):
    on_own, on_image = scales_in(got_ref, 8, 0)
    unpack_kernel(next_got_ref, next_image, tall, tall_rest)
    combined(slid_ref, on_own, next_own_ref, on_image, next_image)
    combined(increment_ref, on_own, own_ref, on_image, image_ref)


def plane_of(ref, rows, first, step=UNITS):
    return [ref[pl.ds(first + cut * step, 32, stride=rows), :] for cut in range(CUTS)]


def put_rows(ref, rows, first, blocks):
    for cut in range(CUTS):
        ref[pl.ds(first + cut * UNITS, 32, stride=rows), :] = blocks[cut]


def get(ref, *place):
    return [ref[(*place, slice(None), pl.ds(cut * LANES, LANES))] for cut in range(CUTS)]


def put(ref, blocks, *place):
    for cut in range(CUTS):
        ref[(*place, slice(None), pl.ds(cut * LANES, LANES))] = blocks[cut]


def index_of(dim):
    return lax.broadcasted_iota(jnp.int32, (32, LANES), dim)


def wrapped(v):
    lane = index_of(1)
    first, middle, last = v
    return [
        jnp.where(lane < LEFT, pltpu.roll(last, LEFT + RIGHT, 1), first),
        middle,
        jnp.where(lane >= LANES - RIGHT, pltpu.roll(first, LANES - LEFT - RIGHT, 1), last),
    ]


def fill_coefficients(got_ref, rows, coef):
    lat = index_of(0)
    for level in range(SPAN):
        lon_part = wrapped(plane_of(got_ref, rows, LON_AT + level, SPAN))
        lat_part = wrapped(plane_of(got_ref, rows, LAT_AT + level, SPAN))
        pairs = list(zip(lon_part, lat_part))
        put(coef, [1.0 - jnp.abs(a) - jnp.abs(c) for a, c in pairs], level, 0)
        put(coef, [jnp.maximum(a, 0.0) for a in lon_part], level, 1)
        put(coef, [jnp.maximum(-a, 0.0) for a in lon_part], level, 2)
        put(coef, [jnp.where(lat == 0, 0.0, jnp.maximum(c, 0.0)) for c in lat_part], level, 3)
        put(coef, [jnp.where(lat == 31, 0.0, jnp.maximum(-c, 0.0)) for c in lat_part], level, 4)


def level_of(unit, odd):
    return jnp.where(unit < 10, lax.rem(unit, 5), lax.rem(unit - 10, 4) + odd)


def from_west(v):
    lane = index_of(1)
    r = [pltpu.roll(x, 1, 1) for x in v]
    return [r[0]] + [jnp.where(lane == 0, r[i - 1], r[i]) for i in range(1, CUTS)]


def from_east(v):
    lane = index_of(1)
    r = [pltpu.roll(x, LANES - 1, 1) for x in v]
    return [jnp.where(lane == LANES - 1, r[i + 1], r[i]) for i in range(CUTS - 1)] + [r[-1]]


def from_south(v):
    return [pltpu.roll(x, 1, 0) for x in v]


def from_north(v):
    return [pltpu.roll(x, 31, 0) for x in v]


def times(coef, level, kind, v):
    return [k * x for k, x in zip(get(coef, level, kind), v)]


def added(*terms):
    return [sum(t[1:], t[0]) for t in zip(*terms)]


def forward(v, coef, level):
    for step in range(STEPS):
        v = added(
            times(coef, level, 0, v),
            times(coef, level, 1, from_west(v)),
            times(coef, level, 2, from_east(v)),
            times(coef, level, 3, from_south(v)),
            times(coef, level, 4, from_north(v)),
        )
    return v


def backward(v, coef, level):
    for step in range(STEPS):
        v = added(
            times(coef, level, 0, v),
            from_east(times(coef, level, 1, v)),
            from_west(times(coef, level, 2, v)),
            from_north(times(coef, level, 3, v)),
            from_south(times(coef, level, 4, v)),
        )
    return v


def row_sum(v):
    lane = index_of(1)
    total = (
        jnp.where(lane >= LEFT, v[0], 0.0) + v[1] + jnp.where(lane < LANES - RIGHT, v[2], 0.0)
    )
    return jnp.sum(total, axis=0, keepdims=True)


def product(*factors):
    return [math.prod(f[1:], start=f[0]) for f in zip(*factors)]


def clear_rest(ref, rows):
    for row in range(CUTS * UNITS, rows):
        ref[pl.ds(row, 32, stride=rows), :] = jnp.zeros((32, LANES), jnp.float32)


def moved_kernel(odd_ref, got_ref, mark_ref, state_ref, moved_ref, back_ref, coef_ref):
    fill_coefficients(got_ref, SEND_ROWS, coef_ref)
    odd = odd_ref[0]

    def one(unit, carry):
        v = wrapped(plane_of(got_ref, SEND_ROWS, unit))
        put(state_ref, v, unit)
        v = forward(v, coef_ref, level_of(unit, odd))
        put(moved_ref, v, unit)
        put_rows(back_ref, BACK_ROWS, unit, v)
        return carry

    lax.fori_loop(0, UNITS, one, 0, unroll=3)
    clear_rest(back_ref, BACK_ROWS)


def weighted_kernel(state_ref, arriving_ref, got_ref, weighted_ref):
    def one(unit, carry):
        w = wrapped(plane_of(got_ref, SEND_ROWS, WEIGHT_AT + unit))
        pairs = zip(w, get(state_ref, unit), get(arriving_ref, unit))
        put(weighted_ref, [k * (s - m) for k, s, m in pairs], unit)
        return carry

    lax.fori_loop(0, UNITS, one, 0, unroll=3)


def adjoint_kernel(odd_ref, coef_ref, weighted_ref, later_ref, part_ref):
    odd = odd_ref[0]

    def one(unit, carry):
        pulled = backward(get(later_ref, unit), coef_ref, level_of(unit, odd))
        put(part_ref, [w - p for w, p in zip(get(weighted_ref, unit), pulled)], unit)
        return carry

    lax.fori_loop(0, UNITS, one, 0, unroll=3)


def image_kernel(
    odd_ref, coef_ref, obs_ref, state_ref, part_ref,
    image_ref, moved_ref, back_ref, moved_back_ref, sums_ref,
):
    odd = odd_ref[0]

    def one(unit, carry):
        state = get(state_ref, unit)
        obs = plane_of(obs_ref, BACK_ROWS, unit)
        image = [p + k * s for p, k, s in zip(get(part_ref, unit), obs, state)]
        image = wrapped(image)
        put(image_ref, image, unit)
        put_rows(back_ref, BACK_ROWS, unit, image)
        moved = forward(image, coef_ref, level_of(unit, odd))
        put(moved_ref, moved, unit)
        put_rows(moved_back_ref, BACK_ROWS, unit, moved)
        own, cross, square, seen = carry
        return (
            own + row_sum(product(state, state)),
            cross + row_sum(product(image, state)),
            square + row_sum(product(image, image)),
            seen + row_sum(product(obs, image, image)),
        )

    zero = jnp.zeros((1, LANES), jnp.float32)
    sums = lax.fori_loop(0, UNITS, one, (zero, zero, zero, zero), unroll=3)
    for row in range(4):
        sums_ref[row : row + 1, :] = sums[row]
    sums_ref[4:8, :] = jnp.zeros((4, LANES), jnp.float32)
    clear_rest(back_ref, BACK_ROWS)
    clear_rest(moved_back_ref, BACK_ROWS)


def norm_kernel(image_ref, arriving_ref, got_ref, sums_ref, out_ref):
    def one(unit, carry):
        w = plane_of(got_ref, SEND_ROWS, WEIGHT_AT + unit)
        change = [q - m for q, m in zip(get(image_ref, unit), get(arriving_ref, unit))]
        return carry + row_sum(product(w, change, change))

    total = lax.fori_loop(0, UNITS, one, jnp.zeros((1, LANES), jnp.float32), unroll=3)
    out_ref[...] = sums_ref[...]
    out_ref[3:4, :] += total


VMEM = pl.BlockSpec(memory_space=pltpu.VMEM)
SMEM = pl.BlockSpec(memory_space=pltpu.SMEM)
PLANES = jax.ShapeDtypeStruct((UNITS, 32, WIDE), jnp.float32)
BACK = jax.ShapeDtypeStruct((32 * BACK_ROWS, LANES), jnp.float32)
SUMS = jax.ShapeDtypeStruct((8, LANES), jnp.float32)
COEF = jax.ShapeDtypeStruct((SPAN, 5, 32, WIDE), jnp.float32)


def call(kernel, outs, ins, flops=0, extra=()):
    moved = sum(4 * math.prod(o.shape) for o in outs)
    return pl.pallas_call(
        kernel,
        out_shape=outs,
        in_specs=[SMEM if i == "s" else VMEM for i in ins],
        out_specs=[VMEM] * len(outs),
        scratch_shapes=list(extra),
        compiler_params=pltpu.CompilerParams(vmem_limit_bytes=16 * 2**20),
        cost_estimate=pl.CostEstimate(flops=flops, bytes_accessed=3 * moved, transcendentals=0),
    )


def passed_along(shard, by):
    devices = lax.axis_size("tm")
    pairs = [(i, i + by) for i in range(devices) if 0 <= i + by < devices]
    return lax.ppermute(shard, "tm", pairs)


def summed_over_tm(tile):
    count, stride = lax.axis_size("tm"), 1
    while stride < count:
        tile = tile + lax.ppermute(tile, "tm", [(i, i ^ stride) for i in range(count)])
        stride *= 2
    return tile


def scales_of(bb, bq, qq, qaq):
    step_0 = bb / bq
    rr = step_0 * step_0 * qq - bb
    grown = 1.0 + rr / bb
    curve = grown * grown * bq - 2.0 * grown * step_0 * qq + step_0 * step_0 * qaq
    step_1 = rr / curve
    return step_0 + step_1 * grown, -step_1 * step_0


def scales_in(got_ref, rows, first):
    return scales_of(
        *(jnp.sum(got_ref[pl.ds(first + k, 32, stride=rows), :], keepdims=True) for k in range(4))
    )


TALL = [pltpu.VMEM((WIDE + 16, LANES), jnp.float32)] * 2


def blocks_of(buffer):
    return buffer.reshape(32, -1, LANES)


def cells_in_planes(cell, weight):
    field, column = cell // COLS, cell % COLS
    lon, lev = column // LEV, column % LEV
    pair, inside = lev % 16, lev // 16
    low = field < 2
    is_even = inside < jnp.where(low, 5, 4)
    slot = field % 2
    unit = jnp.where(
        is_even,
        jnp.where(low, slot * 5 + inside, 10 + slot * 4 + inside),
        jnp.where(low, 10 + slot * 4 + inside - 5, slot * 5 + inside - 4),
    )
    lane = lon + LEFT
    row = (2 * pair + jnp.where(is_even, 0, 1)) * BACK_ROWS + lane // LANES * UNITS + unit
    empty = jnp.zeros((32 * BACK_ROWS * LANES,), jnp.float32)
    return empty.at[row * LANES + lane % LANES].add(weight).reshape(32 * BACK_ROWS, LANES)


def body(forcing_rhs, courant_lon, courant_lat, error_weight, obs_cell, obs_weight):
    odd = lax.rem(lax.axis_index("lat"), 2).reshape(1)
    got = exchanged(pack(forcing_rhs, courant_lon, courant_lat, error_weight))
    obs = cells_in_planes(obs_cell[0], obs_weight[0])
    next_own = passed_along(forcing_rhs, -1)
    got, mark, next_own = lax.optimization_barrier((got, obs[:8], next_own))
    got_obs = exchanged(obs)

    state, moved, moved_back, coef = call(
        moved_kernel, [PLANES, PLANES, BACK, COEF], "svv", 10**8
    )(odd, got, mark)
    arriving = passed_along(moved, 1)
    (weighted,) = call(weighted_kernel, [PLANES], "vvv")(state, arriving, got)
    later = passed_along(weighted, -1)
    (part,) = call(adjoint_kernel, [PLANES], "svvv", 10**8)(odd, coef, weighted, later)
    image, image_moved, image_back, image_moved_back, sums = call(
        image_kernel, [PLANES, PLANES, BACK, BACK, SUMS], "svvvv", 10**8
    )(odd, coef, got_obs, state, part)
    row_shape = jax.ShapeDtypeStruct(forcing_rhs.shape, jnp.float32)
    got_image = exchanged(image_back)
    image_arriving = passed_along(image_moved, 1)
    (sums,) = call(norm_kernel, [SUMS], "vvvv")(image, image_arriving, got, sums)
    got_image, sums = lax.optimization_barrier((got_image, sums))
    next_got_image = passed_along(got_image, -1)
    (image_own,) = call(unpack_kernel, [row_shape], "v", 10**7, TALL)(got_image)
    sums = summed_over_tm(sums)
    sums, image_own, next_got_image = lax.optimization_barrier((sums, image_own, next_got_image))

    is_final = lax.axis_index("tm") == lax.axis_size("tm") - 1

    def last(tile):
        parts = [
            blocks_of(moved_back)[:, : CUTS * UNITS],
            blocks_of(image_moved_back)[:, : CUTS * UNITS],
            jnp.broadcast_to(tile[None, :4], (32, 4, LANES)),
        ]
        back = exchanged(jnp.concatenate(parts, 1).reshape(-1, LANES))
        return call(last_kernel, [row_shape] * 2, "vvv", 10**7, TALL)(back, forcing_rhs, image_own)

    def other(tile):
        back = exchanged(jnp.broadcast_to(tile[None], (32, 8, LANES)).reshape(-1, LANES))
        scratch = [pltpu.VMEM(forcing_rhs.shape, jnp.float32), *TALL]
        return call(other_kernel, [row_shape] * 2, "vvvvv", 10**7, scratch)(
            back, forcing_rhs, image_own, next_own, next_got_image
        )

    return tuple(lax.cond(is_final, last, other, sums))


def solution(mesh):
    placed = (
        P("tm", None, "lat", None),
        P("tm", "lat", None),
        P("tm", "lat", None),
        P("tm", None, "lat", None),
        P("tm", "lat"),
        P("tm", "lat"),
    )
    return jax.shard_map(
        body,
        mesh=mesh,
        in_specs=placed,
        out_specs=(P("tm", None, "lat", None), P("tm", None, "lat", None)),
        check_vma=False,
    )
```

time: 870 us -> 224 us (0.26)
  the two profiles are of different devices: /device:TPU:26 before, /device:TPU:57 now
where the time goes in v2:
time: 224 us; the launch traced here: 223 us
  starting transfers between devices  73.9 us (33%)
  waiting for transfers between devices  62.1 us (28%)
  blocking collectives  33.5 us (15%)
  Pallas kernels  26.1 us (12%)
  other arithmetic  14.3 us (6%)
  local copies, waits for them, and re-layouts  12.4 us (6%)
    all_to_all x3, waiting for transfers between devices, exchanged(): return lax.all_to_all(chunks, 'lat', 0, 0, tiled=True).reshape(-1, LANES)  47.9 us
    all_to_all x1, blocking collectives, exchanged(): return lax.all_to_all(chunks, 'lat', 0, 0, tiled=True).reshape(-1, LANES)  33.5 us
    ppermute x5, starting transfers between devices, passed_along(): return lax.ppermute(shard, 'tm', pairs)  29.4 us
    all_to_all x3, starting transfers between devices, exchanged(): return lax.all_to_all(chunks, 'lat', 0, 0, tiled=True).reshape(-1, LANES)  28.1 us
    ppermute x4, starting transfers between devices, summed_over_tm(): lax.ppermute(tile, 'tm', [(i, i ^ stride) for i in range(count)])  16.3 us
    scatter-add x1, other arithmetic, cells_in_planes(): empty.at[row * LANES + lane % LANES].add(weight)  12.4 us
    unnamed x28, local copies, waits for them, and re-layouts  11.7 us
    pallas_call x1, Pallas kernels, pack(): pl.pallas_call(pack_kernel, out_shape=jax.ShapeDtypeStruct((32 * SEND_ROW...  8.62 us
  transfers between devices with their start and end apart: 12, of which 9 were waited for; matrix products, arithmetic and copies ran while one was open for 6% of the time, Pallas kernels for 3%

profile of v2, /device:TPU:57, one launch (start us, length us, event | category | flops | bytes accessed | tf_op | source)
XLA Modules:
  0.0 223.2 jit_solution(14104302395529486920)
XLA Ops:
  0.6 8.6 %shard_map.81 = f32[4608,128]{1,0:T(8,128)} custom-call(f32[1,4,1,49320]{3,2,1,0:T(1,128)} %own_hbm.1, f32[1,1,49320]{2,1,0:T(1,128)} %lon_hbm.1, f32[1,1,49320]{2,1,0:T(1,128)} %lat_hbm.1, f32[1,4,1,49320]{3,2,1,0:T(1,128)} %weight_hbm.1), custom_call_target="tpu_custom_call" | custom-call | tf_op jit(solution)/shard_map/pallas_call | solution.py:155
  9.3 13.0 %all-to-all-start.2 = ((f32[32,144,128]{2,1,0:T(8,128)}), f32[32,144,128]{2,1,0:T(8,128)S(1)}, u32[]{:S(2)}, u32[]{:S(2)}) async-start(f32[32,144,128]{2,1,0:T(8,128)} %bitcast.49), calls=%async_computation.2 | async-start | bytes 4718592 | tf_op jit(solution)/shard_map/all_to_all | solution.py:39
  22.3 3.8 %collective-permute-start = (f32[1,4,1,49320]{3,2,1,0:T(1,128)S(1)}, f32[1,4,1,49320]{3,2,1,0:T(1,128)}, u32[]{:S(2)}, u32[]{:S(2)}) collective-permute-start(f32[1,4,1,49320]{3,2,1,0:T(1,128)S(1)} %copy-done.12), channel_id=1, source_target_pairs={{32,0},{64,32},{96,64},{128,96},{160,128},{192,160},{224,192},{256... | collective-permute-start | bytes 2367368 | tf_op jit(solution)/shard_map/ppermute | solution.py:482
  26.4 12.4 %scatter_custom_fusion = f32[229376]{0:T(1024)} fusion(s32[2048]{0:T(1024)S(1)} %bitcast.53, f32[2048]{0:T(1024)} %bitcast.54, f32[]{:T(128)} %constant.102.clone.1), kind=kCustom, calls=%fused_computation.2 | custom fusion | flops 2048 | bytes 918016 | tf_op jit(solution)/shard_map/scatter-add | solution.py:530
  39.5 37.2 %all-to-all-done.2 = f32[32,144,128]{2,1,0:T(8,128)S(1)} async-done(((f32[32,144,128]{2,1,0:T(8,128)}), f32[32,144,128]{2,1,0:T(8,128)S(1)}, u32[]{:S(2)}, u32[]{:S(2)}) %all-to-all-start.2) | async-done | bytes 2359328 | tf_op jit(solution)/shard_map/all_to_all | solution.py:39
  76.7 4.3 %shard_map.82 = (f32[18,32,384]{2,1,0:T(8,128)S(1)}, f32[18,32,384]{2,1,0:T(8,128)}, f32[1792,128]{1,0:T(8,128)}, f32[5,5,32,384]{3,2,1,0:T(8,128)S(1)}) custom-call(s32[1]{0:T(128)} %bitcast.4.odd_ref, f32[4608,128]{1,0:T(8,128)S(1)} %bitcast.40, f32[8,128]{1,0:T(8,128)S(1)} %slice_bitcast_fusion.mark_ref), custom_call_target="tpu_custom_call" | custom-call | flops 100000000 | bytes 11747328 | tf_op jit(solution)/shard_map/pallas_call | solution.py:541
  84.3 7.3 %all-to-all-start.3 = ((f32[32,56,128]{2,1,0:T(8,128)}), f32[32,56,128]{2,1,0:T(8,128)S(1)}, u32[]{:S(2)}, u32[]{:S(2)}) async-start(f32[32,56,128]{2,1,0:T(8,128)} %bitcast.50), calls=%async_computation.3 | async-start | bytes 1835008 | tf_op jit(solution)/shard_map/all_to_all | solution.py:39
  92.7 1.9 shard_map.83.weighted_ref
  94.6 12.4 %collective-permute-start.2 = (f32[18,32,384]{2,1,0:T(8,128)S(1)}, f32[18,32,384]{2,1,0:T(8,128)S(1)}, u32[]{:S(2)}, u32[]{:S(2)}) collective-permute-start(f32[18,32,384]{2,1,0:T(8,128)S(1)} %shard_map.83.weighted_ref), channel_id=1, source_target_pairs={{32,0},{64,32},{96,64},{128,96},{160,128},{192,160},{224,192},{256... | collective-permute-start | bytes 2654216 | tf_op jit(solution)/shard_map/ppermute | solution.py:482
  107.0 2.0 collective-permute-done.2.later_ref
  109.0 2.6 %shard_map.84.part_ref = f32[18,32,384]{2,1,0:T(8,128)S(1)} custom-call(s32[1]{0:T(128)} %bitcast.4.odd_ref, f32[5,5,32,384]{3,2,1,0:T(8,128)S(1)} %copy-done.1, f32[18,32,384]{2,1,0:T(8,128)S(1)} %shard_map.83.weighted_ref, f32[18,32,384]{2,1,0:T(8,128)S(1)} %collective-permute-done.2.later_ref), custom_call_target="tpu_custom_call" | custom-call | flops 100000000 | bytes 2654208 | tf_op jit(solution)/shard_map/pallas_call | solution.py:547
  117.3 3.8 %shard_map.85 = (f32[18,32,384]{2,1,0:T(8,128)S(1)}, f32[18,32,384]{2,1,0:T(8,128)S(1)}, f32[1792,128]{1,0:T(8,128)S(1)}, f32[1792,128]{1,0:T(8,128)}, f32[8,128]{1,0:T(8,128)S(1)}) custom-call(s32[1]{0:T(128)} %bitcast.4.odd_ref, f32[5,5,32,384]{3,2,1,0:T(8,128)S(1)} %copy-done.2, f32[1792,128]{1,0:T(8,128)S(1)} %bitcast.46, f32[18,32,384]{2,1,0:T(8,128)S(1)} %copy-done.5, ...), custom_call_target="tpu_custom_call" | custom-call | flops 100000000 | bytes 10825728 | tf_op jit(solution)/shard_map/pallas_call | solution.py:548
  123.8 7.8 %all-to-all-start.4 = ((f32[32,56,128]{2,1,0:T(8,128)}), f32[32,56,128]{2,1,0:T(8,128)S(1)}, u32[]{:S(2)}, u32[]{:S(2)}) async-start(f32[32,56,128]{2,1,0:T(8,128)} %bitcast.47), calls=%async_computation.4 | async-start | bytes 1835008 | tf_op jit(solution)/shard_map/all_to_all | solution.py:39
  132.9 6.3 %collective-permute-done.3.arriving_ref = f32[18,32,384]{2,1,0:T(8,128)S(1)} collective-permute-done((f32[18,32,384]{2,1,0:T(8,128)}, f32[18,32,384]{2,1,0:T(8,128)S(1)}, u32[]{:S(2)}, u32[]{:S(2)}) %collective-permute-start.3) | collective-permute-done | bytes 884768 | tf_op jit(solution)/shard_map/ppermute | solution.py:482
  140.9 9.5 %all-to-all-done.4 = f32[32,56,128]{2,1,0:T(8,128)S(1)} async-done(((f32[32,56,128]{2,1,0:T(8,128)}), f32[32,56,128]{2,1,0:T(8,128)S(1)}, u32[]{:S(2)}, u32[]{:S(2)}) %all-to-all-start.4) | async-done | bytes 917536 | tf_op jit(solution)/shard_map/all_to_all | solution.py:39
  150.4 10.7 %collective-permute-start.8 = (f32[1792,128]{1,0:T(8,128)S(1)}, f32[1792,128]{1,0:T(8,128)}, u32[]{:S(2)}, u32[]{:S(2)}) collective-permute-start(f32[1792,128]{1,0:T(8,128)S(1)} %bitcast.44), channel_id=1, source_target_pairs={{32,0},{64,32},{96,64},{128,96},{160,128},{192,160},{224,192},{256... | collective-permute-start | bytes 2752520 | tf_op jit(solution)/shard_map/ppermute | solution.py:482
  161.1 5.1 %collective-permute-start.4 = (f32[8,128]{1,0:T(8,128)S(1)}, f32[8,128]{1,0:T(8,128)S(1)}, u32[]{:S(2)}, u32[]{:S(2)}) collective-permute-start(f32[8,128]{1,0:T(8,128)S(1)} %shard_map.86), channel_id=1, source_target_pairs={{0,32},{32,0},{64,96},{96,64},{128,160},{160,128},{192,224},{224,1... | collective-permute-start | bytes 12296 | tf_op jit(solution)/shard_map/ppermute | solution.py:488
  167.1 3.0 %collective-permute-start.5 = (f32[8,128]{1,0:T(8,128)S(1)}, f32[8,128]{1,0:T(8,128)S(1)}, u32[]{:S(2)}, u32[]{:S(2)}) collective-permute-start(f32[8,128]{1,0:T(8,128)S(1)} %add.234), channel_id=1, source_target_pairs={{0,64},{32,96},{64,0},{96,32},{128,192},{160,224},{192,128},{224,1... | collective-permute-start | bytes 12296 | tf_op jit(solution)/shard_map/ppermute | solution.py:488
  171.4 4.0 %collective-permute-start.6 = (f32[8,128]{1,0:T(8,128)S(1)}, f32[8,128]{1,0:T(8,128)S(1)}, u32[]{:S(2)}, u32[]{:S(2)}) collective-permute-start(f32[8,128]{1,0:T(8,128)S(1)} %add.235), channel_id=1, source_target_pairs={{0,128},{32,160},{64,192},{96,224},{128,0},{160,32},{192,64},{224,... | collective-permute-start | bytes 12296 | tf_op jit(solution)/shard_map/ppermute | solution.py:488
  176.6 4.2 %collective-permute-start.7 = (f32[8,128]{1,0:T(8,128)S(1)}, f32[8,128]{1,0:T(8,128)S(1)}, u32[]{:S(2)}, u32[]{:S(2)}) collective-permute-start(f32[8,128]{1,0:T(8,128)S(1)} %add.236), channel_id=1, source_target_pairs={{0,256},{32,288},{64,320},{96,352},{128,384},{160,416},{192,448},{... | collective-permute-start | bytes 12296 | tf_op jit(solution)/shard_map/ppermute | solution.py:488
  182.3 2.6 %collective-permute-done.7 = f32[8,128]{1,0:T(8,128)S(1)} collective-permute-done((f32[8,128]{1,0:T(8,128)S(1)}, f32[8,128]{1,0:T(8,128)S(1)}, u32[]{:S(2)}, u32[]{:S(2)}) %collective-permute-start.7) | collective-permute-done | bytes 4128 | tf_op jit(solution)/shard_map/ppermute | solution.py:488
  184.9 38.3 %conditional.1 = ((f32[1,4,1,49320]{3,2,1,0:T(1,128)}, f32[1,4,1,49320]{3,2,1,0:T(1,128)})) conditional(s32[]{:T(128)} %convert_element_type.3, (f32[8,128]{1,0:T(8,128)S(1)}, f32[1,4,1,49320]{3,2,1,0:T(1,128)}, f32[1,4,1,49320]{3,2,1,0:T(1,128)S(1)}, f32[1,4,1,49320]{3,2,1,0:T(1,128)}, f32[1792,128]{1,0:T(8,128)}) %tuple.19, (f32[1792,128]{1,0:T(8,128)}, ...), branch_computations={%region_1.2_spmd, %region_2.3_spmd} | conditional | flops 10917504 | bytes 15302948 | solution.py:579
  186.6 33.5 %all_to_all.24 = f32[32,112,128]{2,1,0:T(8,128)S(1)} all-to-all(f32[32,112,128]{2,1,0:T(8,128)S(1)} %pad_maximum_fusion), channel_id=1, replica_groups=mesh['tm'=16,'lat'=32] {'lat'}, dimensions={0} | all-to-all | bytes 3670016 | tf_op jit(solution)/shard_map/cond/branch_1_fun/all_to_all | solution.py:39
  220.1 3.1 %branch_1_fun.1 = (f32[1,4,1,49320]{3,2,1,0:T(1,128)}, f32[1,4,1,49320]{3,2,1,0:T(1,128)}) custom-call(f32[3584,128]{1,0:T(8,128)S(1)} %bitcast.43, f32[1,4,1,49320]{3,2,1,0:T(1,128)S(1)} %copy-done.13, f32[1,4,1,49320]{3,2,1,0:T(1,128)S(1)} %get-tuple-element.29.image_ref), custom_call_target="tpu_custom_call" | custom-call | flops 10000000 | bytes 4734720 | tf_op jit(solution)/shard_map/cond/branch_1_fun/pallas_call | solution.py:570
  (50 shorter events, 23.3 us)
Async XLA Ops:
  9.3 13.1 %copy-start.12 = (f32[1,4,1,49320]{3,2,1,0:T(1,128)S(1)}, f32[1,4,1,49320]{3,2,1,0:T(1,128)}, u32[]{:S(2)}) copy-start(f32[1,4,1,49320]{3,2,1,0:T(1,128)} %own_hbm.1) | copy-start | bytes 2367364
  9.3 16.8 %copy-start.14 = (s32[1,2048]{1,0:T(1,128)S(1)}, s32[1,2048]{1,0:T(1,128)}, u32[]{:S(2)}) copy-start(s32[1,2048]{1,0:T(1,128)} %param.12) | copy-start | bytes 24580
  9.3 67.4 %all-to-all-start.2 = ((f32[32,144,128]{2,1,0:T(8,128)}), f32[32,144,128]{2,1,0:T(8,128)S(1)}, u32[]{:S(2)}, u32[]{:S(2)}) async-start(f32[32,144,128]{2,1,0:T(8,128)} %bitcast.49), calls=%async_computation.2 | async-start | bytes 4718592 | tf_op jit(solution)/shard_map/all_to_all | solution.py:39
  22.3 17.1 %collective-permute-start = (f32[1,4,1,49320]{3,2,1,0:T(1,128)S(1)}, f32[1,4,1,49320]{3,2,1,0:T(1,128)}, u32[]{:S(2)}, u32[]{:S(2)}) collective-permute-start(f32[1,4,1,49320]{3,2,1,0:T(1,128)S(1)} %copy-done.12), channel_id=1, source_target_pairs={{32,0},{64,32},{96,64},{128,96},{160,128},{192,160},{224,192},{256... | collective-permute-start | bytes 2367368 | tf_op jit(solution)/shard_map/ppermute | solution.py:482
  81.0 1.1 copy-start
  83.0 8.6 %collective-permute-start.1 = (f32[18,32,384]{2,1,0:T(8,128)}, f32[18,32,384]{2,1,0:T(8,128)}, u32[]{:S(2)}, u32[]{:S(2)}) collective-permute-start(f32[18,32,384]{2,1,0:T(8,128)} %get-tuple-element.53), channel_id=1, source_target_pairs={{0,32},{32,64},{64,96},{96,128},{128,160},{160,192},{192,224},{224... | collective-permute-start | bytes 2654216 | tf_op jit(solution)/shard_map/ppermute | solution.py:482
  84.3 29.4 %all-to-all-start.3 = ((f32[32,56,128]{2,1,0:T(8,128)}), f32[32,56,128]{2,1,0:T(8,128)S(1)}, u32[]{:S(2)}, u32[]{:S(2)}) async-start(f32[32,56,128]{2,1,0:T(8,128)} %bitcast.50), calls=%async_computation.3 | async-start | bytes 1835008 | tf_op jit(solution)/shard_map/all_to_all | solution.py:39
  91.5 1.2 copy-start.4
  92.7 16.3 %copy-start.1 = (f32[5,5,32,384]{3,2,1,0:T(8,128)S(1)}, f32[5,5,32,384]{3,2,1,0:T(8,128)}, u32[]{:S(2)}) copy-start(f32[5,5,32,384]{3,2,1,0:T(8,128)} %copy-done) | copy-start | bytes 3686404
  94.6 14.4 %collective-permute-start.2 = (f32[18,32,384]{2,1,0:T(8,128)S(1)}, f32[18,32,384]{2,1,0:T(8,128)S(1)}, u32[]{:S(2)}, u32[]{:S(2)}) collective-permute-start(f32[18,32,384]{2,1,0:T(8,128)S(1)} %shard_map.83.weighted_ref), channel_id=1, source_target_pairs={{32,0},{64,32},{96,64},{128,96},{160,128},{192,160},{224,192},{256... | collective-permute-start | bytes 2654216 | tf_op jit(solution)/shard_map/ppermute | solution.py:482
  111.6 0.9 copy-start.6
  113.6 1.3 copy-start.2
  114.9 1.2 copy-start.5
  116.1 1.2 copy-start.7
  122.9 0.9 copy-start.11
  123.8 26.6 %all-to-all-start.4 = ((f32[32,56,128]{2,1,0:T(8,128)}), f32[32,56,128]{2,1,0:T(8,128)S(1)}, u32[]{:S(2)}, u32[]{:S(2)}) async-start(f32[32,56,128]{2,1,0:T(8,128)} %bitcast.47), calls=%async_computation.4 | async-start | bytes 1835008 | tf_op jit(solution)/shard_map/all_to_all | solution.py:39
  131.6 7.6 %collective-permute-start.3 = (f32[18,32,384]{2,1,0:T(8,128)}, f32[18,32,384]{2,1,0:T(8,128)S(1)}, u32[]{:S(2)}, u32[]{:S(2)}) collective-permute-start(f32[18,32,384]{2,1,0:T(8,128)} %copy-done.11), channel_id=1, source_target_pairs={{0,32},{32,64},{64,96},{96,128},{128,160},{160,192},{192,224},{224... | collective-permute-start | bytes 2654216 | tf_op jit(solution)/shard_map/ppermute | solution.py:482
  139.3 1.2 copy-start.10
  150.4 34.5 %collective-permute-start.8 = (f32[1792,128]{1,0:T(8,128)S(1)}, f32[1792,128]{1,0:T(8,128)}, u32[]{:S(2)}, u32[]{:S(2)}) collective-permute-start(f32[1792,128]{1,0:T(8,128)S(1)} %bitcast.44), channel_id=1, source_target_pairs={{32,0},{64,32},{96,64},{128,96},{160,128},{192,160},{224,192},{256... | collective-permute-start | bytes 2752520 | tf_op jit(solution)/shard_map/ppermute | solution.py:482
  161.1 5.9 %collective-permute-start.4 = (f32[8,128]{1,0:T(8,128)S(1)}, f32[8,128]{1,0:T(8,128)S(1)}, u32[]{:S(2)}, u32[]{:S(2)}) collective-permute-start(f32[8,128]{1,0:T(8,128)S(1)} %shard_map.86), channel_id=1, source_target_pairs={{0,32},{32,0},{64,96},{96,64},{128,160},{160,128},{192,224},{224,1... | collective-permute-start | bytes 12296 | tf_op jit(solution)/shard_map/ppermute | solution.py:488
  167.1 4.3 %collective-permute-start.5 = (f32[8,128]{1,0:T(8,128)S(1)}, f32[8,128]{1,0:T(8,128)S(1)}, u32[]{:S(2)}, u32[]{:S(2)}) collective-permute-start(f32[8,128]{1,0:T(8,128)S(1)} %add.234), channel_id=1, source_target_pairs={{0,64},{32,96},{64,0},{96,32},{128,192},{160,224},{192,128},{224,1... | collective-permute-start | bytes 12296 | tf_op jit(solution)/shard_map/ppermute | solution.py:488
  171.4 5.2 %collective-permute-start.6 = (f32[8,128]{1,0:T(8,128)S(1)}, f32[8,128]{1,0:T(8,128)S(1)}, u32[]{:S(2)}, u32[]{:S(2)}) collective-permute-start(f32[8,128]{1,0:T(8,128)S(1)} %add.235), channel_id=1, source_target_pairs={{0,128},{32,160},{64,192},{96,224},{128,0},{160,32},{192,64},{224,... | collective-permute-start | bytes 12296 | tf_op jit(solution)/shard_map/ppermute | solution.py:488
  176.6 8.2 %collective-permute-start.7 = (f32[8,128]{1,0:T(8,128)S(1)}, f32[8,128]{1,0:T(8,128)S(1)}, u32[]{:S(2)}, u32[]{:S(2)}) collective-permute-start(f32[8,128]{1,0:T(8,128)S(1)} %add.236), channel_id=1, source_target_pairs={{0,256},{32,288},{64,320},{96,352},{128,384},{160,416},{192,448},{... | collective-permute-start | bytes 12296 | tf_op jit(solution)/shard_map/ppermute | solution.py:488
  186.5 33.5 %copy-start.13 = (f32[1,4,1,49320]{3,2,1,0:T(1,128)S(1)}, f32[1,4,1,49320]{3,2,1,0:T(1,128)}, u32[]{:S(2)}) copy-start(f32[1,4,1,49320]{3,2,1,0:T(1,128)} %get-tuple-element.28.own_ref) | copy-start | bytes 2367364 | tf_op jit(solution)/shard_map/cond
  (3 other events, 2.8 us)

commit v3 on v2

--- a/solution.py
+++ b/solution.py
@@ -31,7 +31,8 @@
 WEIGHT_AT = LAT_AT + CUTS * SPAN
 SEND_ROWS = whole_rows(WEIGHT_AT + CUTS * UNITS)
 BACK_ROWS = whole_rows(CUTS * UNITS)
-PAIR_ROWS = whole_rows(2 * CUTS * UNITS + 4)
+HALF = UNITS // 2
+HALF_ROWS = whole_rows(CUTS * HALF)
 
 
 def exchanged(buffer):
@@ -234,13 +235,18 @@
             out_ref[part] = on_first * first_ref[part] + on_second * second_ref[part]
 
 
-def last_kernel(got_ref, own_ref, image_ref, increment_ref, slid_ref, tall, tall_rest):
-    on_own, on_image = scales_in(got_ref, PAIR_ROWS, 2 * CUTS * UNITS)
+def last_kernel(
+    got_ref, got_moved_ref, own_ref, image_ref, increment_ref, slid_ref, tall, tall_rest
+):
+    rows = BACK_ROWS + 8
+    on_own, on_image = scales_in(got_ref, rows, BACK_ROWS)
 
     def load(parity, row):
-        first = pl.ds(parity * PAIR_ROWS + row, 16, stride=2 * PAIR_ROWS)
-        second = pl.ds(parity * PAIR_ROWS + CUTS * UNITS + row, 16, stride=2 * PAIR_ROWS)
-        return on_own * got_ref[first, :] + on_image * got_ref[second, :]
+        cut, unit = divmod(row, UNITS)
+        at = unit // HALF * CUTS * HALF + cut * HALF + unit % HALF
+        first = pl.ds(parity * BACK_ROWS + at, 16, stride=2 * BACK_ROWS)
+        second = pl.ds(parity * rows + row, 16, stride=2 * rows)
+        return on_own * got_moved_ref[first, :] + on_image * got_ref[second, :]
 
     write_fields(load, slid_ref, tall, tall_rest)
     combined(increment_ref, on_own, own_ref, on_image, image_ref)
@@ -260,9 +266,9 @@
     return [ref[pl.ds(first + cut * step, 32, stride=rows), :] for cut in range(CUTS)]
 
 
-def put_rows(ref, rows, first, blocks):
+def put_rows(ref, rows, first, blocks, step=UNITS):
     for cut in range(CUTS):
-        ref[pl.ds(first + cut * UNITS, 32, stride=rows), :] = blocks[cut]
+        ref[pl.ds(first + cut * step, 32, stride=rows), :] = blocks[cut]
 
 
 def get(ref, *place):
@@ -374,53 +380,63 @@
         ref[pl.ds(row, 32, stride=rows), :] = jnp.zeros((32, LANES), jnp.float32)
 
 
-def moved_kernel(odd_ref, got_ref, mark_ref, state_ref, moved_ref, back_ref, coef_ref):
+def moved_planes(first, odd_ref, got_ref, coef_ref, state_ref, moved_ref, back_ref):
+    odd = odd_ref[0]
+
+    def one(k, carry):
+        v = wrapped(plane_of(got_ref, SEND_ROWS, first + k))
+        put(state_ref, v, k)
+        v = forward(v, coef_ref, level_of(first + k, odd))
+        put(moved_ref, v, k)
+        put_rows(back_ref, HALF_ROWS, k, v, HALF)
+        return carry
+
+    lax.fori_loop(0, HALF, one, 0, unroll=3)
+    for row in range(CUTS * HALF, HALF_ROWS):
+        back_ref[pl.ds(row, 32, stride=HALF_ROWS), :] = jnp.zeros((32, LANES), jnp.float32)
+
+
+def first_moved_kernel(odd_ref, got_ref, mark_ref, state_ref, moved_ref, back_ref, coef_ref):
     fill_coefficients(got_ref, SEND_ROWS, coef_ref)
+    moved_planes(0, odd_ref, got_ref, coef_ref, state_ref, moved_ref, back_ref)
+
+
+def second_moved_kernel(odd_ref, got_ref, coef_ref, state_ref, moved_ref, back_ref):
+    moved_planes(HALF, odd_ref, got_ref, coef_ref, state_ref, moved_ref, back_ref)
+
+
+def weighted_kernel(first, state_ref, arriving_ref, got_ref, weighted_ref):
+    def one(k, carry):
+        w = wrapped(plane_of(got_ref, SEND_ROWS, WEIGHT_AT + first + k))
+        pairs = zip(w, get(state_ref, k), get(arriving_ref, k))
+        put(weighted_ref, [x * (s - m) for x, s, m in pairs], k)
+        return carry
+
+    lax.fori_loop(0, HALF, one, 0, unroll=3)
+
+
+def adjoint_kernel(first, odd_ref, coef_ref, weighted_ref, later_ref, part_ref):
     odd = odd_ref[0]
 
-    def one(unit, carry):
-        v = wrapped(plane_of(got_ref, SEND_ROWS, unit))
-        put(state_ref, v, unit)
-        v = forward(v, coef_ref, level_of(unit, odd))
-        put(moved_ref, v, unit)
-        put_rows(back_ref, BACK_ROWS, unit, v)
+    def one(k, carry):
+        pulled = backward(get(later_ref, k), coef_ref, level_of(first + k, odd))
+        put(part_ref, [w - p for w, p in zip(get(weighted_ref, k), pulled)], k)
         return carry
 
-    lax.fori_loop(0, UNITS, one, 0, unroll=3)
-    clear_rest(back_ref, BACK_ROWS)
-
-
-def weighted_kernel(state_ref, arriving_ref, got_ref, weighted_ref):
-    def one(unit, carry):
-        w = wrapped(plane_of(got_ref, SEND_ROWS, WEIGHT_AT + unit))
-        pairs = zip(w, get(state_ref, unit), get(arriving_ref, unit))
-        put(weighted_ref, [k * (s - m) for k, s, m in pairs], unit)
-        return carry
-
-    lax.fori_loop(0, UNITS, one, 0, unroll=3)
-
-
-def adjoint_kernel(odd_ref, coef_ref, weighted_ref, later_ref, part_ref):
-    odd = odd_ref[0]
-
-    def one(unit, carry):
-        pulled = backward(get(later_ref, unit), coef_ref, level_of(unit, odd))
-        put(part_ref, [w - p for w, p in zip(get(weighted_ref, unit), pulled)], unit)
-        return carry
-
-    lax.fori_loop(0, UNITS, one, 0, unroll=3)
+    lax.fori_loop(0, HALF, one, 0, unroll=3)
 
 
 def image_kernel(
-    odd_ref, coef_ref, obs_ref, state_ref, part_ref,
+    odd_ref, coef_ref, obs_ref, first_state_ref, first_part_ref, second_state_ref, second_part_ref,
     image_ref, moved_ref, back_ref, moved_back_ref, sums_ref,
 ):
     odd = odd_ref[0]
 
-    def one(unit, carry):
-        state = get(state_ref, unit)
+    def step(first, state_ref, part_ref, k, carry):
+        unit = first + k
+        state = get(state_ref, k)
         obs = plane_of(obs_ref, BACK_ROWS, unit)
-        image = [p + k * s for p, k, s in zip(get(part_ref, unit), obs, state)]
+        image = [p + x * s for p, x, s in zip(get(part_ref, k), obs, state)]
         image = wrapped(image)
         put(image_ref, image, unit)
         put_rows(back_ref, BACK_ROWS, unit, image)
@@ -435,8 +451,13 @@
             seen + row_sum(product(obs, image, image)),
         )
 
-    zero = jnp.zeros((1, LANES), jnp.float32)
-    sums = lax.fori_loop(0, UNITS, one, (zero, zero, zero, zero), unroll=3)
+    sums = (jnp.zeros((1, LANES), jnp.float32),) * 4
+    for first, state_ref, part_ref in (
+        (0, first_state_ref, first_part_ref),
+        (HALF, second_state_ref, second_part_ref),
+    ):
+        one = functools.partial(step, first, state_ref, part_ref)
+        sums = lax.fori_loop(0, HALF, one, sums, unroll=3)
     for row in range(4):
         sums_ref[row : row + 1, :] = sums[row]
     sums_ref[4:8, :] = jnp.zeros((4, LANES), jnp.float32)
@@ -458,22 +479,53 @@
 VMEM = pl.BlockSpec(memory_space=pltpu.VMEM)
 SMEM = pl.BlockSpec(memory_space=pltpu.SMEM)
 PLANES = jax.ShapeDtypeStruct((UNITS, 32, WIDE), jnp.float32)
+HALF_PLANES = jax.ShapeDtypeStruct((HALF, 32, WIDE), jnp.float32)
+HALF_BACK = jax.ShapeDtypeStruct((32 * HALF_ROWS, LANES), jnp.float32)
 BACK = jax.ShapeDtypeStruct((32 * BACK_ROWS, LANES), jnp.float32)
 SUMS = jax.ShapeDtypeStruct((8, LANES), jnp.float32)
 COEF = jax.ShapeDtypeStruct((SPAN, 5, 32, WIDE), jnp.float32)
 
 
-def call(kernel, outs, ins, flops=0, extra=()):
-    moved = sum(4 * math.prod(o.shape) for o in outs)
-    return pl.pallas_call(
-        kernel,
-        out_shape=outs,
-        in_specs=[SMEM if i == "s" else VMEM for i in ins],
-        out_specs=[VMEM] * len(outs),
-        scratch_shapes=list(extra),
-        compiler_params=pltpu.CompilerParams(vmem_limit_bytes=16 * 2**20),
-        cost_estimate=pl.CostEstimate(flops=flops, bytes_accessed=3 * moved, transcendentals=0),
-    )
+def call(kernel, outs, ins, extra=()):
+    fetched = [k for k, i in enumerate(ins) if i == "f"]
+    if not fetched:
+        whole = kernel
+    else:
+
+        def whole(*refs):
+            refs = list(refs)
+            sems = refs.pop()
+            held = refs[-len(fetched) :]
+            copies = [
+                pltpu.make_async_copy(refs[k], dst, sems.at[n])
+                for n, (k, dst) in enumerate(zip(fetched, held))
+            ]
+            for copy in copies:
+                copy.start()
+            for copy in copies:
+                copy.wait()
+            for k, dst in zip(fetched, held):
+                refs[k] = dst
+            kernel(*refs[: -len(fetched)])
+
+    def run(*arrays):
+        scratch = [*extra, *(pltpu.VMEM(arrays[k].shape, jnp.float32) for k in fetched)]
+        if fetched:
+            scratch.append(pltpu.SemaphoreType.DMA((len(fetched),)))
+        spec = {"s": SMEM, "v": VMEM, "f": pl.BlockSpec(memory_space=pl.ANY)}
+        return pl.pallas_call(
+            whole,
+            out_shape=outs,
+            in_specs=[spec[i] for i in ins],
+            out_specs=[VMEM] * len(outs),
+            scratch_shapes=scratch,
+            compiler_params=pltpu.CompilerParams(
+                vmem_limit_bytes=(60 if fetched else 16) * 2**20
+            ),
+            cost_estimate=pl.CostEstimate(flops=0, bytes_accessed=0, transcendentals=0),
+        )(*arrays)
+
+    return run
 
 
 def passed_along(shard, by):
@@ -483,11 +535,9 @@
 
 
 def summed_over_tm(tile):
-    count, stride = lax.axis_size("tm"), 1
-    while stride < count:
-        tile = tile + lax.ppermute(tile, "tm", [(i, i ^ stride) for i in range(count)])
-        stride *= 2
-    return tile
+    count = lax.axis_size("tm")
+    copies = jnp.broadcast_to(tile[None], (count, *tile.shape))
+    return lax.all_to_all(copies, "tm", 0, 0, tiled=True).sum(0)
 
 
 def scales_of(bb, bq, qq, qaq):
@@ -533,46 +583,73 @@
 def body(forcing_rhs, courant_lon, courant_lat, error_weight, obs_cell, obs_weight):
     odd = lax.rem(lax.axis_index("lat"), 2).reshape(1)
     got = exchanged(pack(forcing_rhs, courant_lon, courant_lat, error_weight))
+    next_own = passed_along(forcing_rhs, -1)
+    obs_cell, next_own = lax.optimization_barrier((obs_cell, next_own))
     obs = cells_in_planes(obs_cell[0], obs_weight[0])
-    next_own = passed_along(forcing_rhs, -1)
-    got, mark, next_own = lax.optimization_barrier((got, obs[:8], next_own))
+    got, mark = lax.optimization_barrier((got, obs[:8]))
     got_obs = exchanged(obs)
 
-    state, moved, moved_back, coef = call(
-        moved_kernel, [PLANES, PLANES, BACK, COEF], "svv", 10**8
+    first_state, first_moved, first_back, coef = call(
+        first_moved_kernel, [HALF_PLANES, HALF_PLANES, HALF_BACK, COEF], "svv"
     )(odd, got, mark)
-    arriving = passed_along(moved, 1)
-    (weighted,) = call(weighted_kernel, [PLANES], "vvv")(state, arriving, got)
-    later = passed_along(weighted, -1)
-    (part,) = call(adjoint_kernel, [PLANES], "svvv", 10**8)(odd, coef, weighted, later)
+    first_arriving = passed_along(first_moved, 1)
+    second_state, second_moved, second_back = call(
+        second_moved_kernel, [HALF_PLANES, HALF_PLANES, HALF_BACK], "svv"
+    )(odd, got, coef)
+    second_arriving = passed_along(second_moved, 1)
+
+    def weigh(first, state, arriving):
+        kernel = functools.partial(weighted_kernel, first)
+        return call(kernel, [HALF_PLANES], "vvv")(state, arriving, got)[0]
+
+    def pull(first, weighted, later):
+        kernel = functools.partial(adjoint_kernel, first)
+        return call(kernel, [HALF_PLANES], "svvv")(odd, coef, weighted, later)[0]
+
+    first_weighted = weigh(0, first_state, first_arriving)
+    first_later = passed_along(first_weighted, -1)
+    second_weighted = weigh(HALF, second_state, second_arriving)
+    second_later = passed_along(second_weighted, -1)
+    first_part = pull(0, first_weighted, first_later)
+    second_part = pull(HALF, second_weighted, second_later)
     image, image_moved, image_back, image_moved_back, sums = call(
-        image_kernel, [PLANES, PLANES, BACK, BACK, SUMS], "svvvv", 10**8
-    )(odd, coef, got_obs, state, part)
+        image_kernel, [PLANES, PLANES, BACK, BACK, SUMS], "sffffff"
+    )(odd, coef, got_obs, first_state, first_part, second_state, second_part)
     row_shape = jax.ShapeDtypeStruct(forcing_rhs.shape, jnp.float32)
-    got_image = exchanged(image_back)
+    is_final = lax.axis_index("tm") == lax.axis_size("tm") - 1
+
+    def image_and_moved(back):
+        parts = [
+            blocks_of(back),
+            blocks_of(first_back)[:, : CUTS * HALF],
+            blocks_of(second_back)[:, : CUTS * HALF],
+            jnp.zeros((32, BACK_ROWS - 2 * CUTS * HALF, LANES), jnp.float32),
+        ]
+        both = blocks_of(exchanged(jnp.concatenate(parts, 1).reshape(-1, LANES)))
+        return both[:, :BACK_ROWS].reshape(-1, LANES), both[:, BACK_ROWS:].reshape(-1, LANES)
+
+    def image_alone(back):
+        return exchanged(back), jnp.zeros_like(back)
+
     image_arriving = passed_along(image_moved, 1)
+    got_image, got_moved = lax.cond(is_final, image_and_moved, image_alone, image_back)
     (sums,) = call(norm_kernel, [SUMS], "vvvv")(image, image_arriving, got, sums)
-    got_image, sums = lax.optimization_barrier((got_image, sums))
     next_got_image = passed_along(got_image, -1)
-    (image_own,) = call(unpack_kernel, [row_shape], "v", 10**7, TALL)(got_image)
+    (image_own,) = call(unpack_kernel, [row_shape], "v", TALL)(got_image)
     sums = summed_over_tm(sums)
     sums, image_own, next_got_image = lax.optimization_barrier((sums, image_own, next_got_image))
 
-    is_final = lax.axis_index("tm") == lax.axis_size("tm") - 1
-
     def last(tile):
-        parts = [
-            blocks_of(moved_back)[:, : CUTS * UNITS],
-            blocks_of(image_moved_back)[:, : CUTS * UNITS],
-            jnp.broadcast_to(tile[None, :4], (32, 4, LANES)),
-        ]
+        parts = [blocks_of(image_moved_back), jnp.broadcast_to(tile[None], (32, 8, LANES))]
         back = exchanged(jnp.concatenate(parts, 1).reshape(-1, LANES))
-        return call(last_kernel, [row_shape] * 2, "vvv", 10**7, TALL)(back, forcing_rhs, image_own)
+        return call(last_kernel, [row_shape] * 2, "vvvv", TALL)(
+            back, got_moved, forcing_rhs, image_own
+        )
 
     def other(tile):
         back = exchanged(jnp.broadcast_to(tile[None], (32, 8, LANES)).reshape(-1, LANES))
         scratch = [pltpu.VMEM(forcing_rhs.shape, jnp.float32), *TALL]
-        return call(other_kernel, [row_shape] * 2, "vvvvv", 10**7, scratch)(
+        return call(other_kernel, [row_shape] * 2, "vvvvv", scratch)(
             back, forcing_rhs, image_own, next_own, next_got_image
         )
 

time: 224 us -> 209 us (0.933)
  blocking collectives: 33.5 us -> 67.6 us
  starting transfers between devices: 73.9 us -> 46.6 us
  waiting for transfers between devices: 62.1 us -> 40.6 us
  local copies, waits for them, and re-layouts: 12.4 us -> 5.05 us
  Pallas kernels: 26.1 us -> 31 us
    all_to_all x1 -> x2, blocking collectives: 33.5 us -> 67.6 us  [exchanged(): return lax.all_to_all(chunks, 'lat', 0, 0, tiled=True).reshape(-1, LANES)]
    ppermute x4 -> x0, starting transfers between devices: 16.3 us -> none  [summed_over_tm(): lax.ppermute(tile, 'tm', [(i, i ^ stride) for i in range(count)])]
    all_to_all x3 -> x2, waiting for transfers between devices: 47.9 us -> 36.8 us  [exchanged(): return lax.all_to_all(chunks, 'lat', 0, 0, tiled=True).reshape(-1, LANES)]
    unnamed x28 -> x26, local copies, waits for them, and re-layouts: 11.7 us -> 2.58 us
    all_to_all x3 -> x2, starting transfers between devices: 28.1 us -> 20.3 us  [exchanged(): return lax.all_to_all(chunks, 'lat', 0, 0, tiled=True).reshape(-1, LANES)]
    ppermute x5 -> x7, starting transfers between devices: 29.4 us -> 21.7 us  [passed_along(): return lax.ppermute(shard, 'tm', pairs)]
    ppermute x5 -> x7, waiting for transfers between devices: 8.32 us -> 1.17 us  [passed_along(): return lax.ppermute(shard, 'tm', pairs)]
    ppermute x4 -> x0, waiting for transfers between devices: 5.93 us -> none  [summed_over_tm(): lax.ppermute(tile, 'tm', [(i, i ^ stride) for i in range(count)])]
  transfers between devices with their start and end apart: 12 -> 10, of which waited for: 9 -> 3; matrix products, arithmetic and copies ran while one was open for 6% -> 8% of each run, Pallas kernels for 3% -> 6%
where the time goes in v3:
time: 209 us; the launch traced here: 208 us
  blocking collectives  67.6 us (32%)
  starting transfers between devices  46.6 us (22%)
  waiting for transfers between devices  40.6 us (19%)
  Pallas kernels  31 us (15%)
  other arithmetic  15.7 us (8%)
  local copies, waits for them, and re-layouts  5.05 us (2%)
    all_to_all x2, blocking collectives, exchanged(): return lax.all_to_all(chunks, 'lat', 0, 0, tiled=True).reshape(-1, LANES)  67.6 us
    all_to_all x2, waiting for transfers between devices, exchanged(): return lax.all_to_all(chunks, 'lat', 0, 0, tiled=True).reshape(-1, LANES)  36.8 us
    pallas_call x10, Pallas kernels, run(): pl.pallas_call(whole, out_shape=outs, in_specs=[spec[i] for i in ins], ou...  22.4 us
    ppermute x7, starting transfers between devices, passed_along(): return lax.ppermute(shard, 'tm', pairs)  21.7 us
    all_to_all x2, starting transfers between devices, exchanged(): return lax.all_to_all(chunks, 'lat', 0, 0, tiled=True).reshape(-1, LANES)  20.3 us
    scatter-add x1, other arithmetic, cells_in_planes(): empty.at[row * LANES + lane % LANES].add(weight)  12.4 us
    pallas_call x1, Pallas kernels, pack(): pl.pallas_call(pack_kernel, out_shape=jax.ShapeDtypeStruct((32 * SEND_ROW...  8.61 us
    all_to_all x1, starting transfers between devices, summed_over_tm(): return lax.all_to_all(copies, 'tm', 0, 0, tiled=True).sum(0)  4.6 us
  transfers between devices with their start and end apart: 10, of which 3 were waited for; matrix products, arithmetic and copies ran while one was open for 8% of the time, Pallas kernels for 6%

profile of v3, /device:TPU:57, one launch (start us, length us, event | category | flops | bytes accessed | tf_op | source)
XLA Modules:
  0.0 207.5 jit_solution(97718450346278815)
XLA Ops:
  0.6 8.6 %shard_map.81 = f32[4608,128]{1,0:T(8,128)} custom-call(f32[1,4,1,49320]{3,2,1,0:T(1,128)} %own_hbm.1, f32[1,1,49320]{2,1,0:T(1,128)} %lon_hbm.1, f32[1,1,49320]{2,1,0:T(1,128)} %lat_hbm.1, f32[1,4,1,49320]{3,2,1,0:T(1,128)} %weight_hbm.1), custom_call_target="tpu_custom_call" | custom-call | tf_op jit(solution)/shard_map/pallas_call | solution.py:156
  9.3 13.0 %all-to-all-start.4 = ((f32[32,144,128]{2,1,0:T(8,128)}), f32[32,144,128]{2,1,0:T(8,128)S(1)}, u32[]{:S(2)}, u32[]{:S(2)}) async-start(f32[32,144,128]{2,1,0:T(8,128)} %bitcast.51), calls=%async_computation.4 | async-start | bytes 4718592 | tf_op jit(solution)/shard_map/all_to_all | solution.py:40
  22.3 3.8 %collective-permute-start = (f32[1,4,1,49320]{3,2,1,0:T(1,128)S(1)}, f32[1,4,1,49320]{3,2,1,0:T(1,128)}, u32[]{:S(2)}, u32[]{:S(2)}) collective-permute-start(f32[1,4,1,49320]{3,2,1,0:T(1,128)S(1)} %copy-done.7), channel_id=1, source_target_pairs={{32,0},{64,32},{96,64},{128,96},{160,128},{192,160},{224,192},{256... | collective-permute-start | bytes 2367368 | tf_op jit(solution)/shard_map/ppermute | solution.py:534
  27.6 12.4 %scatter_custom_fusion = f32[229376]{0:T(1024)} fusion(s32[2048]{0:T(1024)S(1)} %bitcast.59, f32[2048]{0:T(1024)} %bitcast.60, f32[]{:T(128)} %constant.107.clone.1), kind=kCustom, calls=%fused_computation.3 | custom fusion | flops 2048 | bytes 918016 | tf_op jit(solution)/shard_map/scatter-add | solution.py:580
  39.9 36.8 %all-to-all-done.4 = f32[32,144,128]{2,1,0:T(8,128)S(1)} async-done(((f32[32,144,128]{2,1,0:T(8,128)}), f32[32,144,128]{2,1,0:T(8,128)S(1)}, u32[]{:S(2)}, u32[]{:S(2)}) %all-to-all-start.4) | async-done | bytes 2359328 | tf_op jit(solution)/shard_map/all_to_all | solution.py:40
  76.7 7.3 %all-to-all-start.5 = ((f32[32,56,128]{2,1,0:T(8,128)}), f32[32,56,128]{2,1,0:T(8,128)S(1)}, u32[]{:S(2)}, u32[]{:S(2)}) async-start(f32[32,56,128]{2,1,0:T(8,128)} %bitcast.19), calls=%async_computation.5 | async-start | bytes 1835008 | tf_op jit(solution)/shard_map/all_to_all | solution.py:40
  84.7 2.8 %shard_map.82 = (f32[9,32,384]{2,1,0:T(8,128)S(1)}, f32[9,32,384]{2,1,0:T(8,128)S(1)}, f32[1024,128]{1,0:T(8,128)}, f32[5,5,32,384]{3,2,1,0:T(8,128)S(1)}) custom-call(s32[1]{0:T(128)} %bitcast.10.odd_ref.refs_0_, f32[4608,128]{1,0:T(8,128)S(1)} %bitcast.44, f32[8,128]{1,0:T(8,128)S(1)} %slice_bitcast_fusion.mark_ref), custom_call_target="tpu_custom_call" | custom-call | tf_op jit(solution)/shard_map/pallas_call | solution.py:516
  88.7 2.6 %shard_map.85 = (f32[9,32,384]{2,1,0:T(8,128)S(1)}, f32[9,32,384]{2,1,0:T(8,128)S(1)}, f32[1024,128]{1,0:T(8,128)}) custom-call(s32[1]{0:T(128)} %bitcast.10.odd_ref.refs_0_, f32[4608,128]{1,0:T(8,128)S(1)} %bitcast.45, f32[5,5,32,384]{3,2,1,0:T(8,128)S(1)} %get-tuple-element.72.coef_ref.refs_1_), custom_call_target="tpu_custom_call" | custom-call | tf_op jit(solution)/shard_map/pallas_call | solution.py:516
  92.9 7.5 %collective-permute-start.2 = (f32[9,32,384]{2,1,0:T(8,128)S(1)}, f32[9,32,384]{2,1,0:T(8,128)S(1)}, u32[]{:S(2)}, u32[]{:S(2)}) collective-permute-start(f32[9,32,384]{2,1,0:T(8,128)S(1)} %shard_map.83.weighted_ref), channel_id=1, source_target_pairs={{32,0},{64,32},{96,64},{128,96},{160,128},{192,160},{224,192},{256... | collective-permute-start | bytes 1327112 | tf_op jit(solution)/shard_map/ppermute | solution.py:534
  100.7 4.4 %collective-permute-start.4 = (f32[9,32,384]{2,1,0:T(8,128)S(1)}, f32[9,32,384]{2,1,0:T(8,128)S(1)}, u32[]{:S(2)}, u32[]{:S(2)}) collective-permute-start(f32[9,32,384]{2,1,0:T(8,128)S(1)} %shard_map.86.weighted_ref), channel_id=1, source_target_pairs={{32,0},{64,32},{96,64},{128,96},{160,128},{192,160},{224,192},{256... | collective-permute-start | bytes 1327112 | tf_op jit(solution)/shard_map/ppermute | solution.py:534
  105.1 1.3 shard_map.84.refs_4_
  107.2 1.3 shard_map.87.refs_6_
  110.3 6.7 %shard_map.88 = (f32[18,32,384]{2,1,0:T(8,128)}, f32[18,32,384]{2,1,0:T(8,128)}, f32[1792,128]{1,0:T(8,128)}, f32[1792,128]{1,0:T(8,128)}, f32[8,128]{1,0:T(8,128)}) custom-call(s32[1]{0:T(128)} %bitcast.10.odd_ref.refs_0_, f32[5,5,32,384]{3,2,1,0:T(8,128)} %copy-done, f32[1792,128]{1,0:T(8,128)} %bitcast.53, f32[9,32,384]{2,1,0:T(8,128)} %copy-done.1, ...), custom_call_target="tpu_custom_call" | custom-call | tf_op jit(solution)/shard_map/pallas_call | solution.py:516
  118.3 48.2 %conditional.2 = (f32[1792,128]{1,0:T(8,128)S(1)}, f32[1792,128]{1,0:T(8,128)}) conditional(s32[]{:T(128)} %convert_element_type.4, f32[1792,128]{1,0:T(8,128)} %get-tuple-element.80, (f32[1792,128]{1,0:T(8,128)}, f32[1024,128]{1,0:T(8,128)}, f32[1024,128]{1,0:T(8,128)}) %tuple.36), branch_computations={%region_2.3_spmd, %region_3.4_spmd} | conditional | flops 1376256 | bytes 10978216 | solution.py:635
  118.4 1.8 maximum_maximum_fusion
  120.2 45.3 %all_to_all.32 = f32[32,112,128]{2,1,0:T(8,128)S(1)} all-to-all(f32[32,112,128]{2,1,0:T(8,128)S(1)} %maximum_maximum_fusion), channel_id=1, replica_groups=mesh['tm'=16,'lat'=32] {'lat'}, dimensions={0} | all-to-all | bytes 3670016 | tf_op jit(solution)/shard_map/cond/branch_1_fun/all_to_all | solution.py:40
  166.5 2.2 %collective-permute-start.6 = (f32[1792,128]{1,0:T(8,128)}, f32[1792,128]{1,0:T(8,128)}, u32[]{:S(2)}, u32[]{:S(2)}) collective-permute-start(f32[1792,128]{1,0:T(8,128)} %get-tuple-element.98.got_ref), channel_id=1, source_target_pairs={{32,0},{64,32},{96,64},{128,96},{160,128},{192,160},{224,192},{256... | collective-permute-start | bytes 2752520 | tf_op jit(solution)/shard_map/ppermute | solution.py:534
  168.8 1.6 shard_map.89
  171.1 4.6 %all-to-all-start.6 = ((f32[16,8,128]{2,1,0:T(8,128)}), f32[16,8,128]{2,1,0:T(8,128)S(1)}, u32[]{:S(2)}, u32[]{:S(2)}) async-start(f32[16,8,128]{2,1,0:T(8,128)} %broadcast_in_dim.32), calls=%async_computation.6 | async-start | bytes 131072 | tf_op jit(solution)/shard_map/all_to_all | solution.py:540
  175.7 2.6 %shard_map.90 = f32[1,4,1,49320]{3,2,1,0:T(1,128)S(1)} custom-call(f32[1792,128]{1,0:T(8,128)} %get-tuple-element.98.got_ref), custom_call_target="tpu_custom_call" | custom-call | tf_op jit(solution)/shard_map/pallas_call | solution.py:516
  178.3 2.7 %all-to-all-done.6 = f32[16,8,128]{2,1,0:T(8,128)S(1)} async-done(((f32[16,8,128]{2,1,0:T(8,128)}), f32[16,8,128]{2,1,0:T(8,128)S(1)}, u32[]{:S(2)}, u32[]{:S(2)}) %all-to-all-start.6) | async-done | bytes 65568 | tf_op jit(solution)/shard_map/all_to_all | solution.py:540
  181.0 26.5 %conditional.3 = ((f32[1,4,1,49320]{3,2,1,0:T(1,128)}, f32[1,4,1,49320]{3,2,1,0:T(1,128)})) conditional(s32[]{:T(128)} %convert_element_type.4, (f32[8,128]{1,0:T(8,128)S(1)}, f32[1,4,1,49320]{3,2,1,0:T(1,128)S(1)}, f32[1,4,1,49320]{3,2,1,0:T(1,128)S(1)}, f32[1,4,1,49320]{3,2,1,0:T(1,128)}, f32[1792,128]{1,0:T(8,128)}) %tuple.56, ...), branch_computations={%region_4.5_spmd, %region_5.6_spmd} | conditional | flops 262144 | bytes 4329480 | solution.py:656
  182.3 22.3 %all_to_all.34 = f32[32,64,128]{2,1,0:T(8,128)S(1)} all-to-all(f32[32,64,128]{2,1,0:T(8,128)S(1)} %pad_maximum_fusion), channel_id=1, replica_groups=mesh['tm'=16,'lat'=32] {'lat'}, dimensions={0} | all-to-all | bytes 2097152 | tf_op jit(solution)/shard_map/cond/branch_1_fun/all_to_all | solution.py:40
  204.7 2.9 %branch_1_fun.1 = (f32[1,4,1,49320]{3,2,1,0:T(1,128)}, f32[1,4,1,49320]{3,2,1,0:T(1,128)}) custom-call(f32[2048,128]{1,0:T(8,128)S(1)} %bitcast.49, f32[1792,128]{1,0:T(8,128)S(1)} %get-tuple-element.43.got_moved_ref, f32[1,4,1,49320]{3,2,1,0:T(1,128)S(1)} %get-tuple-element.44.own_ref, f32[1,4,1,49320]{3,2,1,0:T(1,128)S(1)} %get-tuple-element.45.image_ref), custom_call_target="tpu_custom_call" | custom-call | tf_op jit(solution)/shard_map/cond/branch_1_fun/pallas_call | solution.py:516
  (48 shorter events, 12.3 us)
Async XLA Ops:
  9.2 13.1 %copy-start.7 = (f32[1,4,1,49320]{3,2,1,0:T(1,128)S(1)}, f32[1,4,1,49320]{3,2,1,0:T(1,128)}, u32[]{:S(2)}) copy-start(f32[1,4,1,49320]{3,2,1,0:T(1,128)} %own_hbm.1) | copy-start | bytes 2367364
  9.3 18.0 %copy-start.12 = (s32[1,2048]{1,0:T(1,128)S(1)}, s32[1,2048]{1,0:T(1,128)}, u32[]{:S(2)}) copy-start(s32[1,2048]{1,0:T(1,128)} %param.14) | copy-start | bytes 24580
  9.3 67.4 %all-to-all-start.4 = ((f32[32,144,128]{2,1,0:T(8,128)}), f32[32,144,128]{2,1,0:T(8,128)S(1)}, u32[]{:S(2)}, u32[]{:S(2)}) async-start(f32[32,144,128]{2,1,0:T(8,128)} %bitcast.51), calls=%async_computation.4 | async-start | bytes 4718592 | tf_op jit(solution)/shard_map/all_to_all | solution.py:40
  22.3 4.9 %collective-permute-start = (f32[1,4,1,49320]{3,2,1,0:T(1,128)S(1)}, f32[1,4,1,49320]{3,2,1,0:T(1,128)}, u32[]{:S(2)}, u32[]{:S(2)}) collective-permute-start(f32[1,4,1,49320]{3,2,1,0:T(1,128)S(1)} %copy-done.7), channel_id=1, source_target_pairs={{32,0},{64,32},{96,64},{128,96},{160,128},{192,160},{224,192},{256... | collective-permute-start | bytes 2367368 | tf_op jit(solution)/shard_map/ppermute | solution.py:534
  76.7 32.7 %all-to-all-start.5 = ((f32[32,56,128]{2,1,0:T(8,128)}), f32[32,56,128]{2,1,0:T(8,128)S(1)}, u32[]{:S(2)}, u32[]{:S(2)}) async-start(f32[32,56,128]{2,1,0:T(8,128)} %bitcast.19), calls=%async_computation.5 | async-start | bytes 1835008 | tf_op jit(solution)/shard_map/all_to_all | solution.py:40
  87.5 5.5 %copy-start.1 = (f32[9,32,384]{2,1,0:T(8,128)}, f32[9,32,384]{2,1,0:T(8,128)S(1)}, u32[]{:S(2)}) copy-start(f32[9,32,384]{2,1,0:T(8,128)S(1)} %get-tuple-element.73.state_ref.refs_3_) | copy-start | bytes 1327108
  87.5 19.8 %copy-start = (f32[5,5,32,384]{3,2,1,0:T(8,128)}, f32[5,5,32,384]{3,2,1,0:T(8,128)S(1)}, u32[]{:S(2)}) copy-start(f32[5,5,32,384]{3,2,1,0:T(8,128)S(1)} %get-tuple-element.72.coef_ref.refs_1_) | copy-start | bytes 3686404
  87.5 5.1 %collective-permute-start.1 = (f32[9,32,384]{2,1,0:T(8,128)S(1)}, f32[9,32,384]{2,1,0:T(8,128)S(1)}, u32[]{:S(2)}, u32[]{:S(2)}) collective-permute-start(f32[9,32,384]{2,1,0:T(8,128)S(1)} %get-tuple-element.74), channel_id=1, source_target_pairs={{0,32},{32,64},{64,96},{96,128},{128,160},{160,192},{192,224},{224... | collective-permute-start | bytes 1327112 | tf_op jit(solution)/shard_map/ppermute | solution.py:534
  91.3 9.1 %copy-start.2 = (f32[9,32,384]{2,1,0:T(8,128)}, f32[9,32,384]{2,1,0:T(8,128)S(1)}, u32[]{:S(2)}) copy-start(f32[9,32,384]{2,1,0:T(8,128)S(1)} %get-tuple-element.75.state_ref.refs_5_) | copy-start | bytes 1327108
  91.3 9.1 %collective-permute-start.3 = (f32[9,32,384]{2,1,0:T(8,128)S(1)}, f32[9,32,384]{2,1,0:T(8,128)S(1)}, u32[]{:S(2)}, u32[]{:S(2)}) collective-permute-start(f32[9,32,384]{2,1,0:T(8,128)S(1)} %get-tuple-element.76), channel_id=1, source_target_pairs={{0,32},{32,64},{64,96},{96,128},{128,160},{160,192},{192,224},{224... | collective-permute-start | bytes 1327112 | tf_op jit(solution)/shard_map/ppermute | solution.py:534
  92.9 12.2 %collective-permute-start.2 = (f32[9,32,384]{2,1,0:T(8,128)S(1)}, f32[9,32,384]{2,1,0:T(8,128)S(1)}, u32[]{:S(2)}, u32[]{:S(2)}) collective-permute-start(f32[9,32,384]{2,1,0:T(8,128)S(1)} %shard_map.83.weighted_ref), channel_id=1, source_target_pairs={{32,0},{64,32},{96,64},{128,96},{160,128},{192,160},{224,192},{256... | collective-permute-start | bytes 1327112 | tf_op jit(solution)/shard_map/ppermute | solution.py:534
  100.7 6.5 %collective-permute-start.4 = (f32[9,32,384]{2,1,0:T(8,128)S(1)}, f32[9,32,384]{2,1,0:T(8,128)S(1)}, u32[]{:S(2)}, u32[]{:S(2)}) collective-permute-start(f32[9,32,384]{2,1,0:T(8,128)S(1)} %shard_map.86.weighted_ref), channel_id=1, source_target_pairs={{32,0},{64,32},{96,64},{128,96},{160,128},{192,160},{224,192},{256... | collective-permute-start | bytes 1327112 | tf_op jit(solution)/shard_map/ppermute | solution.py:534
  106.5 0.8 copy-start.3
  108.6 0.8 copy-start.4
  109.4 1.0 copy-start.11
  117.0 51.8 %collective-permute-start.5 = (f32[18,32,384]{2,1,0:T(8,128)}, f32[18,32,384]{2,1,0:T(8,128)}, u32[]{:S(2)}, u32[]{:S(2)}) collective-permute-start(f32[18,32,384]{2,1,0:T(8,128)} %get-tuple-element.78), channel_id=1, source_target_pairs={{0,32},{32,64},{64,96},{96,128},{128,160},{160,192},{192,224},{224... | collective-permute-start | bytes 2654216 | tf_op jit(solution)/shard_map/ppermute | solution.py:534
  118.3 50.5 %copy-start.5 = (f32[18,32,384]{2,1,0:T(8,128)S(1)}, f32[18,32,384]{2,1,0:T(8,128)}, u32[]{:S(2)}) copy-start(f32[18,32,384]{2,1,0:T(8,128)} %get-tuple-element.77.image_ref) | copy-start | bytes 2654212
  118.3 50.5 %copy-start.6 = (f32[8,128]{1,0:T(8,128)S(1)}, f32[8,128]{1,0:T(8,128)}, u32[]{:S(2)}) copy-start(f32[8,128]{1,0:T(8,128)} %get-tuple-element.79.sums_ref) | copy-start | bytes 12292
  166.5 3.9 %copy-start.9 = (f32[1792,128]{1,0:T(8,128)}, f32[1792,128]{1,0:T(8,128)S(1)}, u32[]{:S(2)}) copy-start(f32[1792,128]{1,0:T(8,128)S(1)} %get-tuple-element.90) | copy-start | bytes 2752516
  166.5 14.4 %collective-permute-start.6 = (f32[1792,128]{1,0:T(8,128)}, f32[1792,128]{1,0:T(8,128)}, u32[]{:S(2)}, u32[]{:S(2)}) collective-permute-start(f32[1792,128]{1,0:T(8,128)} %get-tuple-element.98.got_ref), channel_id=1, source_target_pairs={{32,0},{64,32},{96,64},{128,96},{160,128},{192,160},{224,192},{256... | collective-permute-start | bytes 2752520 | tf_op jit(solution)/shard_map/ppermute | solution.py:534
  170.4 10.6 %copy-start.8 = (f32[1,4,1,49320]{3,2,1,0:T(1,128)S(1)}, f32[1,4,1,49320]{3,2,1,0:T(1,128)}, u32[]{:S(2)}) copy-start(f32[1,4,1,49320]{3,2,1,0:T(1,128)} %own_hbm.1) | copy-start | bytes 2367364
  171.1 9.9 %copy-start.10 = (f32[1792,128]{1,0:T(8,128)S(1)}, f32[1792,128]{1,0:T(8,128)}, u32[]{:S(2)}) copy-start(f32[1792,128]{1,0:T(8,128)} %copy-done.9) | copy-start | bytes 2752516
  171.1 9.9 %all-to-all-start.6 = ((f32[16,8,128]{2,1,0:T(8,128)}), f32[16,8,128]{2,1,0:T(8,128)S(1)}, u32[]{:S(2)}, u32[]{:S(2)}) async-start(f32[16,8,128]{2,1,0:T(8,128)} %broadcast_in_dim.32), calls=%async_computation.6 | async-start | bytes 131072 | tf_op jit(solution)/shard_map/all_to_all | solution.py:540

commit v4 on v3

--- a/solution.py
+++ b/solution.py
@@ -29,7 +29,10 @@
 LON_AT = CUTS * UNITS
 LAT_AT = LON_AT + CUTS * SPAN
 WEIGHT_AT = LAT_AT + CUTS * SPAN
-SEND_ROWS = whole_rows(WEIGHT_AT + CUTS * UNITS)
+WHOLE = UNITS - 1
+SEND_ROWS = whole_rows(WEIGHT_AT + CUTS * WHOLE)
+PIECES = LANES // RIGHT
+FREE = [2 * UNITS + u for u in range(UNITS)] + [LON_AT + 2 * SPAN + i for i in range(SPAN)]
 BACK_ROWS = whole_rows(CUTS * UNITS)
 HALF = UNITS // 2
 HALF_ROWS = whole_rows(CUTS * HALF)
@@ -86,20 +89,27 @@
 
 
 def deal(tall, tall_rest, out_ref, slots):
+    lane = lax.broadcasted_iota(jnp.int32, (16, LANES), 1)
     for cut in range(CUTS):
         main = tall[pl.ds(cut * LANES, LANES), :].T
         rest = tall_rest[pl.ds(cut * LANES, LANES), :].T
         for i in range(9):
             value = main[16 * i : 16 * i + 16] if i < 8 else rest[:16]
             for parity, row in slots[i](cut):
-                out_ref[pl.ds(parity * SEND_ROWS + row, 16, stride=2 * SEND_ROWS), :] = value
-
-
-def slots_of_field(f, base):
+                if row is not None:
+                    out_ref[pl.ds(parity * SEND_ROWS + row, 16, stride=2 * SEND_ROWS), :] = value
+                    continue
+                for piece, at in enumerate(FREE[cut * PIECES : (cut + 1) * PIECES]):
+                    place = pl.ds(parity * SEND_ROWS + at, 16, stride=2 * SEND_ROWS)
+                    moved = pltpu.roll(value, LANES - (piece + 1) * RIGHT, 1) if piece < PIECES - 1 else value
+                    out_ref[place, :] = jnp.where(lane >= LANES - RIGHT, moved, out_ref[place, :])
+
+
+def slots_of_field(f, base, count=UNITS):
     def slot(i):
         even = i < EVEN_N[f]
         unit = EVEN_AT[f] + i if even else ODD_AT[f] + i - EVEN_N[f]
-        return lambda cut: [(0 if even else 1, base + cut * UNITS + unit)]
+        return lambda cut: [(0 if even else 1, base + cut * count + unit if unit < count else None)]
 
     return [slot(i) for i in range(9)]
 
@@ -124,12 +134,12 @@
             ((own_hbm, own), (lon_hbm, lon), (lat_hbm, lat), (weight_hbm, weight))
         )
     ]
-    for copy in copies:
-        copy.start()
+    for k in (1, 2, 0, 3):
+        copies[k].start()
     line[...] = jnp.zeros_like(line)
     tall[...] = jnp.zeros_like(tall)
     tall_rest[...] = jnp.zeros_like(tall_rest)
-    for row in range(WEIGHT_AT + CUTS * UNITS, SEND_ROWS):
+    for row in range(WEIGHT_AT + CUTS * WHOLE, SEND_ROWS):
         out_ref[pl.ds(row, 32, stride=SEND_ROWS), :] = jnp.zeros((32, LANES), jnp.float32)
 
     def one(piece, slots):
@@ -137,16 +147,16 @@
         split_longitudes(line, tall, tall_rest)
         deal(tall, tall_rest, out_ref, slots)
 
-    copies[0].wait()
-    for f in range(4):
-        one(lambda at, n: own[0, f, :, pl.ds(at, n)], slots_of_field(f, 0))
     copies[1].wait()
     one(lambda at, n: lon[0, :, pl.ds(at, n)], slots_of_level(LON_AT))
     copies[2].wait()
     one(lambda at, n: lat[0, :, pl.ds(at, n)], slots_of_level(LAT_AT))
+    copies[0].wait()
+    for f in range(4):
+        one(lambda at, n: own[0, f, :, pl.ds(at, n)], slots_of_field(f, 0))
     copies[3].wait()
     for f in range(4):
-        one(lambda at, n: weight[0, f, :, pl.ds(at, n)], slots_of_field(f, WEIGHT_AT))
+        one(lambda at, n: weight[0, f, :, pl.ds(at, n)], slots_of_field(f, WEIGHT_AT, WHOLE))
 
 
 def pack(*arrays):
@@ -405,14 +415,37 @@
     moved_planes(HALF, odd_ref, got_ref, coef_ref, state_ref, moved_ref, back_ref)
 
 
+def weight_plane(got_ref, unit):
+    return plane_of(got_ref, SEND_ROWS, WEIGHT_AT + unit, WHOLE)
+
+
+def last_weight_plane(got_ref):
+    lane = index_of(1)
+    blocks = []
+    for cut in range(CUTS):
+        block = None
+        for piece, at in enumerate(FREE[cut * PIECES : (cut + 1) * PIECES]):
+            x = got_ref[pl.ds(at, 32, stride=SEND_ROWS), :]
+            x = pltpu.roll(x, (piece + 1) * RIGHT, 1) if piece < PIECES - 1 else x
+            block = x if block is None else jnp.where(lane >= piece * RIGHT, x, block)
+        blocks.append(block)
+    return blocks
+
+
 def weighted_kernel(first, state_ref, arriving_ref, got_ref, weighted_ref):
+    def step(w, k):
+        pairs = zip(wrapped(w), get(state_ref, k), get(arriving_ref, k))
+        put(weighted_ref, [x * (s - m) for x, s, m in pairs], k)
+
     def one(k, carry):
-        w = wrapped(plane_of(got_ref, SEND_ROWS, WEIGHT_AT + first + k))
-        pairs = zip(w, get(state_ref, k), get(arriving_ref, k))
-        put(weighted_ref, [x * (s - m) for x, s, m in pairs], k)
+        step(weight_plane(got_ref, first + k), k)
         return carry
 
-    lax.fori_loop(0, HALF, one, 0, unroll=3)
+    if first + HALF < UNITS:
+        lax.fori_loop(0, HALF, one, 0, unroll=3)
+    else:
+        step(last_weight_plane(got_ref), HALF - 1)
+        lax.fori_loop(0, HALF - 1, one, 0, unroll=4)
 
 
 def adjoint_kernel(first, odd_ref, coef_ref, weighted_ref, later_ref, part_ref):
@@ -466,12 +499,15 @@
 
 
 def norm_kernel(image_ref, arriving_ref, got_ref, sums_ref, out_ref):
+    def term(w, unit):
+        change = [q - m for q, m in zip(get(image_ref, unit), get(arriving_ref, unit))]
+        return row_sum(product(w, change, change))
+
     def one(unit, carry):
-        w = plane_of(got_ref, SEND_ROWS, WEIGHT_AT + unit)
-        change = [q - m for q, m in zip(get(image_ref, unit), get(arriving_ref, unit))]
-        return carry + row_sum(product(w, change, change))
-
-    total = lax.fori_loop(0, UNITS, one, jnp.zeros((1, LANES), jnp.float32), unroll=3)
+        return carry + term(weight_plane(got_ref, unit), unit)
+
+    total = term(last_weight_plane(got_ref), WHOLE) + term(weight_plane(got_ref, WHOLE - 1), WHOLE - 1)
+    total = lax.fori_loop(0, WHOLE - 1, one, total, unroll=4)
     out_ref[...] = sums_ref[...]
     out_ref[3:4, :] += total
 

time: 209 us -> 205 us (0.981)
  waiting for transfers between devices: 40.6 us -> 37.8 us
    all_to_all x2, waiting for transfers between devices: 36.8 us -> 34 us  [exchanged(): return lax.all_to_all(chunks, 'lat', 0, 0, tiled=True).reshape(-1, LANES)]
where the time goes in v4:
time: 205 us; the launch traced here: 204 us
  blocking collectives  67.6 us (33%)
  starting transfers between devices  46.5 us (23%)
  waiting for transfers between devices  37.8 us (18%)
  Pallas kernels  30.2 us (15%)
  other arithmetic  15.8 us (8%)
  local copies, waits for them, and re-layouts  5.06 us (2%)
    all_to_all x2, blocking collectives, exchanged(): return lax.all_to_all(chunks, 'lat', 0, 0, tiled=True).reshape(-1, LANES)  67.6 us
    all_to_all x2, waiting for transfers between devices, exchanged(): return lax.all_to_all(chunks, 'lat', 0, 0, tiled=True).reshape(-1, LANES)  34 us
    pallas_call x10, Pallas kernels, run(): pl.pallas_call(whole, out_shape=outs, in_specs=[spec[i] for i in ins], ou...  22.4 us
    ppermute x7, starting transfers between devices, passed_along(): return lax.ppermute(shard, 'tm', pairs)  21.9 us
    all_to_all x2, starting transfers between devices, exchanged(): return lax.all_to_all(chunks, 'lat', 0, 0, tiled=True).reshape(-1, LANES)  20.2 us
    scatter-add x1, other arithmetic, cells_in_planes(): empty.at[row * LANES + lane % LANES].add(weight)  12.4 us
    pallas_call x1, Pallas kernels, pack(): pl.pallas_call(pack_kernel, out_shape=jax.ShapeDtypeStruct((32 * SEND_ROW...  7.85 us
    all_to_all x1, starting transfers between devices, summed_over_tm(): return lax.all_to_all(copies, 'tm', 0, 0, tiled=True).sum(0)  4.42 us
  transfers between devices with their start and end apart: 10, of which 3 were waited for; matrix products, arithmetic and copies ran while one was open for 8% of the time, Pallas kernels for 6%

profile of v4, /device:TPU:57, one launch (start us, length us, event | category | flops | bytes accessed | tf_op | source)
XLA Modules:
  0.0 203.9 jit_solution(12325675373903084803)
XLA Ops:
  0.6 7.8 %shard_map.81 = f32[4352,128]{1,0:T(8,128)} custom-call(f32[1,4,1,49320]{3,2,1,0:T(1,128)} %own_hbm.1, f32[1,1,49320]{2,1,0:T(1,128)} %lon_hbm.1, f32[1,1,49320]{2,1,0:T(1,128)} %lat_hbm.1, f32[1,4,1,49320]{3,2,1,0:T(1,128)} %weight_hbm.1), custom_call_target="tpu_custom_call" | custom-call | tf_op jit(solution)/shard_map/pallas_call | solution.py:166
  8.5 13.0 %all-to-all-start.4 = ((f32[32,136,128]{2,1,0:T(8,128)}), f32[32,136,128]{2,1,0:T(8,128)S(1)}, u32[]{:S(2)}, u32[]{:S(2)}) async-start(f32[32,136,128]{2,1,0:T(8,128)} %bitcast.51), calls=%async_computation.4 | async-start | bytes 4456448 | tf_op jit(solution)/shard_map/all_to_all | solution.py:43
  21.6 3.8 %collective-permute-start = (f32[1,4,1,49320]{3,2,1,0:T(1,128)S(1)}, f32[1,4,1,49320]{3,2,1,0:T(1,128)}, u32[]{:S(2)}, u32[]{:S(2)}) collective-permute-start(f32[1,4,1,49320]{3,2,1,0:T(1,128)S(1)} %copy-done.7), channel_id=1, source_target_pairs={{32,0},{64,32},{96,64},{128,96},{160,128},{192,160},{224,192},{256... | collective-permute-start | bytes 2367368 | tf_op jit(solution)/shard_map/ppermute | solution.py:570
  26.8 12.4 %scatter_custom_fusion = f32[229376]{0:T(1024)} fusion(s32[2048]{0:T(1024)S(1)} %bitcast.59, f32[2048]{0:T(1024)} %bitcast.60, f32[]{:T(128)} %constant.107.clone.1), kind=kCustom, calls=%fused_computation.3 | custom fusion | flops 2048 | bytes 918016 | tf_op jit(solution)/shard_map/scatter-add | solution.py:616
  39.2 34.0 %all-to-all-done.4 = f32[32,136,128]{2,1,0:T(8,128)S(1)} async-done(((f32[32,136,128]{2,1,0:T(8,128)}), f32[32,136,128]{2,1,0:T(8,128)S(1)}, u32[]{:S(2)}, u32[]{:S(2)}) %all-to-all-start.4) | async-done | bytes 2228256 | tf_op jit(solution)/shard_map/all_to_all | solution.py:43
  73.1 7.1 %all-to-all-start.5 = ((f32[32,56,128]{2,1,0:T(8,128)}), f32[32,56,128]{2,1,0:T(8,128)S(1)}, u32[]{:S(2)}, u32[]{:S(2)}) async-start(f32[32,56,128]{2,1,0:T(8,128)} %bitcast.19), calls=%async_computation.5 | async-start | bytes 1835008 | tf_op jit(solution)/shard_map/all_to_all | solution.py:43
  81.0 2.7 %shard_map.82 = (f32[9,32,384]{2,1,0:T(8,128)S(1)}, f32[9,32,384]{2,1,0:T(8,128)S(1)}, f32[1024,128]{1,0:T(8,128)}, f32[5,5,32,384]{3,2,1,0:T(8,128)S(1)}) custom-call(s32[1]{0:T(128)} %bitcast.10.odd_ref.refs_0_, f32[4352,128]{1,0:T(8,128)S(1)} %bitcast.44, f32[8,128]{1,0:T(8,128)S(1)} %slice_bitcast_fusion.mark_ref), custom_call_target="tpu_custom_call" | custom-call | tf_op jit(solution)/shard_map/pallas_call | solution.py:552
  85.0 2.5 %shard_map.85 = (f32[9,32,384]{2,1,0:T(8,128)S(1)}, f32[9,32,384]{2,1,0:T(8,128)S(1)}, f32[1024,128]{1,0:T(8,128)}) custom-call(s32[1]{0:T(128)} %bitcast.10.odd_ref.refs_0_, f32[4352,128]{1,0:T(8,128)S(1)} %bitcast.45, f32[5,5,32,384]{3,2,1,0:T(8,128)S(1)} %get-tuple-element.72.coef_ref.refs_1_), custom_call_target="tpu_custom_call" | custom-call | tf_op jit(solution)/shard_map/pallas_call | solution.py:552
  89.1 7.6 %collective-permute-start.2 = (f32[9,32,384]{2,1,0:T(8,128)S(1)}, f32[9,32,384]{2,1,0:T(8,128)S(1)}, u32[]{:S(2)}, u32[]{:S(2)}) collective-permute-start(f32[9,32,384]{2,1,0:T(8,128)S(1)} %shard_map.83.weighted_ref), channel_id=1, source_target_pairs={{32,0},{64,32},{96,64},{128,96},{160,128},{192,160},{224,192},{256... | collective-permute-start | bytes 1327112 | tf_op jit(solution)/shard_map/ppermute | solution.py:570
  97.2 4.4 %collective-permute-start.4 = (f32[9,32,384]{2,1,0:T(8,128)S(1)}, f32[9,32,384]{2,1,0:T(8,128)S(1)}, u32[]{:S(2)}, u32[]{:S(2)}) collective-permute-start(f32[9,32,384]{2,1,0:T(8,128)S(1)} %shard_map.86.weighted_ref), channel_id=1, source_target_pairs={{32,0},{64,32},{96,64},{128,96},{160,128},{192,160},{224,192},{256... | collective-permute-start | bytes 1327112 | tf_op jit(solution)/shard_map/ppermute | solution.py:570
  101.6 1.3 shard_map.84.refs_4_
  103.7 1.3 shard_map.87.refs_6_
  106.8 6.7 %shard_map.88 = (f32[18,32,384]{2,1,0:T(8,128)}, f32[18,32,384]{2,1,0:T(8,128)}, f32[1792,128]{1,0:T(8,128)}, f32[1792,128]{1,0:T(8,128)}, f32[8,128]{1,0:T(8,128)}) custom-call(s32[1]{0:T(128)} %bitcast.10.odd_ref.refs_0_, f32[5,5,32,384]{3,2,1,0:T(8,128)} %copy-done, f32[1792,128]{1,0:T(8,128)} %bitcast.53, f32[9,32,384]{2,1,0:T(8,128)} %copy-done.1, ...), custom_call_target="tpu_custom_call" | custom-call | tf_op jit(solution)/shard_map/pallas_call | solution.py:552
  114.8 48.2 %conditional.2 = (f32[1792,128]{1,0:T(8,128)S(1)}, f32[1792,128]{1,0:T(8,128)}) conditional(s32[]{:T(128)} %convert_element_type.4, f32[1792,128]{1,0:T(8,128)} %get-tuple-element.80, (f32[1792,128]{1,0:T(8,128)}, f32[1024,128]{1,0:T(8,128)}, f32[1024,128]{1,0:T(8,128)}) %tuple.36), branch_computations={%region_2.3_spmd, %region_3.4_spmd} | conditional | flops 1376256 | bytes 10978216 | solution.py:671
  114.9 1.8 maximum_maximum_fusion
  116.7 45.3 %all_to_all.32 = f32[32,112,128]{2,1,0:T(8,128)S(1)} all-to-all(f32[32,112,128]{2,1,0:T(8,128)S(1)} %maximum_maximum_fusion), channel_id=1, replica_groups=mesh['tm'=16,'lat'=32] {'lat'}, dimensions={0} | all-to-all | bytes 3670016 | tf_op jit(solution)/shard_map/cond/branch_1_fun/all_to_all | solution.py:43
  163.0 2.2 %collective-permute-start.6 = (f32[1792,128]{1,0:T(8,128)}, f32[1792,128]{1,0:T(8,128)}, u32[]{:S(2)}, u32[]{:S(2)}) collective-permute-start(f32[1792,128]{1,0:T(8,128)} %get-tuple-element.98.got_ref), channel_id=1, source_target_pairs={{32,0},{64,32},{96,64},{128,96},{160,128},{192,160},{224,192},{256... | collective-permute-start | bytes 2752520 | tf_op jit(solution)/shard_map/ppermute | solution.py:570
  165.3 1.6 shard_map.89
  167.6 4.4 %all-to-all-start.6 = ((f32[16,8,128]{2,1,0:T(8,128)}), f32[16,8,128]{2,1,0:T(8,128)S(1)}, u32[]{:S(2)}, u32[]{:S(2)}) async-start(f32[16,8,128]{2,1,0:T(8,128)} %broadcast_in_dim.32), calls=%async_computation.6 | async-start | bytes 131072 | tf_op jit(solution)/shard_map/all_to_all | solution.py:576
  172.0 2.6 %shard_map.90 = f32[1,4,1,49320]{3,2,1,0:T(1,128)S(1)} custom-call(f32[1792,128]{1,0:T(8,128)} %get-tuple-element.98.got_ref), custom_call_target="tpu_custom_call" | custom-call | tf_op jit(solution)/shard_map/pallas_call | solution.py:552
  174.6 2.7 %all-to-all-done.6 = f32[16,8,128]{2,1,0:T(8,128)S(1)} async-done(((f32[16,8,128]{2,1,0:T(8,128)}), f32[16,8,128]{2,1,0:T(8,128)S(1)}, u32[]{:S(2)}, u32[]{:S(2)}) %all-to-all-start.6) | async-done | bytes 65568 | tf_op jit(solution)/shard_map/all_to_all | solution.py:576
  177.3 26.5 %conditional.3 = ((f32[1,4,1,49320]{3,2,1,0:T(1,128)}, f32[1,4,1,49320]{3,2,1,0:T(1,128)})) conditional(s32[]{:T(128)} %convert_element_type.4, (f32[8,128]{1,0:T(8,128)S(1)}, f32[1,4,1,49320]{3,2,1,0:T(1,128)S(1)}, f32[1,4,1,49320]{3,2,1,0:T(1,128)S(1)}, f32[1,4,1,49320]{3,2,1,0:T(1,128)}, f32[1792,128]{1,0:T(8,128)}) %tuple.56, ...), branch_computations={%region_4.5_spmd, %region_5.6_spmd} | conditional | flops 262144 | bytes 4329480 | solution.py:692
  178.7 22.3 %all_to_all.34 = f32[32,64,128]{2,1,0:T(8,128)S(1)} all-to-all(f32[32,64,128]{2,1,0:T(8,128)S(1)} %pad_maximum_fusion), channel_id=1, replica_groups=mesh['tm'=16,'lat'=32] {'lat'}, dimensions={0} | all-to-all | bytes 2097152 | tf_op jit(solution)/shard_map/cond/branch_1_fun/all_to_all | solution.py:43
  201.0 2.9 %branch_1_fun.1 = (f32[1,4,1,49320]{3,2,1,0:T(1,128)}, f32[1,4,1,49320]{3,2,1,0:T(1,128)}) custom-call(f32[2048,128]{1,0:T(8,128)S(1)} %bitcast.49, f32[1792,128]{1,0:T(8,128)S(1)} %get-tuple-element.43.got_moved_ref, f32[1,4,1,49320]{3,2,1,0:T(1,128)S(1)} %get-tuple-element.44.own_ref, f32[1,4,1,49320]{3,2,1,0:T(1,128)S(1)} %get-tuple-element.45.image_ref), custom_call_target="tpu_custom_call" | custom-call | tf_op jit(solution)/shard_map/cond/branch_1_fun/pallas_call | solution.py:552
  (48 shorter events, 12.4 us)
Async XLA Ops:
  8.5 13.1 %copy-start.7 = (f32[1,4,1,49320]{3,2,1,0:T(1,128)S(1)}, f32[1,4,1,49320]{3,2,1,0:T(1,128)}, u32[]{:S(2)}) copy-start(f32[1,4,1,49320]{3,2,1,0:T(1,128)} %own_hbm.1) | copy-start | bytes 2367364
  8.5 18.0 %copy-start.12 = (s32[1,2048]{1,0:T(1,128)S(1)}, s32[1,2048]{1,0:T(1,128)}, u32[]{:S(2)}) copy-start(s32[1,2048]{1,0:T(1,128)} %param.14) | copy-start | bytes 24580
  8.5 64.6 %all-to-all-start.4 = ((f32[32,136,128]{2,1,0:T(8,128)}), f32[32,136,128]{2,1,0:T(8,128)S(1)}, u32[]{:S(2)}, u32[]{:S(2)}) async-start(f32[32,136,128]{2,1,0:T(8,128)} %bitcast.51), calls=%async_computation.4 | async-start | bytes 4456448 | tf_op jit(solution)/shard_map/all_to_all | solution.py:43
  21.6 4.9 %collective-permute-start = (f32[1,4,1,49320]{3,2,1,0:T(1,128)S(1)}, f32[1,4,1,49320]{3,2,1,0:T(1,128)}, u32[]{:S(2)}, u32[]{:S(2)}) collective-permute-start(f32[1,4,1,49320]{3,2,1,0:T(1,128)S(1)} %copy-done.7), channel_id=1, source_target_pairs={{32,0},{64,32},{96,64},{128,96},{160,128},{192,160},{224,192},{256... | collective-permute-start | bytes 2367368 | tf_op jit(solution)/shard_map/ppermute | solution.py:570
  73.1 32.8 %all-to-all-start.5 = ((f32[32,56,128]{2,1,0:T(8,128)}), f32[32,56,128]{2,1,0:T(8,128)S(1)}, u32[]{:S(2)}, u32[]{:S(2)}) async-start(f32[32,56,128]{2,1,0:T(8,128)} %bitcast.19), calls=%async_computation.5 | async-start | bytes 1835008 | tf_op jit(solution)/shard_map/all_to_all | solution.py:43
  83.7 5.4 %copy-start.1 = (f32[9,32,384]{2,1,0:T(8,128)}, f32[9,32,384]{2,1,0:T(8,128)S(1)}, u32[]{:S(2)}) copy-start(f32[9,32,384]{2,1,0:T(8,128)S(1)} %get-tuple-element.73.state_ref.refs_3_) | copy-start | bytes 1327108
  83.7 20.1 %copy-start = (f32[5,5,32,384]{3,2,1,0:T(8,128)}, f32[5,5,32,384]{3,2,1,0:T(8,128)S(1)}, u32[]{:S(2)}) copy-start(f32[5,5,32,384]{3,2,1,0:T(8,128)S(1)} %get-tuple-element.72.coef_ref.refs_1_) | copy-start | bytes 3686404
  83.7 5.1 %collective-permute-start.1 = (f32[9,32,384]{2,1,0:T(8,128)S(1)}, f32[9,32,384]{2,1,0:T(8,128)S(1)}, u32[]{:S(2)}, u32[]{:S(2)}) collective-permute-start(f32[9,32,384]{2,1,0:T(8,128)S(1)} %get-tuple-element.74), channel_id=1, source_target_pairs={{0,32},{32,64},{64,96},{96,128},{128,160},{160,192},{192,224},{224... | collective-permute-start | bytes 1327112 | tf_op jit(solution)/shard_map/ppermute | solution.py:570
  87.5 9.7 %copy-start.2 = (f32[9,32,384]{2,1,0:T(8,128)}, f32[9,32,384]{2,1,0:T(8,128)S(1)}, u32[]{:S(2)}) copy-start(f32[9,32,384]{2,1,0:T(8,128)S(1)} %get-tuple-element.75.state_ref.refs_5_) | copy-start | bytes 1327108
  87.5 9.3 %collective-permute-start.3 = (f32[9,32,384]{2,1,0:T(8,128)S(1)}, f32[9,32,384]{2,1,0:T(8,128)S(1)}, u32[]{:S(2)}, u32[]{:S(2)}) collective-permute-start(f32[9,32,384]{2,1,0:T(8,128)S(1)} %get-tuple-element.76), channel_id=1, source_target_pairs={{0,32},{32,64},{64,96},{96,128},{128,160},{160,192},{192,224},{224... | collective-permute-start | bytes 1327112 | tf_op jit(solution)/shard_map/ppermute | solution.py:570
  89.1 12.5 %collective-permute-start.2 = (f32[9,32,384]{2,1,0:T(8,128)S(1)}, f32[9,32,384]{2,1,0:T(8,128)S(1)}, u32[]{:S(2)}, u32[]{:S(2)}) collective-permute-start(f32[9,32,384]{2,1,0:T(8,128)S(1)} %shard_map.83.weighted_ref), channel_id=1, source_target_pairs={{32,0},{64,32},{96,64},{128,96},{160,128},{192,160},{224,192},{256... | collective-permute-start | bytes 1327112 | tf_op jit(solution)/shard_map/ppermute | solution.py:570
  97.2 6.5 %collective-permute-start.4 = (f32[9,32,384]{2,1,0:T(8,128)S(1)}, f32[9,32,384]{2,1,0:T(8,128)S(1)}, u32[]{:S(2)}, u32[]{:S(2)}) collective-permute-start(f32[9,32,384]{2,1,0:T(8,128)S(1)} %shard_map.86.weighted_ref), channel_id=1, source_target_pairs={{32,0},{64,32},{96,64},{128,96},{160,128},{192,160},{224,192},{256... | collective-permute-start | bytes 1327112 | tf_op jit(solution)/shard_map/ppermute | solution.py:570
  103.0 0.8 copy-start.3
  105.1 0.8 copy-start.4
  105.9 1.0 copy-start.11
  113.5 51.8 %collective-permute-start.5 = (f32[18,32,384]{2,1,0:T(8,128)}, f32[18,32,384]{2,1,0:T(8,128)}, u32[]{:S(2)}, u32[]{:S(2)}) collective-permute-start(f32[18,32,384]{2,1,0:T(8,128)} %get-tuple-element.78), channel_id=1, source_target_pairs={{0,32},{32,64},{64,96},{96,128},{128,160},{160,192},{192,224},{224... | collective-permute-start | bytes 2654216 | tf_op jit(solution)/shard_map/ppermute | solution.py:570
  114.8 50.5 %copy-start.5 = (f32[18,32,384]{2,1,0:T(8,128)S(1)}, f32[18,32,384]{2,1,0:T(8,128)}, u32[]{:S(2)}) copy-start(f32[18,32,384]{2,1,0:T(8,128)} %get-tuple-element.77.image_ref) | copy-start | bytes 2654212
  114.8 50.5 %copy-start.6 = (f32[8,128]{1,0:T(8,128)S(1)}, f32[8,128]{1,0:T(8,128)}, u32[]{:S(2)}) copy-start(f32[8,128]{1,0:T(8,128)} %get-tuple-element.79.sums_ref) | copy-start | bytes 12292
  163.0 3.9 %copy-start.9 = (f32[1792,128]{1,0:T(8,128)}, f32[1792,128]{1,0:T(8,128)S(1)}, u32[]{:S(2)}) copy-start(f32[1792,128]{1,0:T(8,128)S(1)} %get-tuple-element.90) | copy-start | bytes 2752516
  163.0 14.3 %collective-permute-start.6 = (f32[1792,128]{1,0:T(8,128)}, f32[1792,128]{1,0:T(8,128)}, u32[]{:S(2)}, u32[]{:S(2)}) collective-permute-start(f32[1792,128]{1,0:T(8,128)} %get-tuple-element.98.got_ref), channel_id=1, source_target_pairs={{32,0},{64,32},{96,64},{128,96},{160,128},{192,160},{224,192},{256... | collective-permute-start | bytes 2752520 | tf_op jit(solution)/shard_map/ppermute | solution.py:570
  166.9 10.4 %copy-start.8 = (f32[1,4,1,49320]{3,2,1,0:T(1,128)S(1)}, f32[1,4,1,49320]{3,2,1,0:T(1,128)}, u32[]{:S(2)}) copy-start(f32[1,4,1,49320]{3,2,1,0:T(1,128)} %own_hbm.1) | copy-start | bytes 2367364
  167.6 9.8 %copy-start.10 = (f32[1792,128]{1,0:T(8,128)S(1)}, f32[1792,128]{1,0:T(8,128)}, u32[]{:S(2)}) copy-start(f32[1792,128]{1,0:T(8,128)} %copy-done.9) | copy-start | bytes 2752516
  167.6 9.7 %all-to-all-start.6 = ((f32[16,8,128]{2,1,0:T(8,128)}), f32[16,8,128]{2,1,0:T(8,128)S(1)}, u32[]{:S(2)}, u32[]{:S(2)}) async-start(f32[16,8,128]{2,1,0:T(8,128)} %broadcast_in_dim.32), calls=%async_computation.6 | async-start | bytes 131072 | tf_op jit(solution)/shard_map/all_to_all | solution.py:576

commit v5 on v4

--- a/solution.py
+++ b/solution.py
@@ -246,17 +246,18 @@
 
 
 def last_kernel(
-    got_ref, got_moved_ref, own_ref, image_ref, increment_ref, slid_ref, tall, tall_rest
+    got_ref, first_half_ref, second_half_ref, own_ref, image_ref, increment_ref, slid_ref, tall, tall_rest
 ):
     rows = BACK_ROWS + 8
     on_own, on_image = scales_in(got_ref, rows, BACK_ROWS)
 
     def load(parity, row):
         cut, unit = divmod(row, UNITS)
-        at = unit // HALF * CUTS * HALF + cut * HALF + unit % HALF
+        half_ref = second_half_ref if unit >= HALF else first_half_ref
+        at = BACK_ROWS - HALF_ROWS + cut * HALF + unit % HALF
         first = pl.ds(parity * BACK_ROWS + at, 16, stride=2 * BACK_ROWS)
         second = pl.ds(parity * rows + row, 16, stride=2 * rows)
-        return on_own * got_moved_ref[first, :] + on_image * got_ref[second, :]
+        return on_own * half_ref[first, :] + on_image * got_ref[second, :]
 
     write_fields(load, slid_ref, tall, tall_rest)
     combined(increment_ref, on_own, own_ref, on_image, image_ref)
@@ -398,21 +399,35 @@
         put(state_ref, v, k)
         v = forward(v, coef_ref, level_of(first + k, odd))
         put(moved_ref, v, k)
-        put_rows(back_ref, HALF_ROWS, k, v, HALF)
+        if back_ref is not None:
+            put_rows(back_ref, HALF_ROWS, k, v, HALF)
         return carry
 
     lax.fori_loop(0, HALF, one, 0, unroll=3)
+
+
+def clear_half(back_ref):
     for row in range(CUTS * HALF, HALF_ROWS):
         back_ref[pl.ds(row, 32, stride=HALF_ROWS), :] = jnp.zeros((32, LANES), jnp.float32)
 
 
-def first_moved_kernel(odd_ref, got_ref, mark_ref, state_ref, moved_ref, back_ref, coef_ref):
+def half_back_kernel(planes_ref, back_ref):
+    def one(k, carry):
+        put_rows(back_ref, HALF_ROWS, k, get(planes_ref, k), HALF)
+        return carry
+
+    lax.fori_loop(0, HALF, one, 0, unroll=3)
+    clear_half(back_ref)
+
+
+def first_moved_kernel(odd_ref, got_ref, mark_ref, state_ref, moved_ref, coef_ref):
     fill_coefficients(got_ref, SEND_ROWS, coef_ref)
-    moved_planes(0, odd_ref, got_ref, coef_ref, state_ref, moved_ref, back_ref)
+    moved_planes(0, odd_ref, got_ref, coef_ref, state_ref, moved_ref, None)
 
 
 def second_moved_kernel(odd_ref, got_ref, coef_ref, state_ref, moved_ref, back_ref):
     moved_planes(HALF, odd_ref, got_ref, coef_ref, state_ref, moved_ref, back_ref)
+    clear_half(back_ref)
 
 
 def weight_plane(got_ref, unit):
@@ -432,10 +447,12 @@
     return blocks
 
 
-def weighted_kernel(first, state_ref, arriving_ref, got_ref, weighted_ref):
+def weighted_kernel(first, inner_ref, state_ref, arriving_ref, got_ref, weighted_ref):
+    keep = inner_ref[0].astype(jnp.float32)
+
     def step(w, k):
         pairs = zip(wrapped(w), get(state_ref, k), get(arriving_ref, k))
-        put(weighted_ref, [x * (s - m) for x, s, m in pairs], k)
+        put(weighted_ref, [x * (s - keep * m) for x, s, m in pairs], k)
 
     def one(k, carry):
         step(weight_plane(got_ref, first + k), k)
@@ -549,6 +566,7 @@
         if fetched:
             scratch.append(pltpu.SemaphoreType.DMA((len(fetched),)))
         spec = {"s": SMEM, "v": VMEM, "f": pl.BlockSpec(memory_space=pl.ANY)}
+        spec["a"] = spec["f"]
         return pl.pallas_call(
             whole,
             out_shape=outs,
@@ -564,9 +582,9 @@
     return run
 
 
-def passed_along(shard, by):
+def passed_along(shard, by, ring=False):
     devices = lax.axis_size("tm")
-    pairs = [(i, i + by) for i in range(devices) if 0 <= i + by < devices]
+    pairs = [(i, (i + by) % devices) for i in range(devices) if ring or 0 <= i + by < devices]
     return lax.ppermute(shard, "tm", pairs)
 
 
@@ -618,17 +636,19 @@
 
 def body(forcing_rhs, courant_lon, courant_lat, error_weight, obs_cell, obs_weight):
     odd = lax.rem(lax.axis_index("lat"), 2).reshape(1)
+    here, subs = lax.axis_index("tm"), lax.axis_size("tm")
+    inner = jnp.minimum(here, 1).reshape(1)
     got = exchanged(pack(forcing_rhs, courant_lon, courant_lat, error_weight))
     next_own = passed_along(forcing_rhs, -1)
     obs_cell, next_own = lax.optimization_barrier((obs_cell, next_own))
     obs = cells_in_planes(obs_cell[0], obs_weight[0])
-    got, mark = lax.optimization_barrier((got, obs[:8]))
+    got, mark = lax.optimization_barrier((got, obs))
     got_obs = exchanged(obs)
 
-    first_state, first_moved, first_back, coef = call(
-        first_moved_kernel, [HALF_PLANES, HALF_PLANES, HALF_BACK, COEF], "svv"
+    first_state, first_moved, coef = call(
+        first_moved_kernel, [HALF_PLANES, HALF_PLANES, COEF], "sva"
     )(odd, got, mark)
-    first_arriving = passed_along(first_moved, 1)
+    first_arriving = passed_along(first_moved, 1, True)
     second_state, second_moved, second_back = call(
         second_moved_kernel, [HALF_PLANES, HALF_PLANES, HALF_BACK], "svv"
     )(odd, got, coef)
@@ -636,7 +656,7 @@
 
     def weigh(first, state, arriving):
         kernel = functools.partial(weighted_kernel, first)
-        return call(kernel, [HALF_PLANES], "vvv")(state, arriving, got)[0]
+        return call(kernel, [HALF_PLANES], "svvv")(inner, state, arriving, got)[0]
 
     def pull(first, weighted, later):
         kernel = functools.partial(adjoint_kernel, first)
@@ -652,25 +672,32 @@
         image_kernel, [PLANES, PLANES, BACK, BACK, SUMS], "sffffff"
     )(odd, coef, got_obs, first_state, first_part, second_state, second_part)
     row_shape = jax.ShapeDtypeStruct(forcing_rhs.shape, jnp.float32)
-    is_final = lax.axis_index("tm") == lax.axis_size("tm") - 1
-
-    def image_and_moved(back):
-        parts = [
-            blocks_of(back),
-            blocks_of(first_back)[:, : CUTS * HALF],
-            blocks_of(second_back)[:, : CUTS * HALF],
-            jnp.zeros((32, BACK_ROWS - 2 * CUTS * HALF, LANES), jnp.float32),
-        ]
-        both = blocks_of(exchanged(jnp.concatenate(parts, 1).reshape(-1, LANES)))
-        return both[:, :BACK_ROWS].reshape(-1, LANES), both[:, BACK_ROWS:].reshape(-1, LANES)
-
     def image_alone(back):
-        return exchanged(back), jnp.zeros_like(back)
+        image = exchanged(back)
+        return image, image, jnp.zeros_like(image)
+
+    def image_and(back, half):
+        both = jnp.concatenate([blocks_of(back), blocks_of(half)], 1)
+        both = blocks_of(exchanged(both.reshape(-1, LANES)))
+        image, half = both[:, :BACK_ROWS], both[:, HALF_ROWS:]
+        return image.reshape(-1, LANES), half.reshape(-1, LANES)
+
+    def image_of_first(back):
+        (half_back,) = call(half_back_kernel, [HALF_BACK], "v")(first_arriving)
+        image, half = image_and(back, half_back)
+        return image, half, jnp.zeros_like(image)
+
+    def image_of_last(back):
+        image, half = image_and(back, second_back)
+        return image, image, half
 
     image_arriving = passed_along(image_moved, 1)
-    got_image, got_moved = lax.cond(is_final, image_and_moved, image_alone, image_back)
+    which = jnp.where(here == subs - 1, 2, jnp.where(here == 0, 1, 0))
+    got_image, leaving, got_half = lax.switch(
+        which, (image_alone, image_of_first, image_of_last), image_back
+    )
     (sums,) = call(norm_kernel, [SUMS], "vvvv")(image, image_arriving, got, sums)
-    next_got_image = passed_along(got_image, -1)
+    next_got_image = passed_along(leaving, -1, True)
     (image_own,) = call(unpack_kernel, [row_shape], "v", TALL)(got_image)
     sums = summed_over_tm(sums)
     sums, image_own, next_got_image = lax.optimization_barrier((sums, image_own, next_got_image))
@@ -678,8 +705,8 @@
     def last(tile):
         parts = [blocks_of(image_moved_back), jnp.broadcast_to(tile[None], (32, 8, LANES))]
         back = exchanged(jnp.concatenate(parts, 1).reshape(-1, LANES))
-        return call(last_kernel, [row_shape] * 2, "vvvv", TALL)(
-            back, got_moved, forcing_rhs, image_own
+        return call(last_kernel, [row_shape] * 2, "vvvvv", TALL)(
+            back, next_got_image, got_half, forcing_rhs, image_own
         )
 
     def other(tile):
@@ -689,7 +716,7 @@
             back, forcing_rhs, image_own, next_own, next_got_image
         )
 
-    return tuple(lax.cond(is_final, last, other, sums))
+    return tuple(lax.cond(here == subs - 1, last, other, sums))
 
 
 def solution(mesh):

time: 205 us -> 205 us (level)
  blocking collectives: 67.6 us -> 63 us
  local copies, waits for them, and re-layouts: 5.06 us -> 9.08 us
  starting transfers between devices: 46.5 us -> 42.7 us
  Pallas kernels: 30.2 us -> 33.3 us
    ppermute x7, starting transfers between devices: 21.9 us -> 15 us  [passed_along(): return lax.ppermute(shard, 'tm', pairs)]
    all_to_all x2, blocking collectives: 67.6 us -> 63 us  [exchanged(): return lax.all_to_all(chunks, 'lat', 0, 0, tiled=True).reshape(-1, LANES)]
    pallas_call x10, Pallas kernels: 22.4 us -> 25.5 us  [run(): pl.pallas_call(whole, out_shape=outs, in_specs=[spec[i] for i in ins], ou...]
    all_to_all x1, starting transfers between devices: 4.42 us -> 7.45 us  [summed_over_tm(): return lax.all_to_all(copies, 'tm', 0, 0, tiled=True).sum(0)]
    unnamed x26 -> x28, local copies, waits for them, and re-layouts: 2.58 us -> 5.17 us
    cond x0 -> x1, local copies, waits for them, and re-layouts: none -> 2.18 us
  transfers between devices with their start and end apart: 10 -> 10, of which waited for: 3 -> 4; matrix products, arithmetic and copies ran while one was open for 8% -> 9% of each run, Pallas kernels for 6% -> 7%
where the time goes in v5:
time: 205 us; the launch traced here: 204 us
  blocking collectives  63 us (31%)
  starting transfers between devices  42.7 us (21%)
  waiting for transfers between devices  39.4 us (19%)
  Pallas kernels  33.3 us (16%)
  other arithmetic  15.5 us (8%)
  local copies, waits for them, and re-layouts  9.08 us (4%)
    all_to_all x2, blocking collectives, exchanged(): return lax.all_to_all(chunks, 'lat', 0, 0, tiled=True).reshape(-1, LANES)  63 us
    all_to_all x2, waiting for transfers between devices, exchanged(): return lax.all_to_all(chunks, 'lat', 0, 0, tiled=True).reshape(-1, LANES)  33.9 us
    pallas_call x10, Pallas kernels, run(): pl.pallas_call(whole, out_shape=outs, in_specs=[spec[i] for i in ins], ou...  25.5 us
    all_to_all x2, starting transfers between devices, exchanged(): return lax.all_to_all(chunks, 'lat', 0, 0, tiled=True).reshape(-1, LANES)  20.3 us
    ppermute x7, starting transfers between devices, passed_along(): return lax.ppermute(shard, 'tm', pairs)  15 us
    scatter-add x1, other arithmetic, cells_in_planes(): empty.at[row * LANES + lane % LANES].add(weight)  12.4 us
    pallas_call x1, Pallas kernels, pack(): pl.pallas_call(pack_kernel, out_shape=jax.ShapeDtypeStruct((32 * SEND_ROW...  7.82 us
    all_to_all x1, starting transfers between devices, summed_over_tm(): return lax.all_to_all(copies, 'tm', 0, 0, tiled=True).sum(0)  7.45 us
  transfers between devices with their start and end apart: 10, of which 4 were waited for; matrix products, arithmetic and copies ran while one was open for 9% of the time, Pallas kernels for 7%

profile of v5, /device:TPU:57, one launch (start us, length us, event | category | flops | bytes accessed | tf_op | source)
XLA Modules:
  0.0 203.9 jit_solution(12879030168472192676)
XLA Ops:
  0.6 7.8 %shard_map.81 = f32[4352,128]{1,0:T(8,128)} custom-call(f32[1,4,1,49320]{3,2,1,0:T(1,128)} %own_hbm.1, f32[1,1,49320]{2,1,0:T(1,128)} %lon_hbm.1, f32[1,1,49320]{2,1,0:T(1,128)} %lat_hbm.1, f32[1,4,1,49320]{3,2,1,0:T(1,128)} %weight_hbm.1), custom_call_target="tpu_custom_call" | custom-call | tf_op jit(solution)/shard_map/pallas_call | solution.py:166
  8.5 13.0 %all-to-all-start.5 = ((f32[32,136,128]{2,1,0:T(8,128)}), f32[32,136,128]{2,1,0:T(8,128)S(1)}, u32[]{:S(2)}, u32[]{:S(2)}) async-start(f32[32,136,128]{2,1,0:T(8,128)} %bitcast.51), calls=%async_computation.5 | async-start | bytes 4456448 | tf_op jit(solution)/shard_map/all_to_all | solution.py:43
  21.5 3.8 %collective-permute-start = (f32[1,4,1,49320]{3,2,1,0:T(1,128)S(1)}, f32[1,4,1,49320]{3,2,1,0:T(1,128)}, u32[]{:S(2)}, u32[]{:S(2)}) collective-permute-start(f32[1,4,1,49320]{3,2,1,0:T(1,128)S(1)} %copy-done.10), channel_id=1, source_target_pairs={{32,0},{64,32},{96,64},{128,96},{160,128},{192,160},{224,192},{256... | collective-permute-start | bytes 2367368 | tf_op jit(solution)/shard_map/ppermute | solution.py:588
  26.8 12.4 %scatter_custom_fusion = f32[229376]{0:T(1024)} fusion(s32[2048]{0:T(1024)S(1)} %bitcast.58, f32[2048]{0:T(1024)} %bitcast.59, f32[]{:T(128)} %constant.107.clone.1), kind=kCustom, calls=%fused_computation.4 | custom fusion | flops 2048 | bytes 918016 | tf_op jit(solution)/shard_map/scatter-add | solution.py:634
  39.2 33.9 %all-to-all-done.5 = f32[32,136,128]{2,1,0:T(8,128)S(1)} async-done(((f32[32,136,128]{2,1,0:T(8,128)}), f32[32,136,128]{2,1,0:T(8,128)S(1)}, u32[]{:S(2)}, u32[]{:S(2)}) %all-to-all-start.5) | async-done | bytes 2228256 | tf_op jit(solution)/shard_map/all_to_all | solution.py:43
  73.1 7.3 %all-to-all-start.6 = ((f32[32,56,128]{2,1,0:T(8,128)}), f32[32,56,128]{2,1,0:T(8,128)}, u32[]{:S(2)}, u32[]{:S(2)}) async-start(f32[32,56,128]{2,1,0:T(8,128)} %bitcast.18), calls=%async_computation.6 | async-start | bytes 1835008 | tf_op jit(solution)/shard_map/all_to_all | solution.py:43
  80.4 2.3 %shard_map.82 = (f32[9,32,384]{2,1,0:T(8,128)S(1)}, f32[9,32,384]{2,1,0:T(8,128)}, f32[5,5,32,384]{3,2,1,0:T(8,128)S(1)}) custom-call(s32[1]{0:T(128)} %bitcast.9.odd_ref.refs_0_, f32[4352,128]{1,0:T(8,128)S(1)} %bitcast.43, f32[1792,128]{1,0:T(8,128)} %bitcast.17.mark_ref), custom_call_target="tpu_custom_call" | custom-call | tf_op jit(solution)/shard_map/pallas_call | solution.py:570
  84.0 2.7 %shard_map.85 = (f32[9,32,384]{2,1,0:T(8,128)S(1)}, f32[9,32,384]{2,1,0:T(8,128)}, f32[1024,128]{1,0:T(8,128)}) custom-call(s32[1]{0:T(128)} %bitcast.9.odd_ref.refs_0_, f32[4352,128]{1,0:T(8,128)S(1)} %bitcast.44, f32[5,5,32,384]{3,2,1,0:T(8,128)S(1)} %get-tuple-element.75.coef_ref.refs_1_), custom_call_target="tpu_custom_call" | custom-call | tf_op jit(solution)/shard_map/pallas_call | solution.py:570
  90.6 1.4 shard_map.83.weighted_ref
  92.0 5.0 %collective-permute-start.2 = (f32[9,32,384]{2,1,0:T(8,128)S(1)}, f32[9,32,384]{2,1,0:T(8,128)S(1)}, u32[]{:S(2)}, u32[]{:S(2)}) collective-permute-start(f32[9,32,384]{2,1,0:T(8,128)S(1)} %shard_map.83.weighted_ref), channel_id=1, source_target_pairs={{32,0},{64,32},{96,64},{128,96},{160,128},{192,160},{224,192},{256... | collective-permute-start | bytes 1327112 | tf_op jit(solution)/shard_map/ppermute | solution.py:588
  97.0 1.4 shard_map.86.weighted_ref
  98.5 3.0 %collective-permute-start.4 = (f32[9,32,384]{2,1,0:T(8,128)S(1)}, f32[9,32,384]{2,1,0:T(8,128)S(1)}, u32[]{:S(2)}, u32[]{:S(2)}) collective-permute-start(f32[9,32,384]{2,1,0:T(8,128)S(1)} %shard_map.86.weighted_ref), channel_id=1, source_target_pairs={{32,0},{64,32},{96,64},{128,96},{160,128},{192,160},{224,192},{256... | collective-permute-start | bytes 1327112 | tf_op jit(solution)/shard_map/ppermute | solution.py:588
  105.8 6.7 %shard_map.88 = (f32[18,32,384]{2,1,0:T(8,128)}, f32[18,32,384]{2,1,0:T(8,128)}, f32[1792,128]{1,0:T(8,128)}, f32[1792,128]{1,0:T(8,128)}, f32[8,128]{1,0:T(8,128)}) custom-call(s32[1]{0:T(128)} %bitcast.9.odd_ref.refs_0_, f32[5,5,32,384]{3,2,1,0:T(8,128)} %copy-done, f32[1792,128]{1,0:T(8,128)} %bitcast.19.refs_2_, f32[9,32,384]{2,1,0:T(8,128)} %copy-done.3, ...), custom_call_target="tpu_custom_call" | custom-call | tf_op jit(solution)/shard_map/pallas_call | solution.py:570
  113.8 45.2 %conditional.2 = (f32[1792,128]{1,0:T(8,128)S(1)}, f32[32,56,128]{2,1,0:T(8,128)}, f32[32,56,128]{2,1,0:T(8,128)}) conditional(s32[]{:T(128)} %clamp.3, f32[1792,128]{1,0:T(8,128)} %get-tuple-element.83, (f32[1792,128]{1,0:T(8,128)}, f32[9,32,384]{2,1,0:T(8,128)}) %tuple.34, (f32[1792,128]{1,0:T(8,128)}, f32[1024,128]{1,0:T(8,128)}) %tuple.35), branch_computations={%region_2.3_spmd, %region_3.4_spmd, %region_4.5_spmd} | conditional | flops 360448 | bytes 14024760 | solution.py:696
  113.8 1.5 pad_maximum_fusion.1
  115.3 40.4 %all_to_all.37 = f32[32,88,128]{2,1,0:T(8,128)S(1)} all-to-all(f32[32,88,128]{2,1,0:T(8,128)S(1)} %pad_maximum_fusion.1), channel_id=1, replica_groups=mesh['tm'=16,'lat'=32] {'lat'}, dimensions={0} | all-to-all | bytes 2883584 | tf_op jit(solution)/shard_map/cond/branch_2_fun/all_to_all | solution.py:43
  156.8 2.2 %copy.20 = f32[32,56,128]{2,1,0:T(8,128)} copy(f32[32,56,128]{2,1,0:T(8,128)} %get-tuple-element.111) | data formatting | bytes 1835008 | tf_op jit(solution)/shard_map/cond
  160.0 1.6 shard_map.89
  162.2 7.5 %all-to-all-start.7 = ((f32[16,8,128]{2,1,0:T(8,128)}), f32[16,8,128]{2,1,0:T(8,128)S(1)}, u32[]{:S(2)}, u32[]{:S(2)}) async-start(f32[16,8,128]{2,1,0:T(8,128)} %broadcast_in_dim.32), calls=%async_computation.7 | async-start | bytes 131072 | tf_op jit(solution)/shard_map/all_to_all | solution.py:594
  169.7 2.6 %shard_map.90 = f32[1,4,1,49320]{3,2,1,0:T(1,128)S(1)} custom-call(f32[1792,128]{1,0:T(8,128)} %bitcast.21.got_ref), custom_call_target="tpu_custom_call" | custom-call | tf_op jit(solution)/shard_map/pallas_call | solution.py:570
  172.3 3.5 %all-to-all-done.7 = f32[16,8,128]{2,1,0:T(8,128)S(1)} async-done(((f32[16,8,128]{2,1,0:T(8,128)}), f32[16,8,128]{2,1,0:T(8,128)S(1)}, u32[]{:S(2)}, u32[]{:S(2)}) %all-to-all-start.7) | async-done | bytes 65568 | tf_op jit(solution)/shard_map/all_to_all | solution.py:594
  175.9 28.0 %conditional.3 = ((f32[1,4,1,49320]{3,2,1,0:T(1,128)}, f32[1,4,1,49320]{3,2,1,0:T(1,128)})) conditional(s32[]{:T(128)} %convert_element_type.3, (f32[8,128]{1,0:T(8,128)S(1)}, f32[1,4,1,49320]{3,2,1,0:T(1,128)S(1)}, f32[1,4,1,49320]{3,2,1,0:T(1,128)S(1)}, f32[1,4,1,49320]{3,2,1,0:T(1,128)}, f32[1792,128]{1,0:T(8,128)}) %tuple.52, ...), branch_computations={%region_5.6_spmd, %region_6.7_spmd} | conditional | flops 262144 | bytes 4329480 | solution.py:719
  177.3 22.6 %all_to_all.39 = f32[32,64,128]{2,1,0:T(8,128)S(1)} all-to-all(f32[32,64,128]{2,1,0:T(8,128)S(1)} %pad_maximum_fusion.2), channel_id=1, replica_groups=mesh['tm'=16,'lat'=32] {'lat'}, dimensions={0} | all-to-all | bytes 2097152 | tf_op jit(solution)/shard_map/cond/branch_1_fun/all_to_all | solution.py:43
  199.9 4.1 %branch_1_fun.3 = (f32[1,4,1,49320]{3,2,1,0:T(1,128)}, f32[1,4,1,49320]{3,2,1,0:T(1,128)}) custom-call(f32[2048,128]{1,0:T(8,128)S(1)} %bitcast.48, f32[1792,128]{1,0:T(8,128)} %get-tuple-element.45.first_half_ref, f32[1792,128]{1,0:T(8,128)S(1)} %get-tuple-element.46.second_half_ref, f32[1,4,1,49320]{3,2,1,0:T(1,128)S(1)} %get-tuple-element.47.own_ref, ...), custom_call_target="tpu_custom_call" | custom-call | tf_op jit(solution)/shard_map/cond/branch_1_fun/pallas_call | solution.py:570
  (48 shorter events, 16.3 us)
Async XLA Ops:
  8.5 13.1 %copy-start.10 = (f32[1,4,1,49320]{3,2,1,0:T(1,128)S(1)}, f32[1,4,1,49320]{3,2,1,0:T(1,128)}, u32[]{:S(2)}) copy-start(f32[1,4,1,49320]{3,2,1,0:T(1,128)} %own_hbm.1) | copy-start | bytes 2367364
  8.5 18.0 %copy-start.14 = (s32[1,2048]{1,0:T(1,128)S(1)}, s32[1,2048]{1,0:T(1,128)}, u32[]{:S(2)}) copy-start(s32[1,2048]{1,0:T(1,128)} %param.15) | copy-start | bytes 24580
  8.5 64.6 %all-to-all-start.5 = ((f32[32,136,128]{2,1,0:T(8,128)}), f32[32,136,128]{2,1,0:T(8,128)S(1)}, u32[]{:S(2)}, u32[]{:S(2)}) async-start(f32[32,136,128]{2,1,0:T(8,128)} %bitcast.51), calls=%async_computation.5 | async-start | bytes 4456448 | tf_op jit(solution)/shard_map/all_to_all | solution.py:43
  21.5 4.9 %collective-permute-start = (f32[1,4,1,49320]{3,2,1,0:T(1,128)S(1)}, f32[1,4,1,49320]{3,2,1,0:T(1,128)}, u32[]{:S(2)}, u32[]{:S(2)}) collective-permute-start(f32[1,4,1,49320]{3,2,1,0:T(1,128)S(1)} %copy-done.10), channel_id=1, source_target_pairs={{32,0},{64,32},{96,64},{128,96},{160,128},{192,160},{224,192},{256... | collective-permute-start | bytes 2367368 | tf_op jit(solution)/shard_map/ppermute | solution.py:588
  73.1 32.7 %all-to-all-start.6 = ((f32[32,56,128]{2,1,0:T(8,128)}), f32[32,56,128]{2,1,0:T(8,128)}, u32[]{:S(2)}, u32[]{:S(2)}) async-start(f32[32,56,128]{2,1,0:T(8,128)} %bitcast.18), calls=%async_computation.6 | async-start | bytes 1835008 | tf_op jit(solution)/shard_map/all_to_all | solution.py:43
  82.7 0.8 copy-start.3
  83.4 20.2 %copy-start = (f32[5,5,32,384]{3,2,1,0:T(8,128)}, f32[5,5,32,384]{3,2,1,0:T(8,128)S(1)}, u32[]{:S(2)}) copy-start(f32[5,5,32,384]{3,2,1,0:T(8,128)S(1)} %get-tuple-element.75.coef_ref.refs_1_) | copy-start | bytes 3686404
  83.4 6.2 %collective-permute-start.1 = (f32[9,32,384]{2,1,0:T(8,128)}, f32[9,32,384]{2,1,0:T(8,128)}, u32[]{:S(2)}, u32[]{:S(2)}) collective-permute-start(f32[9,32,384]{2,1,0:T(8,128)} %get-tuple-element.77), channel_id=1, source_target_pairs={{0,32},{32,64},{64,96},{96,128},{128,160},{160,192},{192,224},{224... | collective-permute-start | bytes 1327112 | tf_op jit(solution)/shard_map/ppermute | solution.py:588
  86.7 0.8 copy-start.5
  87.5 9.5 %collective-permute-start.3 = (f32[9,32,384]{2,1,0:T(8,128)}, f32[9,32,384]{2,1,0:T(8,128)}, u32[]{:S(2)}, u32[]{:S(2)}) collective-permute-start(f32[9,32,384]{2,1,0:T(8,128)} %get-tuple-element.79), channel_id=1, source_target_pairs={{0,32},{32,64},{64,96},{96,128},{128,160},{160,192},{192,224},{224... | collective-permute-start | bytes 1327112 | tf_op jit(solution)/shard_map/ppermute | solution.py:588
  89.6 1.0 copy-start.4
  90.6 6.4 %copy-start.6 = (f32[9,32,384]{2,1,0:T(8,128)S(1)}, f32[9,32,384]{2,1,0:T(8,128)}, u32[]{:S(2)}) copy-start(f32[9,32,384]{2,1,0:T(8,128)} %copy-done.5) | copy-start | bytes 1327108
  92.0 9.5 %collective-permute-start.2 = (f32[9,32,384]{2,1,0:T(8,128)S(1)}, f32[9,32,384]{2,1,0:T(8,128)S(1)}, u32[]{:S(2)}, u32[]{:S(2)}) collective-permute-start(f32[9,32,384]{2,1,0:T(8,128)S(1)} %shard_map.83.weighted_ref), channel_id=1, source_target_pairs={{32,0},{64,32},{96,64},{128,96},{160,128},{192,160},{224,192},{256... | collective-permute-start | bytes 1327112 | tf_op jit(solution)/shard_map/ppermute | solution.py:588
  98.5 5.1 %collective-permute-start.4 = (f32[9,32,384]{2,1,0:T(8,128)S(1)}, f32[9,32,384]{2,1,0:T(8,128)S(1)}, u32[]{:S(2)}, u32[]{:S(2)}) collective-permute-start(f32[9,32,384]{2,1,0:T(8,128)S(1)} %shard_map.86.weighted_ref), channel_id=1, source_target_pairs={{32,0},{64,32},{96,64},{128,96},{160,128},{192,160},{224,192},{256... | collective-permute-start | bytes 1327112 | tf_op jit(solution)/shard_map/ppermute | solution.py:588
  102.8 0.8 copy-start.1
  104.9 0.8 copy-start.2
  112.4 46.5 %collective-permute-start.5 = (f32[18,32,384]{2,1,0:T(8,128)}, f32[18,32,384]{2,1,0:T(8,128)}, u32[]{:S(2)}, u32[]{:S(2)}) collective-permute-start(f32[18,32,384]{2,1,0:T(8,128)} %get-tuple-element.81), channel_id=1, source_target_pairs={{0,32},{32,64},{64,96},{96,128},{128,160},{160,192},{192,224},{224... | collective-permute-start | bytes 2654216 | tf_op jit(solution)/shard_map/ppermute | solution.py:588
  113.8 46.2 %copy-start.7 = (f32[18,32,384]{2,1,0:T(8,128)S(1)}, f32[18,32,384]{2,1,0:T(8,128)}, u32[]{:S(2)}) copy-start(f32[18,32,384]{2,1,0:T(8,128)} %get-tuple-element.80.image_ref) | copy-start | bytes 2654212
  113.8 46.2 %copy-start.8 = (f32[8,128]{1,0:T(8,128)S(1)}, f32[8,128]{1,0:T(8,128)}, u32[]{:S(2)}) copy-start(f32[8,128]{1,0:T(8,128)} %get-tuple-element.82.sums_ref) | copy-start | bytes 12292
  159.0 1.0 copy-start.12
  159.0 16.9 %collective-permute-start.6 = (f32[1792,128]{1,0:T(8,128)}, f32[1792,128]{1,0:T(8,128)}, u32[]{:S(2)}, u32[]{:S(2)}) collective-permute-start(f32[1792,128]{1,0:T(8,128)} %bitcast.22), channel_id=1, source_target_pairs={{0,480},{32,0},{64,32},{96,64},{128,96},{160,128},{192,160},{224,1... | collective-permute-start | bytes 2752520 | tf_op jit(solution)/shard_map/ppermute | solution.py:588
  161.6 14.3 %copy-start.11 = (f32[1,4,1,49320]{3,2,1,0:T(1,128)S(1)}, f32[1,4,1,49320]{3,2,1,0:T(1,128)}, u32[]{:S(2)}) copy-start(f32[1,4,1,49320]{3,2,1,0:T(1,128)} %own_hbm.1) | copy-start | bytes 2367364
  161.6 14.3 %copy-start.13 = (f32[1792,128]{1,0:T(8,128)S(1)}, f32[1792,128]{1,0:T(8,128)}, u32[]{:S(2)}) copy-start(f32[1792,128]{1,0:T(8,128)} %copy-done.12) | copy-start | bytes 2752516
  162.2 13.6 %all-to-all-start.7 = ((f32[16,8,128]{2,1,0:T(8,128)}), f32[16,8,128]{2,1,0:T(8,128)S(1)}, u32[]{:S(2)}, u32[]{:S(2)}) async-start(f32[16,8,128]{2,1,0:T(8,128)} %broadcast_in_dim.32), calls=%async_computation.7 | async-start | bytes 131072 | tf_op jit(solution)/shard_map/all_to_all | solution.py:594

commit v6 on v4

--- a/solution.py
+++ b/solution.py
@@ -549,6 +549,7 @@
         if fetched:
             scratch.append(pltpu.SemaphoreType.DMA((len(fetched),)))
         spec = {"s": SMEM, "v": VMEM, "f": pl.BlockSpec(memory_space=pl.ANY)}
+        spec["a"] = spec["f"]
         return pl.pallas_call(
             whole,
             out_shape=outs,
@@ -622,11 +623,11 @@
     next_own = passed_along(forcing_rhs, -1)
     obs_cell, next_own = lax.optimization_barrier((obs_cell, next_own))
     obs = cells_in_planes(obs_cell[0], obs_weight[0])
-    got, mark = lax.optimization_barrier((got, obs[:8]))
+    got, mark = lax.optimization_barrier((got, obs))
     got_obs = exchanged(obs)
 
     first_state, first_moved, first_back, coef = call(
-        first_moved_kernel, [HALF_PLANES, HALF_PLANES, HALF_BACK, COEF], "svv"
+        first_moved_kernel, [HALF_PLANES, HALF_PLANES, HALF_BACK, COEF], "sva"
     )(odd, got, mark)
     first_arriving = passed_along(first_moved, 1)
     second_state, second_moved, second_back = call(

time: 205 us -> 204 us (level)
  no operation moved by 1% of the time
where the time goes in v6:
time: 204 us; the launch traced here: 203 us
  blocking collectives  67.6 us (33%)
  starting transfers between devices  46.5 us (23%)
  waiting for transfers between devices  37.8 us (19%)
  Pallas kernels  30.2 us (15%)
  other arithmetic  15.8 us (8%)
  local copies, waits for them, and re-layouts  4.37 us (2%)
    all_to_all x2, blocking collectives, exchanged(): return lax.all_to_all(chunks, 'lat', 0, 0, tiled=True).reshape(-1, LANES)  67.6 us
    all_to_all x2, waiting for transfers between devices, exchanged(): return lax.all_to_all(chunks, 'lat', 0, 0, tiled=True).reshape(-1, LANES)  34 us
    pallas_call x10, Pallas kernels, run(): pl.pallas_call(whole, out_shape=outs, in_specs=[spec[i] for i in ins], ou...  22.4 us
    ppermute x7, starting transfers between devices, passed_along(): return lax.ppermute(shard, 'tm', pairs)  21.9 us
    all_to_all x2, starting transfers between devices, exchanged(): return lax.all_to_all(chunks, 'lat', 0, 0, tiled=True).reshape(-1, LANES)  20.2 us
    scatter-add x1, other arithmetic, cells_in_planes(): empty.at[row * LANES + lane % LANES].add(weight)  12.4 us
    pallas_call x1, Pallas kernels, pack(): pl.pallas_call(pack_kernel, out_shape=jax.ShapeDtypeStruct((32 * SEND_ROW...  7.85 us
    all_to_all x1, starting transfers between devices, summed_over_tm(): return lax.all_to_all(copies, 'tm', 0, 0, tiled=True).sum(0)  4.42 us
  transfers between devices with their start and end apart: 10, of which 3 were waited for; matrix products, arithmetic and copies ran while one was open for 8% of the time, Pallas kernels for 6%

profile of v6, /device:TPU:57, one launch (start us, length us, event | category | flops | bytes accessed | tf_op | source)
XLA Modules:
  0.0 203.2 jit_solution(13633405530039236048)
XLA Ops:
  0.6 7.8 %shard_map.81 = f32[4352,128]{1,0:T(8,128)} custom-call(f32[1,4,1,49320]{3,2,1,0:T(1,128)} %own_hbm.1, f32[1,1,49320]{2,1,0:T(1,128)} %lon_hbm.1, f32[1,1,49320]{2,1,0:T(1,128)} %lat_hbm.1, f32[1,4,1,49320]{3,2,1,0:T(1,128)} %weight_hbm.1), custom_call_target="tpu_custom_call" | custom-call | tf_op jit(solution)/shard_map/pallas_call | solution.py:166
  8.5 13.0 %all-to-all-start.4 = ((f32[32,136,128]{2,1,0:T(8,128)}), f32[32,136,128]{2,1,0:T(8,128)S(1)}, u32[]{:S(2)}, u32[]{:S(2)}) async-start(f32[32,136,128]{2,1,0:T(8,128)} %bitcast.50), calls=%async_computation.4 | async-start | bytes 4456448 | tf_op jit(solution)/shard_map/all_to_all | solution.py:43
  21.6 3.8 %collective-permute-start = (f32[1,4,1,49320]{3,2,1,0:T(1,128)S(1)}, f32[1,4,1,49320]{3,2,1,0:T(1,128)}, u32[]{:S(2)}, u32[]{:S(2)}) collective-permute-start(f32[1,4,1,49320]{3,2,1,0:T(1,128)S(1)} %copy-done.7), channel_id=1, source_target_pairs={{32,0},{64,32},{96,64},{128,96},{160,128},{192,160},{224,192},{256... | collective-permute-start | bytes 2367368 | tf_op jit(solution)/shard_map/ppermute | solution.py:571
  26.8 12.4 %scatter_custom_fusion = f32[229376]{0:T(1024)} fusion(s32[2048]{0:T(1024)S(1)} %bitcast.58, f32[2048]{0:T(1024)} %bitcast.59, f32[]{:T(128)} %constant.107.clone.1), kind=kCustom, calls=%fused_computation.3 | custom fusion | flops 2048 | bytes 918016 | tf_op jit(solution)/shard_map/scatter-add | solution.py:617
  39.2 34.0 %all-to-all-done.4 = f32[32,136,128]{2,1,0:T(8,128)S(1)} async-done(((f32[32,136,128]{2,1,0:T(8,128)}), f32[32,136,128]{2,1,0:T(8,128)S(1)}, u32[]{:S(2)}, u32[]{:S(2)}) %all-to-all-start.4) | async-done | bytes 2228256 | tf_op jit(solution)/shard_map/all_to_all | solution.py:43
  73.1 7.1 %all-to-all-start.5 = ((f32[32,56,128]{2,1,0:T(8,128)}), f32[32,56,128]{2,1,0:T(8,128)S(1)}, u32[]{:S(2)}, u32[]{:S(2)}) async-start(f32[32,56,128]{2,1,0:T(8,128)} %bitcast.19), calls=%async_computation.5 | async-start | bytes 1835008 | tf_op jit(solution)/shard_map/all_to_all | solution.py:43
  80.3 2.7 %shard_map.82 = (f32[9,32,384]{2,1,0:T(8,128)S(1)}, f32[9,32,384]{2,1,0:T(8,128)S(1)}, f32[1024,128]{1,0:T(8,128)}, f32[5,5,32,384]{3,2,1,0:T(8,128)S(1)}) custom-call(s32[1]{0:T(128)} %bitcast.10.odd_ref.refs_0_, f32[4352,128]{1,0:T(8,128)S(1)} %bitcast.43, f32[1792,128]{1,0:T(8,128)} %bitcast.18.mark_ref), custom_call_target="tpu_custom_call" | custom-call | tf_op jit(solution)/shard_map/pallas_call | solution.py:553
  84.3 2.5 %shard_map.85 = (f32[9,32,384]{2,1,0:T(8,128)S(1)}, f32[9,32,384]{2,1,0:T(8,128)S(1)}, f32[1024,128]{1,0:T(8,128)}) custom-call(s32[1]{0:T(128)} %bitcast.10.odd_ref.refs_0_, f32[4352,128]{1,0:T(8,128)S(1)} %bitcast.44, f32[5,5,32,384]{3,2,1,0:T(8,128)S(1)} %get-tuple-element.72.coef_ref.refs_1_), custom_call_target="tpu_custom_call" | custom-call | tf_op jit(solution)/shard_map/pallas_call | solution.py:553
  88.4 7.6 %collective-permute-start.2 = (f32[9,32,384]{2,1,0:T(8,128)S(1)}, f32[9,32,384]{2,1,0:T(8,128)S(1)}, u32[]{:S(2)}, u32[]{:S(2)}) collective-permute-start(f32[9,32,384]{2,1,0:T(8,128)S(1)} %shard_map.83.weighted_ref), channel_id=1, source_target_pairs={{32,0},{64,32},{96,64},{128,96},{160,128},{192,160},{224,192},{256... | collective-permute-start | bytes 1327112 | tf_op jit(solution)/shard_map/ppermute | solution.py:571
  96.5 4.4 %collective-permute-start.4 = (f32[9,32,384]{2,1,0:T(8,128)S(1)}, f32[9,32,384]{2,1,0:T(8,128)S(1)}, u32[]{:S(2)}, u32[]{:S(2)}) collective-permute-start(f32[9,32,384]{2,1,0:T(8,128)S(1)} %shard_map.86.weighted_ref), channel_id=1, source_target_pairs={{32,0},{64,32},{96,64},{128,96},{160,128},{192,160},{224,192},{256... | collective-permute-start | bytes 1327112 | tf_op jit(solution)/shard_map/ppermute | solution.py:571
  101.0 1.3 shard_map.84.refs_4_
  103.1 1.3 shard_map.87.refs_6_
  106.2 6.7 %shard_map.88 = (f32[18,32,384]{2,1,0:T(8,128)}, f32[18,32,384]{2,1,0:T(8,128)}, f32[1792,128]{1,0:T(8,128)}, f32[1792,128]{1,0:T(8,128)}, f32[8,128]{1,0:T(8,128)}) custom-call(s32[1]{0:T(128)} %bitcast.10.odd_ref.refs_0_, f32[5,5,32,384]{3,2,1,0:T(8,128)} %copy-done, f32[1792,128]{1,0:T(8,128)} %bitcast.52, f32[9,32,384]{2,1,0:T(8,128)} %copy-done.1, ...), custom_call_target="tpu_custom_call" | custom-call | tf_op jit(solution)/shard_map/pallas_call | solution.py:553
  114.1 48.2 %conditional.2 = (f32[1792,128]{1,0:T(8,128)S(1)}, f32[1792,128]{1,0:T(8,128)}) conditional(s32[]{:T(128)} %convert_element_type.4, f32[1792,128]{1,0:T(8,128)} %get-tuple-element.80, (f32[1792,128]{1,0:T(8,128)}, f32[1024,128]{1,0:T(8,128)}, f32[1024,128]{1,0:T(8,128)}) %tuple.36), branch_computations={%region_2.3_spmd, %region_3.4_spmd} | conditional | flops 1376256 | bytes 10978216 | solution.py:672
  114.2 1.8 maximum_maximum_fusion
  116.0 45.3 %all_to_all.32 = f32[32,112,128]{2,1,0:T(8,128)S(1)} all-to-all(f32[32,112,128]{2,1,0:T(8,128)S(1)} %maximum_maximum_fusion), channel_id=1, replica_groups=mesh['tm'=16,'lat'=32] {'lat'}, dimensions={0} | all-to-all | bytes 3670016 | tf_op jit(solution)/shard_map/cond/branch_1_fun/all_to_all | solution.py:43
  162.4 2.2 %collective-permute-start.6 = (f32[1792,128]{1,0:T(8,128)}, f32[1792,128]{1,0:T(8,128)}, u32[]{:S(2)}, u32[]{:S(2)}) collective-permute-start(f32[1792,128]{1,0:T(8,128)} %get-tuple-element.98.got_ref), channel_id=1, source_target_pairs={{32,0},{64,32},{96,64},{128,96},{160,128},{192,160},{224,192},{256... | collective-permute-start | bytes 2752520 | tf_op jit(solution)/shard_map/ppermute | solution.py:571
  164.6 1.6 shard_map.89
  166.9 4.4 %all-to-all-start.6 = ((f32[16,8,128]{2,1,0:T(8,128)}), f32[16,8,128]{2,1,0:T(8,128)S(1)}, u32[]{:S(2)}, u32[]{:S(2)}) async-start(f32[16,8,128]{2,1,0:T(8,128)} %broadcast_in_dim.32), calls=%async_computation.6 | async-start | bytes 131072 | tf_op jit(solution)/shard_map/all_to_all | solution.py:577
  171.3 2.6 %shard_map.90 = f32[1,4,1,49320]{3,2,1,0:T(1,128)S(1)} custom-call(f32[1792,128]{1,0:T(8,128)} %get-tuple-element.98.got_ref), custom_call_target="tpu_custom_call" | custom-call | tf_op jit(solution)/shard_map/pallas_call | solution.py:553
  173.9 2.7 %all-to-all-done.6 = f32[16,8,128]{2,1,0:T(8,128)S(1)} async-done(((f32[16,8,128]{2,1,0:T(8,128)}), f32[16,8,128]{2,1,0:T(8,128)S(1)}, u32[]{:S(2)}, u32[]{:S(2)}) %all-to-all-start.6) | async-done | bytes 65568 | tf_op jit(solution)/shard_map/all_to_all | solution.py:577
  176.6 26.5 %conditional.3 = ((f32[1,4,1,49320]{3,2,1,0:T(1,128)}, f32[1,4,1,49320]{3,2,1,0:T(1,128)})) conditional(s32[]{:T(128)} %convert_element_type.4, (f32[8,128]{1,0:T(8,128)S(1)}, f32[1,4,1,49320]{3,2,1,0:T(1,128)S(1)}, f32[1,4,1,49320]{3,2,1,0:T(1,128)S(1)}, f32[1,4,1,49320]{3,2,1,0:T(1,128)}, f32[1792,128]{1,0:T(8,128)}) %tuple.56, ...), branch_computations={%region_4.5_spmd, %region_5.6_spmd} | conditional | flops 262144 | bytes 4329480 | solution.py:693
  178.0 22.3 %all_to_all.34 = f32[32,64,128]{2,1,0:T(8,128)S(1)} all-to-all(f32[32,64,128]{2,1,0:T(8,128)S(1)} %pad_maximum_fusion), channel_id=1, replica_groups=mesh['tm'=16,'lat'=32] {'lat'}, dimensions={0} | all-to-all | bytes 2097152 | tf_op jit(solution)/shard_map/cond/branch_1_fun/all_to_all | solution.py:43
  200.3 2.9 %branch_1_fun.1 = (f32[1,4,1,49320]{3,2,1,0:T(1,128)}, f32[1,4,1,49320]{3,2,1,0:T(1,128)}) custom-call(f32[2048,128]{1,0:T(8,128)S(1)} %bitcast.48, f32[1792,128]{1,0:T(8,128)S(1)} %get-tuple-element.43.got_moved_ref, f32[1,4,1,49320]{3,2,1,0:T(1,128)S(1)} %get-tuple-element.44.own_ref, f32[1,4,1,49320]{3,2,1,0:T(1,128)S(1)} %get-tuple-element.45.image_ref), custom_call_target="tpu_custom_call" | custom-call | tf_op jit(solution)/shard_map/cond/branch_1_fun/pallas_call | solution.py:553
  (47 shorter events, 11.7 us)
Async XLA Ops:
  8.5 13.1 %copy-start.7 = (f32[1,4,1,49320]{3,2,1,0:T(1,128)S(1)}, f32[1,4,1,49320]{3,2,1,0:T(1,128)}, u32[]{:S(2)}) copy-start(f32[1,4,1,49320]{3,2,1,0:T(1,128)} %own_hbm.1) | copy-start | bytes 2367364
  8.5 18.0 %copy-start.12 = (s32[1,2048]{1,0:T(1,128)S(1)}, s32[1,2048]{1,0:T(1,128)}, u32[]{:S(2)}) copy-start(s32[1,2048]{1,0:T(1,128)} %param.14) | copy-start | bytes 24580
  8.5 64.6 %all-to-all-start.4 = ((f32[32,136,128]{2,1,0:T(8,128)}), f32[32,136,128]{2,1,0:T(8,128)S(1)}, u32[]{:S(2)}, u32[]{:S(2)}) async-start(f32[32,136,128]{2,1,0:T(8,128)} %bitcast.50), calls=%async_computation.4 | async-start | bytes 4456448 | tf_op jit(solution)/shard_map/all_to_all | solution.py:43
  21.6 4.9 %collective-permute-start = (f32[1,4,1,49320]{3,2,1,0:T(1,128)S(1)}, f32[1,4,1,49320]{3,2,1,0:T(1,128)}, u32[]{:S(2)}, u32[]{:S(2)}) collective-permute-start(f32[1,4,1,49320]{3,2,1,0:T(1,128)S(1)} %copy-done.7), channel_id=1, source_target_pairs={{32,0},{64,32},{96,64},{128,96},{160,128},{192,160},{224,192},{256... | collective-permute-start | bytes 2367368 | tf_op jit(solution)/shard_map/ppermute | solution.py:571
  73.1 32.1 %all-to-all-start.5 = ((f32[32,56,128]{2,1,0:T(8,128)}), f32[32,56,128]{2,1,0:T(8,128)S(1)}, u32[]{:S(2)}, u32[]{:S(2)}) async-start(f32[32,56,128]{2,1,0:T(8,128)} %bitcast.19), calls=%async_computation.5 | async-start | bytes 1835008 | tf_op jit(solution)/shard_map/all_to_all | solution.py:43
  83.0 5.4 %copy-start.1 = (f32[9,32,384]{2,1,0:T(8,128)}, f32[9,32,384]{2,1,0:T(8,128)S(1)}, u32[]{:S(2)}) copy-start(f32[9,32,384]{2,1,0:T(8,128)S(1)} %get-tuple-element.73.state_ref.refs_3_) | copy-start | bytes 1327108
  83.0 20.1 %copy-start = (f32[5,5,32,384]{3,2,1,0:T(8,128)}, f32[5,5,32,384]{3,2,1,0:T(8,128)S(1)}, u32[]{:S(2)}) copy-start(f32[5,5,32,384]{3,2,1,0:T(8,128)S(1)} %get-tuple-element.72.coef_ref.refs_1_) | copy-start | bytes 3686404
  83.0 5.1 %collective-permute-start.1 = (f32[9,32,384]{2,1,0:T(8,128)S(1)}, f32[9,32,384]{2,1,0:T(8,128)S(1)}, u32[]{:S(2)}, u32[]{:S(2)}) collective-permute-start(f32[9,32,384]{2,1,0:T(8,128)S(1)} %get-tuple-element.74), channel_id=1, source_target_pairs={{0,32},{32,64},{64,96},{96,128},{128,160},{160,192},{192,224},{224... | collective-permute-start | bytes 1327112 | tf_op jit(solution)/shard_map/ppermute | solution.py:571
  86.8 9.7 %copy-start.2 = (f32[9,32,384]{2,1,0:T(8,128)}, f32[9,32,384]{2,1,0:T(8,128)S(1)}, u32[]{:S(2)}) copy-start(f32[9,32,384]{2,1,0:T(8,128)S(1)} %get-tuple-element.75.state_ref.refs_5_) | copy-start | bytes 1327108
  86.8 9.3 %collective-permute-start.3 = (f32[9,32,384]{2,1,0:T(8,128)S(1)}, f32[9,32,384]{2,1,0:T(8,128)S(1)}, u32[]{:S(2)}, u32[]{:S(2)}) collective-permute-start(f32[9,32,384]{2,1,0:T(8,128)S(1)} %get-tuple-element.76), channel_id=1, source_target_pairs={{0,32},{32,64},{64,96},{96,128},{128,160},{160,192},{192,224},{224... | collective-permute-start | bytes 1327112 | tf_op jit(solution)/shard_map/ppermute | solution.py:571
  88.4 12.5 %collective-permute-start.2 = (f32[9,32,384]{2,1,0:T(8,128)S(1)}, f32[9,32,384]{2,1,0:T(8,128)S(1)}, u32[]{:S(2)}, u32[]{:S(2)}) collective-permute-start(f32[9,32,384]{2,1,0:T(8,128)S(1)} %shard_map.83.weighted_ref), channel_id=1, source_target_pairs={{32,0},{64,32},{96,64},{128,96},{160,128},{192,160},{224,192},{256... | collective-permute-start | bytes 1327112 | tf_op jit(solution)/shard_map/ppermute | solution.py:571
  96.5 6.5 %collective-permute-start.4 = (f32[9,32,384]{2,1,0:T(8,128)S(1)}, f32[9,32,384]{2,1,0:T(8,128)S(1)}, u32[]{:S(2)}, u32[]{:S(2)}) collective-permute-start(f32[9,32,384]{2,1,0:T(8,128)S(1)} %shard_map.86.weighted_ref), channel_id=1, source_target_pairs={{32,0},{64,32},{96,64},{128,96},{160,128},{192,160},{224,192},{256... | collective-permute-start | bytes 1327112 | tf_op jit(solution)/shard_map/ppermute | solution.py:571
  102.3 0.8 copy-start.3
  104.4 0.8 copy-start.4
  105.2 1.0 copy-start.11
  112.8 51.8 %collective-permute-start.5 = (f32[18,32,384]{2,1,0:T(8,128)}, f32[18,32,384]{2,1,0:T(8,128)}, u32[]{:S(2)}, u32[]{:S(2)}) collective-permute-start(f32[18,32,384]{2,1,0:T(8,128)} %get-tuple-element.78), channel_id=1, source_target_pairs={{0,32},{32,64},{64,96},{96,128},{128,160},{160,192},{192,224},{224... | collective-permute-start | bytes 2654216 | tf_op jit(solution)/shard_map/ppermute | solution.py:571
  114.1 50.5 %copy-start.5 = (f32[18,32,384]{2,1,0:T(8,128)S(1)}, f32[18,32,384]{2,1,0:T(8,128)}, u32[]{:S(2)}) copy-start(f32[18,32,384]{2,1,0:T(8,128)} %get-tuple-element.77.image_ref) | copy-start | bytes 2654212
  114.1 50.5 %copy-start.6 = (f32[8,128]{1,0:T(8,128)S(1)}, f32[8,128]{1,0:T(8,128)}, u32[]{:S(2)}) copy-start(f32[8,128]{1,0:T(8,128)} %get-tuple-element.79.sums_ref) | copy-start | bytes 12292
  162.4 3.9 %copy-start.9 = (f32[1792,128]{1,0:T(8,128)}, f32[1792,128]{1,0:T(8,128)S(1)}, u32[]{:S(2)}) copy-start(f32[1792,128]{1,0:T(8,128)S(1)} %get-tuple-element.90) | copy-start | bytes 2752516
  162.4 14.3 %collective-permute-start.6 = (f32[1792,128]{1,0:T(8,128)}, f32[1792,128]{1,0:T(8,128)}, u32[]{:S(2)}, u32[]{:S(2)}) collective-permute-start(f32[1792,128]{1,0:T(8,128)} %get-tuple-element.98.got_ref), channel_id=1, source_target_pairs={{32,0},{64,32},{96,64},{128,96},{160,128},{192,160},{224,192},{256... | collective-permute-start | bytes 2752520 | tf_op jit(solution)/shard_map/ppermute | solution.py:571
  166.2 10.4 %copy-start.8 = (f32[1,4,1,49320]{3,2,1,0:T(1,128)S(1)}, f32[1,4,1,49320]{3,2,1,0:T(1,128)}, u32[]{:S(2)}) copy-start(f32[1,4,1,49320]{3,2,1,0:T(1,128)} %own_hbm.1) | copy-start | bytes 2367364
  166.9 9.8 %copy-start.10 = (f32[1792,128]{1,0:T(8,128)S(1)}, f32[1792,128]{1,0:T(8,128)}, u32[]{:S(2)}) copy-start(f32[1792,128]{1,0:T(8,128)} %copy-done.9) | copy-start | bytes 2752516
  166.9 9.7 %all-to-all-start.6 = ((f32[16,8,128]{2,1,0:T(8,128)}), f32[16,8,128]{2,1,0:T(8,128)S(1)}, u32[]{:S(2)}, u32[]{:S(2)}) async-start(f32[16,8,128]{2,1,0:T(8,128)} %broadcast_in_dim.32), calls=%async_computation.6 | async-start | bytes 131072 | tf_op jit(solution)/shard_map/all_to_all | solution.py:577

commit v7 on v6

--- a/solution.py
+++ b/solution.py
@@ -659,8 +659,7 @@
         parts = [
             blocks_of(back),
             blocks_of(first_back)[:, : CUTS * HALF],
-            blocks_of(second_back)[:, : CUTS * HALF],
-            jnp.zeros((32, BACK_ROWS - 2 * CUTS * HALF, LANES), jnp.float32),
+            blocks_of(second_back)[:, : BACK_ROWS - CUTS * HALF],
         ]
         both = blocks_of(exchanged(jnp.concatenate(parts, 1).reshape(-1, LANES)))
         return both[:, :BACK_ROWS].reshape(-1, LANES), both[:, BACK_ROWS:].reshape(-1, LANES)

time: 204 us -> 204 us (level)
  no operation moved by 1% of the time
where the time goes in v7:
time: 204 us; the launch traced here: 203 us
  blocking collectives  67.6 us (33%)
  starting transfers between devices  46.5 us (23%)
  waiting for transfers between devices  37.8 us (19%)
  Pallas kernels  30.2 us (15%)
  other arithmetic  15.7 us (8%)
  local copies, waits for them, and re-layouts  4.3 us (2%)
    all_to_all x2, blocking collectives, exchanged(): return lax.all_to_all(chunks, 'lat', 0, 0, tiled=True).reshape(-1, LANES)  67.6 us
    all_to_all x2, waiting for transfers between devices, exchanged(): return lax.all_to_all(chunks, 'lat', 0, 0, tiled=True).reshape(-1, LANES)  34 us
    pallas_call x10, Pallas kernels, run(): pl.pallas_call(whole, out_shape=outs, in_specs=[spec[i] for i in ins], ou...  22.4 us
    ppermute x7, starting transfers between devices, passed_along(): return lax.ppermute(shard, 'tm', pairs)  21.9 us
    all_to_all x2, starting transfers between devices, exchanged(): return lax.all_to_all(chunks, 'lat', 0, 0, tiled=True).reshape(-1, LANES)  20.2 us
    scatter-add x1, other arithmetic, cells_in_planes(): empty.at[row * LANES + lane % LANES].add(weight)  12.4 us
    pallas_call x1, Pallas kernels, pack(): pl.pallas_call(pack_kernel, out_shape=jax.ShapeDtypeStruct((32 * SEND_ROW...  7.85 us
    all_to_all x1, starting transfers between devices, summed_over_tm(): return lax.all_to_all(copies, 'tm', 0, 0, tiled=True).sum(0)  4.42 us
  transfers between devices with their start and end apart: 10, of which 3 were waited for; matrix products, arithmetic and copies ran while one was open for 8% of the time, Pallas kernels for 6%

profile of v7, /device:TPU:57, one launch (start us, length us, event | category | flops | bytes accessed | tf_op | source)
XLA Modules:
  0.0 203.0 jit_solution(3000768820766480106)
XLA Ops:
  0.6 7.8 %shard_map.81 = f32[4352,128]{1,0:T(8,128)} custom-call(f32[1,4,1,49320]{3,2,1,0:T(1,128)} %own_hbm.1, f32[1,1,49320]{2,1,0:T(1,128)} %lon_hbm.1, f32[1,1,49320]{2,1,0:T(1,128)} %lat_hbm.1, f32[1,4,1,49320]{3,2,1,0:T(1,128)} %weight_hbm.1), custom_call_target="tpu_custom_call" | custom-call | tf_op jit(solution)/shard_map/pallas_call | solution.py:166
  8.5 13.0 %all-to-all-start.4 = ((f32[32,136,128]{2,1,0:T(8,128)}), f32[32,136,128]{2,1,0:T(8,128)S(1)}, u32[]{:S(2)}, u32[]{:S(2)}) async-start(f32[32,136,128]{2,1,0:T(8,128)} %bitcast.50), calls=%async_computation.4 | async-start | bytes 4456448 | tf_op jit(solution)/shard_map/all_to_all | solution.py:43
  21.6 3.8 %collective-permute-start = (f32[1,4,1,49320]{3,2,1,0:T(1,128)S(1)}, f32[1,4,1,49320]{3,2,1,0:T(1,128)}, u32[]{:S(2)}, u32[]{:S(2)}) collective-permute-start(f32[1,4,1,49320]{3,2,1,0:T(1,128)S(1)} %copy-done.7), channel_id=1, source_target_pairs={{32,0},{64,32},{96,64},{128,96},{160,128},{192,160},{224,192},{256... | collective-permute-start | bytes 2367368 | tf_op jit(solution)/shard_map/ppermute | solution.py:571
  26.8 12.4 %scatter_custom_fusion = f32[229376]{0:T(1024)} fusion(s32[2048]{0:T(1024)S(1)} %bitcast.58, f32[2048]{0:T(1024)} %bitcast.59, f32[]{:T(128)} %constant.105.clone.1), kind=kCustom, calls=%fused_computation.3 | custom fusion | flops 2048 | bytes 918016 | tf_op jit(solution)/shard_map/scatter-add | solution.py:617
  39.2 34.0 %all-to-all-done.4 = f32[32,136,128]{2,1,0:T(8,128)S(1)} async-done(((f32[32,136,128]{2,1,0:T(8,128)}), f32[32,136,128]{2,1,0:T(8,128)S(1)}, u32[]{:S(2)}, u32[]{:S(2)}) %all-to-all-start.4) | async-done | bytes 2228256 | tf_op jit(solution)/shard_map/all_to_all | solution.py:43
  73.1 7.1 %all-to-all-start.5 = ((f32[32,56,128]{2,1,0:T(8,128)}), f32[32,56,128]{2,1,0:T(8,128)S(1)}, u32[]{:S(2)}, u32[]{:S(2)}) async-start(f32[32,56,128]{2,1,0:T(8,128)} %bitcast.19), calls=%async_computation.5 | async-start | bytes 1835008 | tf_op jit(solution)/shard_map/all_to_all | solution.py:43
  80.3 2.7 %shard_map.82 = (f32[9,32,384]{2,1,0:T(8,128)S(1)}, f32[9,32,384]{2,1,0:T(8,128)S(1)}, f32[1024,128]{1,0:T(8,128)}, f32[5,5,32,384]{3,2,1,0:T(8,128)S(1)}) custom-call(s32[1]{0:T(128)} %bitcast.10.odd_ref.refs_0_, f32[4352,128]{1,0:T(8,128)S(1)} %bitcast.43, f32[1792,128]{1,0:T(8,128)} %bitcast.18.mark_ref), custom_call_target="tpu_custom_call" | custom-call | tf_op jit(solution)/shard_map/pallas_call | solution.py:553
  84.3 2.5 %shard_map.85 = (f32[9,32,384]{2,1,0:T(8,128)S(1)}, f32[9,32,384]{2,1,0:T(8,128)S(1)}, f32[1024,128]{1,0:T(8,128)}) custom-call(s32[1]{0:T(128)} %bitcast.10.odd_ref.refs_0_, f32[4352,128]{1,0:T(8,128)S(1)} %bitcast.44, f32[5,5,32,384]{3,2,1,0:T(8,128)S(1)} %get-tuple-element.72.coef_ref.refs_1_), custom_call_target="tpu_custom_call" | custom-call | tf_op jit(solution)/shard_map/pallas_call | solution.py:553
  88.4 7.6 %collective-permute-start.2 = (f32[9,32,384]{2,1,0:T(8,128)S(1)}, f32[9,32,384]{2,1,0:T(8,128)S(1)}, u32[]{:S(2)}, u32[]{:S(2)}) collective-permute-start(f32[9,32,384]{2,1,0:T(8,128)S(1)} %shard_map.83.weighted_ref), channel_id=1, source_target_pairs={{32,0},{64,32},{96,64},{128,96},{160,128},{192,160},{224,192},{256... | collective-permute-start | bytes 1327112 | tf_op jit(solution)/shard_map/ppermute | solution.py:571
  96.5 4.4 %collective-permute-start.4 = (f32[9,32,384]{2,1,0:T(8,128)S(1)}, f32[9,32,384]{2,1,0:T(8,128)S(1)}, u32[]{:S(2)}, u32[]{:S(2)}) collective-permute-start(f32[9,32,384]{2,1,0:T(8,128)S(1)} %shard_map.86.weighted_ref), channel_id=1, source_target_pairs={{32,0},{64,32},{96,64},{128,96},{160,128},{192,160},{224,192},{256... | collective-permute-start | bytes 1327112 | tf_op jit(solution)/shard_map/ppermute | solution.py:571
  101.0 1.3 shard_map.84.refs_4_
  103.1 1.3 shard_map.87.refs_6_
  106.2 6.7 %shard_map.88 = (f32[18,32,384]{2,1,0:T(8,128)}, f32[18,32,384]{2,1,0:T(8,128)}, f32[1792,128]{1,0:T(8,128)}, f32[1792,128]{1,0:T(8,128)}, f32[8,128]{1,0:T(8,128)}) custom-call(s32[1]{0:T(128)} %bitcast.10.odd_ref.refs_0_, f32[5,5,32,384]{3,2,1,0:T(8,128)} %copy-done, f32[1792,128]{1,0:T(8,128)} %bitcast.52, f32[9,32,384]{2,1,0:T(8,128)} %copy-done.1, ...), custom_call_target="tpu_custom_call" | custom-call | tf_op jit(solution)/shard_map/pallas_call | solution.py:553
  114.1 48.1 %conditional.2 = (f32[1792,128]{1,0:T(8,128)S(1)}, f32[1792,128]{1,0:T(8,128)}) conditional(s32[]{:T(128)} %convert_element_type.4, f32[1792,128]{1,0:T(8,128)} %get-tuple-element.80, (f32[1792,128]{1,0:T(8,128)}, f32[1024,128]{1,0:T(8,128)}, f32[1024,128]{1,0:T(8,128)}) %tuple.36), branch_computations={%region_2.3_spmd, %region_3.4_spmd} | conditional | flops 917504 | bytes 11010064 | solution.py:671
  114.2 1.7 pad_maximum_fusion
  115.9 45.3 %all_to_all.32 = f32[32,112,128]{2,1,0:T(8,128)S(1)} all-to-all(f32[32,112,128]{2,1,0:T(8,128)S(1)} %pad_maximum_fusion), channel_id=1, replica_groups=mesh['tm'=16,'lat'=32] {'lat'}, dimensions={0} | all-to-all | bytes 3670016 | tf_op jit(solution)/shard_map/cond/branch_1_fun/all_to_all | solution.py:43
  162.2 2.2 %collective-permute-start.6 = (f32[1792,128]{1,0:T(8,128)}, f32[1792,128]{1,0:T(8,128)}, u32[]{:S(2)}, u32[]{:S(2)}) collective-permute-start(f32[1792,128]{1,0:T(8,128)} %get-tuple-element.98.got_ref), channel_id=1, source_target_pairs={{32,0},{64,32},{96,64},{128,96},{160,128},{192,160},{224,192},{256... | collective-permute-start | bytes 2752520 | tf_op jit(solution)/shard_map/ppermute | solution.py:571
  164.4 1.6 shard_map.89
  166.7 4.4 %all-to-all-start.6 = ((f32[16,8,128]{2,1,0:T(8,128)}), f32[16,8,128]{2,1,0:T(8,128)S(1)}, u32[]{:S(2)}, u32[]{:S(2)}) async-start(f32[16,8,128]{2,1,0:T(8,128)} %broadcast_in_dim.32), calls=%async_computation.6 | async-start | bytes 131072 | tf_op jit(solution)/shard_map/all_to_all | solution.py:577
  171.1 2.6 %shard_map.90 = f32[1,4,1,49320]{3,2,1,0:T(1,128)S(1)} custom-call(f32[1792,128]{1,0:T(8,128)} %get-tuple-element.98.got_ref), custom_call_target="tpu_custom_call" | custom-call | tf_op jit(solution)/shard_map/pallas_call | solution.py:553
  173.8 2.7 %all-to-all-done.6 = f32[16,8,128]{2,1,0:T(8,128)S(1)} async-done(((f32[16,8,128]{2,1,0:T(8,128)}), f32[16,8,128]{2,1,0:T(8,128)S(1)}, u32[]{:S(2)}, u32[]{:S(2)}) %all-to-all-start.6) | async-done | bytes 65568 | tf_op jit(solution)/shard_map/all_to_all | solution.py:577
  176.5 26.5 %conditional.3 = ((f32[1,4,1,49320]{3,2,1,0:T(1,128)}, f32[1,4,1,49320]{3,2,1,0:T(1,128)})) conditional(s32[]{:T(128)} %convert_element_type.4, (f32[8,128]{1,0:T(8,128)S(1)}, f32[1,4,1,49320]{3,2,1,0:T(1,128)S(1)}, f32[1,4,1,49320]{3,2,1,0:T(1,128)S(1)}, f32[1,4,1,49320]{3,2,1,0:T(1,128)}, f32[1792,128]{1,0:T(8,128)}) %tuple.56, ...), branch_computations={%region_4.5_spmd, %region_5.6_spmd} | conditional | flops 262144 | bytes 4329480 | solution.py:692
  177.8 22.3 %all_to_all.34 = f32[32,64,128]{2,1,0:T(8,128)S(1)} all-to-all(f32[32,64,128]{2,1,0:T(8,128)S(1)} %pad_maximum_fusion.1), channel_id=1, replica_groups=mesh['tm'=16,'lat'=32] {'lat'}, dimensions={0} | all-to-all | bytes 2097152 | tf_op jit(solution)/shard_map/cond/branch_1_fun/all_to_all | solution.py:43
  200.2 2.9 %branch_1_fun.1 = (f32[1,4,1,49320]{3,2,1,0:T(1,128)}, f32[1,4,1,49320]{3,2,1,0:T(1,128)}) custom-call(f32[2048,128]{1,0:T(8,128)S(1)} %bitcast.48, f32[1792,128]{1,0:T(8,128)S(1)} %get-tuple-element.43.got_moved_ref, f32[1,4,1,49320]{3,2,1,0:T(1,128)S(1)} %get-tuple-element.44.own_ref, f32[1,4,1,49320]{3,2,1,0:T(1,128)S(1)} %get-tuple-element.45.image_ref), custom_call_target="tpu_custom_call" | custom-call | tf_op jit(solution)/shard_map/cond/branch_1_fun/pallas_call | solution.py:553
  (45 shorter events, 11.6 us)
Async XLA Ops:
  8.5 13.1 %copy-start.7 = (f32[1,4,1,49320]{3,2,1,0:T(1,128)S(1)}, f32[1,4,1,49320]{3,2,1,0:T(1,128)}, u32[]{:S(2)}) copy-start(f32[1,4,1,49320]{3,2,1,0:T(1,128)} %own_hbm.1) | copy-start | bytes 2367364
  8.5 18.0 %copy-start.12 = (s32[1,2048]{1,0:T(1,128)S(1)}, s32[1,2048]{1,0:T(1,128)}, u32[]{:S(2)}) copy-start(s32[1,2048]{1,0:T(1,128)} %param.14) | copy-start | bytes 24580
  8.5 64.6 %all-to-all-start.4 = ((f32[32,136,128]{2,1,0:T(8,128)}), f32[32,136,128]{2,1,0:T(8,128)S(1)}, u32[]{:S(2)}, u32[]{:S(2)}) async-start(f32[32,136,128]{2,1,0:T(8,128)} %bitcast.50), calls=%async_computation.4 | async-start | bytes 4456448 | tf_op jit(solution)/shard_map/all_to_all | solution.py:43
  21.6 4.9 %collective-permute-start = (f32[1,4,1,49320]{3,2,1,0:T(1,128)S(1)}, f32[1,4,1,49320]{3,2,1,0:T(1,128)}, u32[]{:S(2)}, u32[]{:S(2)}) collective-permute-start(f32[1,4,1,49320]{3,2,1,0:T(1,128)S(1)} %copy-done.7), channel_id=1, source_target_pairs={{32,0},{64,32},{96,64},{128,96},{160,128},{192,160},{224,192},{256... | collective-permute-start | bytes 2367368 | tf_op jit(solution)/shard_map/ppermute | solution.py:571
  73.1 32.1 %all-to-all-start.5 = ((f32[32,56,128]{2,1,0:T(8,128)}), f32[32,56,128]{2,1,0:T(8,128)S(1)}, u32[]{:S(2)}, u32[]{:S(2)}) async-start(f32[32,56,128]{2,1,0:T(8,128)} %bitcast.19), calls=%async_computation.5 | async-start | bytes 1835008 | tf_op jit(solution)/shard_map/all_to_all | solution.py:43
  83.0 5.4 %copy-start.1 = (f32[9,32,384]{2,1,0:T(8,128)}, f32[9,32,384]{2,1,0:T(8,128)S(1)}, u32[]{:S(2)}) copy-start(f32[9,32,384]{2,1,0:T(8,128)S(1)} %get-tuple-element.73.state_ref.refs_3_) | copy-start | bytes 1327108
  83.0 20.1 %copy-start = (f32[5,5,32,384]{3,2,1,0:T(8,128)}, f32[5,5,32,384]{3,2,1,0:T(8,128)S(1)}, u32[]{:S(2)}) copy-start(f32[5,5,32,384]{3,2,1,0:T(8,128)S(1)} %get-tuple-element.72.coef_ref.refs_1_) | copy-start | bytes 3686404
  83.0 5.1 %collective-permute-start.1 = (f32[9,32,384]{2,1,0:T(8,128)S(1)}, f32[9,32,384]{2,1,0:T(8,128)S(1)}, u32[]{:S(2)}, u32[]{:S(2)}) collective-permute-start(f32[9,32,384]{2,1,0:T(8,128)S(1)} %get-tuple-element.74), channel_id=1, source_target_pairs={{0,32},{32,64},{64,96},{96,128},{128,160},{160,192},{192,224},{224... | collective-permute-start | bytes 1327112 | tf_op jit(solution)/shard_map/ppermute | solution.py:571
  86.8 9.7 %copy-start.2 = (f32[9,32,384]{2,1,0:T(8,128)}, f32[9,32,384]{2,1,0:T(8,128)S(1)}, u32[]{:S(2)}) copy-start(f32[9,32,384]{2,1,0:T(8,128)S(1)} %get-tuple-element.75.state_ref.refs_5_) | copy-start | bytes 1327108
  86.8 9.3 %collective-permute-start.3 = (f32[9,32,384]{2,1,0:T(8,128)S(1)}, f32[9,32,384]{2,1,0:T(8,128)S(1)}, u32[]{:S(2)}, u32[]{:S(2)}) collective-permute-start(f32[9,32,384]{2,1,0:T(8,128)S(1)} %get-tuple-element.76), channel_id=1, source_target_pairs={{0,32},{32,64},{64,96},{96,128},{128,160},{160,192},{192,224},{224... | collective-permute-start | bytes 1327112 | tf_op jit(solution)/shard_map/ppermute | solution.py:571
  88.4 12.5 %collective-permute-start.2 = (f32[9,32,384]{2,1,0:T(8,128)S(1)}, f32[9,32,384]{2,1,0:T(8,128)S(1)}, u32[]{:S(2)}, u32[]{:S(2)}) collective-permute-start(f32[9,32,384]{2,1,0:T(8,128)S(1)} %shard_map.83.weighted_ref), channel_id=1, source_target_pairs={{32,0},{64,32},{96,64},{128,96},{160,128},{192,160},{224,192},{256... | collective-permute-start | bytes 1327112 | tf_op jit(solution)/shard_map/ppermute | solution.py:571
  96.5 6.5 %collective-permute-start.4 = (f32[9,32,384]{2,1,0:T(8,128)S(1)}, f32[9,32,384]{2,1,0:T(8,128)S(1)}, u32[]{:S(2)}, u32[]{:S(2)}) collective-permute-start(f32[9,32,384]{2,1,0:T(8,128)S(1)} %shard_map.86.weighted_ref), channel_id=1, source_target_pairs={{32,0},{64,32},{96,64},{128,96},{160,128},{192,160},{224,192},{256... | collective-permute-start | bytes 1327112 | tf_op jit(solution)/shard_map/ppermute | solution.py:571
  102.3 0.8 copy-start.3
  104.4 0.8 copy-start.4
  105.2 1.0 copy-start.11
  112.8 51.6 %collective-permute-start.5 = (f32[18,32,384]{2,1,0:T(8,128)}, f32[18,32,384]{2,1,0:T(8,128)}, u32[]{:S(2)}, u32[]{:S(2)}) collective-permute-start(f32[18,32,384]{2,1,0:T(8,128)} %get-tuple-element.78), channel_id=1, source_target_pairs={{0,32},{32,64},{64,96},{96,128},{128,160},{160,192},{192,224},{224... | collective-permute-start | bytes 2654216 | tf_op jit(solution)/shard_map/ppermute | solution.py:571
  114.1 50.3 %copy-start.5 = (f32[18,32,384]{2,1,0:T(8,128)S(1)}, f32[18,32,384]{2,1,0:T(8,128)}, u32[]{:S(2)}) copy-start(f32[18,32,384]{2,1,0:T(8,128)} %get-tuple-element.77.image_ref) | copy-start | bytes 2654212
  114.1 50.3 %copy-start.6 = (f32[8,128]{1,0:T(8,128)S(1)}, f32[8,128]{1,0:T(8,128)}, u32[]{:S(2)}) copy-start(f32[8,128]{1,0:T(8,128)} %get-tuple-element.79.sums_ref) | copy-start | bytes 12292
  162.2 3.9 %copy-start.9 = (f32[1792,128]{1,0:T(8,128)}, f32[1792,128]{1,0:T(8,128)S(1)}, u32[]{:S(2)}) copy-start(f32[1792,128]{1,0:T(8,128)S(1)} %get-tuple-element.90) | copy-start | bytes 2752516
  162.2 14.3 %collective-permute-start.6 = (f32[1792,128]{1,0:T(8,128)}, f32[1792,128]{1,0:T(8,128)}, u32[]{:S(2)}, u32[]{:S(2)}) collective-permute-start(f32[1792,128]{1,0:T(8,128)} %get-tuple-element.98.got_ref), channel_id=1, source_target_pairs={{32,0},{64,32},{96,64},{128,96},{160,128},{192,160},{224,192},{256... | collective-permute-start | bytes 2752520 | tf_op jit(solution)/shard_map/ppermute | solution.py:571
  166.1 10.4 %copy-start.8 = (f32[1,4,1,49320]{3,2,1,0:T(1,128)S(1)}, f32[1,4,1,49320]{3,2,1,0:T(1,128)}, u32[]{:S(2)}) copy-start(f32[1,4,1,49320]{3,2,1,0:T(1,128)} %own_hbm.1) | copy-start | bytes 2367364
  166.7 9.8 %copy-start.10 = (f32[1792,128]{1,0:T(8,128)S(1)}, f32[1792,128]{1,0:T(8,128)}, u32[]{:S(2)}) copy-start(f32[1792,128]{1,0:T(8,128)} %copy-done.9) | copy-start | bytes 2752516
  166.7 9.7 %all-to-all-start.6 = ((f32[16,8,128]{2,1,0:T(8,128)}), f32[16,8,128]{2,1,0:T(8,128)S(1)}, u32[]{:S(2)}, u32[]{:S(2)}) async-start(f32[16,8,128]{2,1,0:T(8,128)} %broadcast_in_dim.32), calls=%async_computation.6 | async-start | bytes 131072 | tf_op jit(solution)/shard_map/all_to_all | solution.py:577
